TPU v7x, 128 devices: a whole 4x4x4 slice. The times are simulated.
128 devices in a mesh: px: 8 (over x, core), py: 16 (over y, z).
Axes of the slice: x: 4, y: 4, z: 4, core: 2. Of those that a mesh axis runs over, the one named last changes fastest.
Arguments:
- horiz_div: float32 [128, 1024, 1024], P('py', 'px'), may hold values from -6 to 6
- w_star: float32 [128, 1024, 1024], P('py', 'px'), may hold values from -6 to 6
- air_temp: bfloat16 [128, 1024, 1024], P('py', 'px'), may hold values from -6 to 6
- roof_level: int32 [1024, 1024], P('px'), may hold values from 0 to 63
- facet_cells: int32 [128, 4096], P(('px', 'py')), may hold values from -1 to 1048575, as said below
- facet_temp: float32 [128, 4096], P(('px', 'py')), may hold values from -6 to 6
- net_radiation: float32 [128, 4096], P(('px', 'py')), may hold values from -6 to 6
- heat_capacity: float32 [128, 4096], P(('px', 'py')), may hold values from 1 to 4
- drag_coef: float32 [128, 4096], P(('px', 'py')), may hold values from 0.05 to 0.5
- heat_coef: float32 [128, 4096], P(('px', 'py')), may hold values from 0.05 to 0.5
Outputs:
- w_new: float32 [128, 1024, 1024], P('py', 'px')
- theta_new: bfloat16 [128, 1024, 1024], P('py', 'px')
- facet_temp_new: float32 [128, 4096], P(('px', 'py'))
Inputs may be any that keep to these rules, and one draw needn't show every extreme that they name: `facet_cells`: in each block of 32 rows the non-empty rows come first. For every device one owner's block is full, the same owner for all devices.
All inputs are finite; a program needn't handle non-finite values.
Results may differ from a plain program's by a relative error of at most 0.001.
Values sent between devices are 32-bit elements; how exact they have to be, the bound alone decides.
No kernel may reach another device: no remote copies, remote signals or barrier semaphores. Data moves between devices by JAX's collectives and lax.ppermute only.
A program may use at most 128 MiB of HBM per device.

v0:
```python
import math

import jax
import jax.numpy as jnp
from jax import lax
from jax.sharding import PartitionSpec as P


def fourier_table(size):
    positions = jnp.arange(size, dtype=jnp.int32)
    half_size = size // 2
    wave_num = jnp.where(positions <= half_size, positions, positions - half_size)
    phases = positions[:, None] * wave_num[None, :] % size
    angles = 2.0 * math.pi / size * phases.astype(jnp.float32)
    norm_edge = 1.0 / math.sqrt(size)
    norm_mid = math.sqrt(2.0 / size)
    columns = positions[None, :]
    basis = jnp.where(
        columns == 0,
        norm_edge,
        jnp.where(
            columns < half_size,
            norm_mid * jnp.cos(angles),
            jnp.where(
                columns == half_size, norm_edge * jnp.cos(angles), norm_mid * jnp.sin(angles)
            ),
        ),
    )
    eigenvalue = 2.0 * jnp.cos(2.0 * math.pi / size * wave_num.astype(jnp.float32)) - 2.0
    return (basis, eigenvalue)


def cosine_table(size):
    positions = jnp.arange(size, dtype=jnp.int32)
    odd_pos = 2 * positions + 1
    phases = odd_pos[:, None] * odd_pos[None, :] % (8 * size)
    angles = math.pi / (4.0 * size) * phases.astype(jnp.float32)
    basis = math.sqrt(2.0 / size) * jnp.cos(angles)
    eigenvalue = 2.0 * jnp.cos(math.pi / size * (positions.astype(jnp.float32) + 0.5)) - 2.0
    return (basis, eigenvalue)


def body(
    horiz_div,
    w_star,
    air_temp,
    roof_level,
    facet_cells,
    facet_temp,
    net_radiation,
    heat_capacity,
    drag_coef,
    heat_coef,
):
    level_count, row_count, x_cells = w_star.shape
    px_count = lax.axis_size("px")
    py_count = lax.axis_size("py")
    cell_ids = facet_cells[0]
    is_live = cell_ids >= 0
    safe_ids = jnp.maximum(cell_ids, 0)
    w_flat = w_star.reshape(-1)
    temp_flat = air_temp.reshape(-1).astype(jnp.float32)
    sampled = jnp.stack(
        [jnp.where(is_live, w_flat[safe_ids], 0.0), jnp.where(is_live, temp_flat[safe_ids], 0.0)]
    )
    arrived = lax.all_to_all(sampled, ("px", "py"), split_axis=1, concat_axis=1, tiled=True)
    w_cell = arrived[0]
    temp_cell = arrived[1]
    speeds = jnp.sqrt(w_cell * w_cell + 0.25)
    stress = drag_coef[0] * speeds * w_cell
    heat_flux = heat_coef[0] * speeds * (facet_temp[0] - temp_cell)
    new_temp = (
        facet_temp[0] + (net_radiation[0] - heat_flux - 0.5 * facet_temp[0]) / heat_capacity[0]
    )
    outgoing_flux = jnp.stack([stress, heat_flux])
    returned = lax.all_to_all(outgoing_flux, ("px", "py"), split_axis=1, concat_axis=1, tiled=True)
    momentum_sink = jnp.where(is_live, returned[0], 0.0)
    warmed = jnp.where(is_live, returned[1], 0.0)
    w_corr = w_flat.at[safe_ids].add(-momentum_sink).reshape(w_star.shape)
    theta_new = temp_flat.at[safe_ids].add(warmed).astype(jnp.bfloat16).reshape(air_temp.shape)
    basis_x, eigen_x = fourier_table(x_cells)
    y_cells = row_count * px_count
    basis_y, eigen_y = fourier_table(y_cells)
    z_cells = level_count * py_count
    basis_z, eigen_z = cosine_table(z_cells)
    highest = lax.Precision.HIGHEST
    fields = jnp.stack([horiz_div, w_corr])
    modes_x = jnp.einsum("fzyx,xk->fzky", fields, basis_x, precision=highest)
    modes_xy = jnp.einsum(
        "fzky,ym->fzmk",
        lax.all_to_all(modes_x, "px", split_axis=2, concat_axis=3, tiled=True),
        basis_y,
        precision=highest,
    )
    column = lax.all_to_all(modes_xy, "py", split_axis=2, concat_axis=1, tiled=True)
    kx_width = x_cells // px_count
    ky_width = y_cells // py_count
    eigen_xl = lax.dynamic_slice_in_dim(eigen_x, lax.axis_index("px") * kx_width, kx_width)
    eigen_yl = lax.dynamic_slice_in_dim(eigen_y, lax.axis_index("py") * ky_width, ky_width)
    w_column = column[1]
    w_shifted = jnp.concatenate([w_column[1:], jnp.zeros_like(w_column[:1])], axis=0)
    source = column[0] + w_shifted - w_column
    rotated = jnp.einsum("zab,zm->mab", source, basis_z, precision=highest)
    denominator = eigen_z[:, None, None] + eigen_yl[None, :, None] + eigen_xl[None, None, :]
    potential = jnp.einsum("mab,zm->zab", rotated / denominator, basis_z, precision=highest)
    outgoing = potential - jnp.concatenate([potential[:1], potential[:-1]], axis=0)
    returned_z = lax.all_to_all(outgoing[None], "py", split_axis=1, concat_axis=2, tiled=True)
    spectral_y = jnp.einsum("fzmk,ym->fzky", returned_z, basis_y, precision=highest)
    physical = jnp.einsum(
        "fzky,xk->fzyx",
        lax.all_to_all(spectral_y, "px", split_axis=3, concat_axis=2, tiled=True),
        basis_x,
        precision=highest,
    )[0]
    level_ids = lax.axis_index("py") * level_count + jnp.arange(level_count, dtype=jnp.int32)
    inside_solid = level_ids[:, None, None] < roof_level[None, :, :]
    w_new = jnp.where(inside_solid, 0.0, w_corr - physical)
    return (w_new, theta_new, new_temp[None])


def solution(mesh):
    placed = (
        P("py", "px", None),
        P("py", "px", None),
        P("py", "px", None),
        P("px", None),
        P(("px", "py"), None),
        P(("px", "py"), None),
        P(("px", "py"), None),
        P(("px", "py"), None),
        P(("px", "py"), None),
        P(("px", "py"), None),
    )
    return jax.shard_map(
        body,
        mesh=mesh,
        in_specs=placed,
        out_specs=(P("py", "px", None), P("py", "px", None), P(("px", "py"), None)),
        check_vma=False,
    )
```

profile of v0, /device:TPU:1, one launch (start us, length us, event | category | flops | bytes accessed | tf_op | source)
XLA Modules:
  0.0 962.2 jit_solution(17607176750551303584)
XLA Ops:
  9.4 89.0 %gather_fusion.1 = f32[4096]{0:T(1024)S(1)} fusion(f32[1048576]{0:T(1024)} %bitcast.94, s32[4096]{0:T(1024)S(1)} %broadcast_clamp_fusion), kind=kCustom, calls=%fused_computation.1 | custom fusion | bytes 49152 | tf_op jit(solution)/shard_map/gather | solution.py:64
  98.5 89.7 %gather_fusion = f32[4096]{0:T(1024)S(1)} fusion(f32[1048576]{0:T(1024)} %bitcast.92, s32[4096]{0:T(1024)S(1)} %broadcast_clamp_fusion), kind=kCustom, calls=%fused_computation | custom fusion | bytes 49152 | tf_op jit(solution)/shard_map/gather | solution.py:64
  189.2 26.0 %all-to-all-start = ((f32[2,128,32]{2,0,1:T(2,128)}), f32[2,128,32]{2,0,1:T(2,128)S(1)}, u32[]{:S(2)}, u32[]{:S(2)}) async-start(f32[2,128,32]{2,0,1:T(2,128)} %copy.63), calls=%async_computation | async-start | bytes 262144 | tf_op jit(solution)/shard_map/all_to_all | solution.py:66
  215.4 9.9 %all-to-all-done = f32[2,128,32]{2,0,1:T(2,128)S(1)} async-done(((f32[2,128,32]{2,0,1:T(2,128)}), f32[2,128,32]{2,0,1:T(2,128)S(1)}, u32[]{:S(2)}, u32[]{:S(2)}) %all-to-all-start) | async-done | bytes 32800 | tf_op jit(solution)/shard_map/all_to_all | solution.py:66
  233.0 10.0 %all-to-all-done.1 = f32[2,128,32]{2,0,1:T(2,128)S(1)} async-done(((f32[2,128,32]{2,0,1:T(2,128)}), f32[2,128,32]{2,0,1:T(2,128)S(1)}, u32[]{:S(2)}, u32[]{:S(2)}) %all-to-all-start.1) | async-done | bytes 32800 | tf_op jit(solution)/shard_map/all_to_all | solution.py:76
  243.5 26.3 %scatter_fusion = f32[1048576]{0:T(1024)} fusion(f32[1048576]{0:T(1024)} %bitcast.93, s32[4096]{0:T(1024)S(1)} %bitcast.107, f32[4096]{0:T(1024)S(1)} %get-tuple-element.15), kind=kCustom, calls=%fused_computation.2 | custom fusion | flops 4096 | bytes 65536 | tf_op jit(solution)/shard_map/scatter-add | solution.py:79
  269.8 4.9 stack_reshape.3
  279.0 90.6 %fusion.27 = f32[2,8,1024,128]{3,2,1,0:T(8,128)} fusion(s32[1024]{0:T(1024)S(1)} %compare_select_fusion, pred[1024]{0:T(1024)(128)(4,1)S(1)} %get-tuple-element.16, pred[1024]{0:T(1024)(128)(4,1)S(1)} %get-tuple-element.17, pred[1024]{0:T(1024)(128)(4,1)S(1)} %iota_compare_fusion.2, f32[2,8,128,1024]{3,2,1,0:T(8,128)S(1)} %fusion.118), kind=kOutput, calls=%fused_computation.38 | convolution fusion | flops 25790775296 | bytes 16784384 | tf_op jit(solution)/shard_map/fzyx,xk->fzky/dot_general | solution.py:88
  369.6 8.2 copy.66
  377.8 98.1 %all_to_all.75 = f32[2,8,1024,128]{3,1,0,2:T(8,128)S(1)} all-to-all(f32[2,8,1024,128]{3,1,0,2:T(8,128)S(1)} %copy.66), channel_id=1, replica_groups=mesh['px'=8,'py'=16] {'px'}, dimensions={2} | all-to-all | bytes 16777216 | tf_op jit(solution)/shard_map/all_to_all | solution.py:91
  476.0 8.1 copy.93
  484.0 9.3 all_to_all.59
  493.3 90.6 %fusion.24 = f32[2,8,1024,128]{3,2,1,0:T(8,128)S(1)} fusion(f32[2,8,128,1024]{3,2,1,0:T(8,128)} %all_to_all.59, s32[1024]{0:T(1024)S(1)} %compare_select_fusion, pred[1024]{0:T(1024)(128)(4,1)S(1)} %get-tuple-element.16, pred[1024]{0:T(1024)(128)(4,1)S(1)} %get-tuple-element.17, pred[1024]{0:T(1024)(128)(4,1)S(1)} %iota_compare_fusion.2), kind=kOutput, calls=%fused_computation.37 | convolution fusion | flops 25790775296 | bytes 16784384 | tf_op jit(solution)/shard_map/fzky,ym->fzmk/dot_general | solution.py:89
  583.9 8.1 copy.69
  592.0 4.9 all-to-all-start.3
  597.2 144.4 %all-to-all-done.3 = f32[2,8,1024,128]{3,1,0,2:T(8,128)} async-done(((f32[2,8,1024,128]{3,1,0,2:T(8,128)}), f32[2,8,1024,128]{3,1,0,2:T(8,128)}, u32[]{:S(2)}, u32[]{:S(2)}) %all-to-all-start.3) | async-done | bytes 8388640 | tf_op jit(solution)/shard_map/all_to_all | solution.py:95
  741.6 6.1 copy.70
  753.1 6.8 fusion.16
  759.9 4.8 fusion.18
  766.2 4.4 copy.75
  770.6 8.6 all-to-all-start.4
  779.2 18.4 %fusion.120 = f32[1024,1024,1]{1,0,2:T(8,128)} fusion(pred[1024]{0:T(1024)(128)(4,1)S(1)} %get-tuple-element.16, s32[1024]{0:T(1024)S(1)} %compare_select_fusion, pred[1024]{0:T(1024)(128)(4,1)S(1)} %get-tuple-element.17, pred[1024]{0:T(1024)(128)(4,1)S(1)} %iota_compare_fusion.2), kind=kLoop, calls=%fused_computation.20.clone.clone.clone.1 | loop fusion | flops 20971520 | bytes 4201472 | tf_op jit(solution)/shard_map/fzmk,ym->fzky/dot_general | solution.py:108
  797.6 32.1 %all-to-all-done.4 = f32[1,128,64,128]{3,2,0,1:T(8,128)} async-done(((f32[1,128,64,128]{3,2,0,1:T(8,128)}), f32[1,128,64,128]{3,2,0,1:T(8,128)}, u32[]{:S(2)}, u32[]{:S(2)}) %all-to-all-start.4) | async-done | bytes 4194336 | tf_op jit(solution)/shard_map/all_to_all | solution.py:107
  833.1 28.0 %fusion.32 = f32[1,8,128,1024]{3,2,1,0:T(8,128)} fusion(f32[8,1024,128]{2,1,0:T(8,128)S(1)} %bitcast.104, f32[1024,1024,1]{1,0,2:T(8,128)S(1)} %copy-done), kind=kOutput, calls=%fused_computation.39 | convolution fusion | flops 12884901888 | bytes 12582912 | tf_op jit(solution)/shard_map/fzmk,ym->fzky/dot_general | solution.py:108
  861.1 5.4 copy.78
  866.5 12.0 %all-to-all-start.5 = ((f32[1,8,128,1024]{2,1,0,3:T(8,128)}), f32[1,8,128,1024]{2,1,0,3:T(8,128)}, u32[]{:S(2)}, u32[]{:S(2)}) async-start(f32[1,8,128,1024]{2,1,0,3:T(8,128)} %copy.78), calls=%async_computation.5 | async-start | bytes 8388608 | tf_op jit(solution)/shard_map/all_to_all | solution.py:111
  878.5 18.3 %fusion.116 = f32[1024,1024,1]{1,0,2:T(8,128)} fusion(pred[1024]{0:T(1024)(128)(4,1)S(1)} %get-tuple-element.16, s32[1024]{0:T(1024)S(1)} %compare_select_fusion, pred[1024]{0:T(1024)(128)(4,1)S(1)} %get-tuple-element.17, pred[1024]{0:T(1024)(128)(4,1)S(1)} %iota_compare_fusion.2), kind=kLoop, calls=%fused_computation.18.clone.clone.clone.1 | loop fusion | flops 20971520 | bytes 4201472 | tf_op jit(solution)/shard_map/fzky,xk->fzyx/dot_general | solution.py:109
  896.8 4.9 reshape.158
  901.7 25.7 %scatter_fusion.1 = f32[1048576]{0:T(1024)} fusion(f32[1048576]{0:T(1024)} %bitcast.95, s32[4096]{0:T(1024)S(1)} %bitcast.108, f32[4096]{0:T(1024)S(1)} %get-tuple-element.14), kind=kCustom, calls=%fused_computation.3 | custom fusion | flops 4096 | bytes 65536 | tf_op jit(solution)/shard_map/scatter-add | solution.py:80
  932.1 6.6 copy.94
  938.7 5.0 reshape.160
  943.7 18.3 %subtract_select_fusion = f32[8,128,1024]{2,1,0:T(8,128)} fusion(f32[8,128,1024]{2,1,0:T(8,128)} %reshape.158, s32[128,1024]{1,0:T(8,128)S(1)} %copy-done.2, s32[8]{0:T(128)S(1)} %iota_add_fusion, f32[8,1024,128]{1,2,0:T(8,128)} %reshape.160, f32[1024,1024,1]{1,0,2:T(8,128)} %fusion.116), kind=kOutput, calls=%fused_computation.29 | convolution fusion | flops 12888047616 | bytes 17301536 | tf_op jit(solution)/shard_map/fzky,xk->fzyx/dot_general | solution.py:109
  (66 shorter events, 37.6 us)
Async XLA Ops:
  3.4 3.0 copy-start.1
  98.4 89.8 %copy-start.3 = (s32[1,4096]{1,0:T(1,128)S(1)}, s32[1,4096]{1,0:T(1,128)}, u32[]{:S(2)}) copy-start(s32[1,4096]{1,0:T(1,128)} %param.14) | copy-start | bytes 49156
  98.4 127.4 %copy-start.4 = (f32[1,4096]{1,0:T(1,128)S(1)}, f32[1,4096]{1,0:T(1,128)}, u32[]{:S(2)}) copy-start(f32[1,4096]{1,0:T(1,128)} %param.15) | copy-start | bytes 49156
  98.4 127.4 %copy-start.5 = (f32[1,4096]{1,0:T(1,128)S(1)}, f32[1,4096]{1,0:T(1,128)}, u32[]{:S(2)}) copy-start(f32[1,4096]{1,0:T(1,128)} %param.17) | copy-start | bytes 49156
  98.5 127.4 %copy-start.6 = (f32[1,4096]{1,0:T(1,128)S(1)}, f32[1,4096]{1,0:T(1,128)}, u32[]{:S(2)}) copy-start(f32[1,4096]{1,0:T(1,128)} %param.16) | copy-start | bytes 49156
  98.5 127.4 %copy-start.7 = (f32[1,4096]{1,0:T(1,128)S(1)}, f32[1,4096]{1,0:T(1,128)}, u32[]{:S(2)}) copy-start(f32[1,4096]{1,0:T(1,128)} %param.19) | copy-start | bytes 49156
  98.5 127.4 %copy-start.8 = (f32[1,4096]{1,0:T(1,128)S(1)}, f32[1,4096]{1,0:T(1,128)}, u32[]{:S(2)}) copy-start(f32[1,4096]{1,0:T(1,128)} %param.18) | copy-start | bytes 49156
  189.2 36.1 %all-to-all-start = ((f32[2,128,32]{2,0,1:T(2,128)}), f32[2,128,32]{2,0,1:T(2,128)S(1)}, u32[]{:S(2)}, u32[]{:S(2)}) async-start(f32[2,128,32]{2,0,1:T(2,128)} %copy.63), calls=%async_computation | async-start | bytes 262144 | tf_op jit(solution)/shard_map/all_to_all | solution.py:66
  228.8 14.2 %all-to-all-start.1 = ((f32[2,128,32]{2,0,1:T(2,128)}), f32[2,128,32]{2,0,1:T(2,128)S(1)}, u32[]{:S(2)}, u32[]{:S(2)}) async-start(f32[2,128,32]{2,0,1:T(2,128)} %copy.64), calls=%async_computation.1 | async-start | bytes 262144 | tf_op jit(solution)/shard_map/all_to_all | solution.py:76
  592.0 149.7 %all-to-all-start.3 = ((f32[2,8,1024,128]{3,1,0,2:T(8,128)}), f32[2,8,1024,128]{3,1,0,2:T(8,128)}, u32[]{:S(2)}, u32[]{:S(2)}) async-start(f32[2,8,1024,128]{3,1,0,2:T(8,128)} %copy.69), calls=%async_computation.3 | async-start | bytes 16777216 | tf_op jit(solution)/shard_map/all_to_all | solution.py:95
  770.6 59.1 %all-to-all-start.4 = ((f32[1,128,64,128]{3,2,0,1:T(8,128)}), f32[1,128,64,128]{3,2,0,1:T(8,128)}, u32[]{:S(2)}, u32[]{:S(2)}) async-start(f32[1,128,64,128]{3,2,0,1:T(8,128)} %copy.75), calls=%async_computation.4 | async-start | bytes 8388608 | tf_op jit(solution)/shard_map/all_to_all | solution.py:107
  829.7 3.4 copy-start
  866.5 65.6 %all-to-all-start.5 = ((f32[1,8,128,1024]{2,1,0,3:T(8,128)}), f32[1,8,128,1024]{2,1,0,3:T(8,128)}, u32[]{:S(2)}, u32[]{:S(2)}) async-start(f32[1,8,128,1024]{2,1,0,3:T(8,128)} %copy.78), calls=%async_computation.5 | async-start | bytes 8388608 | tf_op jit(solution)/shard_map/all_to_all | solution.py:111
  938.7 5.0 copy-start.2
where the time goes:
time: 975 us; the launch traced here: 962 us
  local copies, waits for them, and re-layouts  268 us (27%)
  matrix products  239 us (25%)
  waiting for transfers between devices  196 us (20%)
  other arithmetic  103 us (11%)
  blocking collectives  98.1 us (10%)
  starting transfers between devices  55.8 us (6%)
    all_to_all x1, waiting for transfers between devices, body(): lax.all_to_all(modes_xy, 'py', split_axis=2, concat_axis=1, tiled=True)  144 us
    all_to_all x1, blocking collectives, body(): lax.all_to_all(modes_x, 'px', split_axis=2, concat_axis=3, tiled=True)  98.1 us
    dot_general x1, matrix products, body(): modes_x = jnp.einsum('fzyx,xk->fzky', fields, basis_x, precision=highest)  90.6 us
    dot_general x1, matrix products, body(): jnp.einsum('fzky,ym->fzmk', lax.all_to_all(modes_x, 'px', split_axis=2, c...  90.6 us
    gather x1, local copies, waits for them, and re-layouts, body(): w_flat[safe_ids]  89.7 us
    gather x1, local copies, waits for them, and re-layouts, body(): temp_flat[safe_ids]  89 us
    all_to_all x1, waiting for transfers between devices, body(): lax.all_to_all(outgoing[None], 'py', split_axis=1, concat_axis=2, tiled=T...  32.1 us
    dot_general x1, matrix products, body(): jnp.einsum('fzmk,ym->fzky', returned_z, basis_y, precision=highest)  28 us
  transfers between devices with their start and end apart: 5, of which 4 were waited for; matrix products, arithmetic and copies ran while one was open for 8% of the time, Pallas kernels for 0%

commit v1 on v0

v1 whole, which is shorter than its diff:
```python
import functools
import math

import jax
import jax.numpy as jnp
import numpy as np
from jax import lax
from jax.experimental import pallas as pl
from jax.experimental.pallas import tpu as pltpu
from jax.sharding import PartitionSpec as P

N = 1024
NPX, NPY = 8, 16
LEV, ROWS = 8, 128
OWNERS, SLOT = 128, 32
MIB = 1 << 20
F32, BF16 = jnp.float32, jnp.bfloat16


def mode_table():
    classes = [np.arange(0, 513, 4), np.arange(2, 513, 4), np.arange(1, 512, 2)]
    n = np.arange(N)
    cols, waves = [], []
    for ks in classes:
        for k in ks:
            edge = k == 0 or k == N // 2
            norm = math.sqrt((1.0 if edge else 2.0) / N)
            cols.append(norm * np.cos(2 * np.pi * ((n * k) % N) / N))
            waves.append(k)
        for k in ks:
            if k == 0 or k == N // 2:
                continue
            cols.append(math.sqrt(2.0 / N) * np.sin(2 * np.pi * ((n * k) % N) / N))
            waves.append(k)
    table = np.stack(cols, axis=1)
    eigen = -4.0 * np.sin(np.pi * np.array(waves) / N) ** 2
    return table, eigen


def split_np(a):
    a = a.astype(np.float32)
    hi = a.astype(jnp.bfloat16)
    lo = (a - hi.astype(np.float32)).astype(jnp.bfloat16)
    return hi, lo


TABLE, EIGEN = mode_table()
T_EE = TABLE[:256, :256]
T_EO = TABLE[:256, 256:512]
T_OD = TABLE[:512, 512:]


def split(v):
    hi = v.astype(BF16)
    return hi, (v - hi.astype(F32)).astype(BF16)


def dot3(ah, al, bh, bl):
    d = functools.partial(jnp.dot, preferred_element_type=F32)
    return d(ah, bh) + (d(al, bh) + d(ah, bl))


def params(mb, sem=None):
    return pltpu.CompilerParams(vmem_limit_bytes=mb * MIB)


VM = pl.BlockSpec(memory_space=pltpu.VMEM)
SM = pl.BlockSpec(memory_space=pltpu.SMEM)


def load_tiles(w_ref, a_ref, wt, tt):
    def one(i, c):
        for half in range(2):
            tr = 2 * i + half
            for ct in range(8):
                wt[pl.ds(pl.multiple_of(tr * 64 + ct * 8, 8), 8), :] = w_ref[
                    pl.ds(pl.multiple_of(tr * 8, 8), 8), ct * 128:(ct + 1) * 128]
        for ct in range(8):
            v = a_ref[pl.ds(pl.multiple_of(i * 16, 16), 16), ct * 128:(ct + 1) * 128].astype(F32)
            tt[pl.ds(pl.multiple_of(i * 128 + ct * 8, 8), 8), :] = v[:8]
            tt[pl.ds(pl.multiple_of(i * 128 + 64 + ct * 8, 8), 8), :] = v[8:]
        return c
    lax.fori_loop(0, 64, one, 0)


def gather_kernel(addr, ids_ref, w_ref, a_ref, wc_ref, tc_ref, wt, tt, gw, gt):
    load_tiles(w_ref, a_ref, wt, tt)

    def one(o, c):
        for s in range(SLOT):
            a = addr[o * SLOT + s]
            gw[pl.ds(s * OWNERS + o, 1), :] = wt[pl.ds(a, 1), :]
            gt[pl.ds(s * OWNERS + o, 1), :] = tt[pl.ds(a, 1), :]
        return c
    lax.fori_loop(0, OWNERS, one, 0)
    ids = ids_ref[...]
    lane = lax.broadcasted_iota(jnp.int32, (OWNERS, 128), 1)
    slot = lax.broadcasted_iota(jnp.int32, (OWNERS, SLOT), 1)
    wc = jnp.zeros((OWNERS, SLOT), F32)
    tc = jnp.zeros((OWNERS, SLOT), F32)
    for s in range(SLOT):
        col = ids[:, s:s + 1]
        hit = lane == jnp.where(col >= 0, col & 127, -1)
        rows = slice(s * OWNERS, (s + 1) * OWNERS)
        wv = jnp.sum(jnp.where(hit, gw[rows, :], 0.0), axis=1, keepdims=True)
        tv = jnp.sum(jnp.where(hit, gt[rows, :], 0.0), axis=1, keepdims=True)
        wc = jnp.where(slot == s, wv, wc)
        tc = jnp.where(slot == s, tv, tc)
    wc_ref[...] = wc
    tc_ref[...] = tc


def gather_cells(addr, ids, w2, a2):
    out = jax.ShapeDtypeStruct((OWNERS, SLOT), F32)
    return pl.pallas_call(
        gather_kernel, out_shape=(out, out), in_specs=[SM, VM, VM, VM], out_specs=(VM, VM),
        scratch_shapes=[pltpu.VMEM((8192, 128), F32), pltpu.VMEM((8192, 128), F32),
                        pltpu.VMEM((4096, 128), F32), pltpu.VMEM((4096, 128), F32)],
        compiler_params=params(40), name="facet_gather",
    )(addr, ids, w2, a2)


def scatter_kernel(addr, ids_ref, wc_ref, tc_ref, od_ref, w_ref, a_ref,
                   wo_ref, th_ref, heat_ref, wt, tt, cw, ct_):
    load_tiles(w_ref, a_ref, wt, tt)
    ids = ids_ref[...]
    wc, tc = wc_ref[...], tc_ref[...]
    ft, drag, heat = od_ref[:, 0:32], od_ref[:, 32:64], od_ref[:, 64:96]
    speed = jnp.sqrt(wc * wc + 0.25)
    stress = drag * speed * wc
    flux = heat * speed * (ft - tc)
    heat_ref[...] = flux
    lane = lax.broadcasted_iota(jnp.int32, (OWNERS, 128), 1)
    for s in range(SLOT):
        col = ids[:, s:s + 1]
        hit = lane == jnp.where(col >= 0, col & 127, -1)
        rows = slice(s * OWNERS, (s + 1) * OWNERS)
        cw[rows, :] = jnp.where(hit, -stress[:, s:s + 1], 0.0)
        ct_[rows, :] = jnp.where(hit, flux[:, s:s + 1], 0.0)

    def one(o, c):
        for s in range(SLOT):
            a = addr[o * SLOT + s]
            wt[pl.ds(a, 1), :] = wt[pl.ds(a, 1), :] + cw[pl.ds(s * OWNERS + o, 1), :]
            tt[pl.ds(a, 1), :] = tt[pl.ds(a, 1), :] + ct_[pl.ds(s * OWNERS + o, 1), :]
        return c
    lax.fori_loop(0, OWNERS, one, 0)

    def put(i, c):
        for half in range(2):
            tr = 2 * i + half
            for ct in range(8):
                wo_ref[pl.ds(pl.multiple_of(tr * 8, 8), 8), ct * 128:(ct + 1) * 128] = wt[
                    pl.ds(pl.multiple_of(tr * 64 + ct * 8, 8), 8), :]
        for ct in range(8):
            v0 = tt[pl.ds(pl.multiple_of(i * 128 + ct * 8, 8), 8), :]
            v1 = tt[pl.ds(pl.multiple_of(i * 128 + 64 + ct * 8, 8), 8), :]
            th_ref[pl.ds(pl.multiple_of(i * 16, 16), 16), ct * 128:(ct + 1) * 128] = (
                jnp.concatenate([v0, v1], axis=0).astype(BF16))
        return c
    lax.fori_loop(0, 64, put, 0)


def scatter_fluxes(addr, ids, wc, tc, od, w2, a2):
    return pl.pallas_call(
        scatter_kernel,
        out_shape=(jax.ShapeDtypeStruct((1024, 1024), F32), jax.ShapeDtypeStruct((1024, 1024), BF16),
                   jax.ShapeDtypeStruct((OWNERS, SLOT), F32)),
        in_specs=[SM, VM, VM, VM, VM, VM, VM], out_specs=(VM, VM, VM),
        scratch_shapes=[pltpu.VMEM((8192, 128), F32), pltpu.VMEM((8192, 128), F32),
                        pltpu.VMEM((4096, 128), F32), pltpu.VMEM((4096, 128), F32)],
        compiler_params=params(48), name="facet_scatter",
    )(addr, ids, wc, tc, od, w2, a2)


def x_forward_kernel(h_ref, w_ref, wn_ref, halo_ref, eh, el, oh, ol, dh, dl, out_ref):
    step = pl.program_id(0)
    up = jnp.where(step == 3, halo_ref[0], wn_ref[0])
    r0 = h_ref[0] + w_ref[1] - w_ref[0]
    r1 = h_ref[1] + up - w_ref[1]
    r = jnp.concatenate([r0, r1], axis=0)
    s, d = r[:, :512] + r[:, 512:], r[:, :512] - r[:, 512:]
    ee, eo = s[:, :256] + s[:, 256:], s[:, :256] - s[:, 256:]

    def put(res, b0):
        for b in range(res.shape[1] // 128):
            for l in range(2):
                out_ref[b0 + b, l] = res[l * 128:(l + 1) * 128, b * 128:(b + 1) * 128]
    put(dot3(*split(ee), eh[...], el[...]), 0)
    put(dot3(*split(eo), oh[...], ol[...]), 2)
    put(dot3(*split(d), dh[...], dl[...]), 4)


def table_specs():
    small = pl.BlockSpec((256, 256), lambda g: (0, 0))
    big = pl.BlockSpec((512, 512), lambda g: (0, 0))
    return [small] * 4 + [big] * 2


def tables(transposed):
    out = []
    for t in (T_EE, T_EO, T_OD):
        out += [jnp.asarray(v) for v in split_np(t.T if transposed else t)]
    return out


def x_forward(h, w, halo):
    return pl.pallas_call(
        x_forward_kernel, grid=(4,),
        out_shape=jax.ShapeDtypeStruct((NPX, LEV, ROWS, 128), F32),
        in_specs=[pl.BlockSpec((2, 128, 1024), lambda g: (g, 0, 0)),
                  pl.BlockSpec((2, 128, 1024), lambda g: (g, 0, 0)),
                  pl.BlockSpec((1, 128, 1024), lambda g: (jnp.minimum(2 * g + 2, 7), 0, 0)),
                  pl.BlockSpec((1, 128, 1024), lambda g: (0, 0, 0))] + table_specs(),
        out_specs=pl.BlockSpec((NPX, 2, ROWS, 128), lambda g: (0, g, 0, 0)),
        compiler_params=params(40), name="x_forward",
    )(h, w, w, halo, *tables(False))


def slab_polys(lam):
    phi = [None] * 9
    phi[8] = jnp.ones_like(lam)
    delta = -lam
    phi[7] = phi[8] + delta
    for k in range(6, -1, -1):
        delta = delta - lam * phi[k + 1]
        phi[k] = phi[k + 1] + delta
    theta = [jnp.ones_like(lam), 2.0 - lam]
    for k in range(2, 8):
        theta.append((2.0 - lam) * theta[k - 1] - theta[k - 2])
    return phi, theta, delta


def y_forward_kernel(x_ref, lam_ref, eh, el, oh, ol, dh, dl, r_ref, al_ref, keep):
    step = pl.program_id(0)
    x = jnp.concatenate([x_ref[:, 0], x_ref[:, 1]], axis=-1).reshape(1024, 256)
    s, d = x[:512] + x[512:], x[:512] - x[512:]
    ee, eo = s[:256] + s[256:], s[:256] - s[256:]

    def left(th, tl, v):
        vh, vl = split(v)
        return dot3(th, tl, vh, vl)

    def put(res, k0):
        for l in range(2):
            part = res[:, l * 128:(l + 1) * 128]
            r_ref[l, k0:k0 + res.shape[0], :] = part
            keep[2 * step + l, k0:k0 + res.shape[0], :] = part
    put(left(eh[...], el[...], ee), 0)
    put(left(oh[...], ol[...], eo), 256)
    put(left(dh[...], dl[...], d), 512)

    @pl.when(step == 3)
    def _():
        def one(t, c):
            rows = pl.ds(pl.multiple_of(t * 16, 16), 16)
            phi, theta, _ = slab_polys(lam_ref[rows, :])
            inv = -1.0 / phi[0]
            a0 = phi[1] * keep[0, rows, :]
            a7 = keep[0, rows, :]
            for k in range(1, 8):
                a0 = a0 + phi[k + 1] * keep[k, rows, :]
                a7 = a7 + theta[k] * keep[k, rows, :]
            inner = pl.ds(pl.multiple_of((t % 4) * 16, 16), 16)
            al_ref[t // 4, 0, inner, :] = a0 * inv
            al_ref[t // 4, 1, inner, :] = a7 * inv
            return c
        lax.fori_loop(0, 64, one, 0)


def y_forward(x, lam):
    whole = pl.BlockSpec((N, 128), lambda g: (0, 0))
    return pl.pallas_call(
        y_forward_kernel, grid=(4,),
        out_shape=(jax.ShapeDtypeStruct((LEV, N, 128), F32), jax.ShapeDtypeStruct((NPY, 2, 64, 128), F32)),
        in_specs=[pl.BlockSpec((NPX, 2, ROWS, 128), lambda g: (0, g, 0, 0)), whole] + table_specs(),
        out_specs=(pl.BlockSpec((2, N, 128), lambda g: (g, 0, 0)),
                   pl.BlockSpec((NPY, 2, 64, 128), lambda g: (0, 0, 0, 0))),
        scratch_shapes=[pltpu.VMEM((LEV, N, 128), F32)],
        compiler_params=params(40), name="y_forward",
    )(x, lam, *tables(True))


def ladder_kernel(al_ref, lam_ref, out_ref):
    for t in range(8):
        rows = slice(t * 8, (t + 1) * 8)
        phi, theta, delta = slab_polys(lam_ref[rows, :])
        inv = 1.0 / phi[0]
        n07, n77, c = inv, theta[7] * inv, delta * inv
        A = [None] * 17
        B = [None] * 17
        e = [None] * 17
        A[16] = jnp.zeros_like(inv)
        B[16] = jnp.full_like(inv, -2.0)
        for j in range(15, -1, -1):
            g, q = al_ref[j, 0, rows, :], al_ref[j, 1, rows, :]
            e[j + 1] = 1.0 / (1.0 - n77 * B[j + 1])
            be = B[j + 1] * e[j + 1]
            A[j] = g + n07 * (A[j + 1] + be * (q + n77 * A[j + 1]))
            B[j] = n07 * n07 * be - c
        p = -A[0] / B[0]
        for j in range(16):
            out_ref[j, 0, rows, :] = p
            p = (al_ref[j, 1, rows, :] + n77 * A[j + 1] + n07 * p) * e[j + 1]
            out_ref[j, 1, rows, :] = A[j + 1] + B[j + 1] * p


def ladder(al, lam):
    return pl.pallas_call(
        ladder_kernel, out_shape=jax.ShapeDtypeStruct((NPY, 2, 64, 128), F32),
        in_specs=[VM, VM], out_specs=VM, compiler_params=params(16), name="ladder",
    )(al, lam)


def y_inverse_kernel(r_ref, pu_ref, lam_ref, eh, el, oh, ol, dh, dl, out_ref, sh, sl):
    step = pl.program_id(0)

    @pl.when(step == 0)
    def _():
        def one(t, c):
            rows = pl.ds(pl.multiple_of(t * 16, 16), 16)
            inner = pl.ds(pl.multiple_of((t % 4) * 16, 16), 16)
            low = pu_ref[t // 4, 0, inner, :]
            top = pu_ref[t // 4, 1, inner, :]
            lam = lam_ref[rows, :]
            cs = [None] * 8
            fs = [None] * 8
            cs[7] = 1.0 / (1.0 - lam)
            fs[7] = top_f = -r_ref[7, rows, :] - (-top)
            for k in range(6, -1, -1):
                cs[k] = 1.0 / (2.0 - lam - cs[k + 1])
                f = -r_ref[k, rows, :]
                if k == 0:
                    f = f + low
                fs[k] = f + cs[k + 1] * fs[k + 1]
            prev = low
            for k in range(8):
                p = cs[k] * (fs[k] + prev) if k else cs[k] * fs[k]
                hi, lo = split(p - prev)
                sh[k // 2, rows, (k % 2) * 128:(k % 2 + 1) * 128] = hi
                sl[k // 2, rows, (k % 2) * 128:(k % 2 + 1) * 128] = lo
                prev = p
            return c
        lax.fori_loop(0, 64, one, 0)

    def left(th, tl, lo, hi):
        return dot3(th, tl, sh[step, lo:hi, :], sl[step, lo:hi, :])
    t0 = left(eh[...], el[...], 0, 256)
    t1 = left(oh[...], ol[...], 256, 512)
    d = left(dh[...], dl[...], 512, 1024)
    ev = (t0 + t1, t0 - t1)
    for i in range(4):
        base = ev[i // 2][(i % 2) * 128:(i % 2 + 1) * 128]
        odd = d[i * 128:(i + 1) * 128]
        for l in range(2):
            cols = slice(l * 128, (l + 1) * 128)
            out_ref[i, l] = base[:, cols] + odd[:, cols]
            out_ref[i + 4, l] = base[:, cols] - odd[:, cols]


def y_inverse(r, pu, lam):
    return pl.pallas_call(
        y_inverse_kernel, grid=(4,),
        out_shape=jax.ShapeDtypeStruct((NPX, LEV, ROWS, 128), F32),
        in_specs=[pl.BlockSpec((LEV, N, 128), lambda g: (0, 0, 0)),
                  pl.BlockSpec((NPY, 2, 64, 128), lambda g: (0, 0, 0, 0)),
                  pl.BlockSpec((N, 128), lambda g: (0, 0))] + table_specs(),
        out_specs=pl.BlockSpec((NPX, 2, ROWS, 128), lambda g: (0, g, 0, 0)),
        scratch_shapes=[pltpu.VMEM((4, N, 256), BF16), pltpu.VMEM((4, N, 256), BF16)],
        compiler_params=params(40), name="y_inverse",
    )(r, pu, lam, *tables(False))


def x_inverse_kernel(base_ref, y_ref, w_ref, roof_ref, eh, el, oh, ol, dh, dl, out_ref):
    step = pl.program_id(0)

    def cat(b0, b1):
        return jnp.concatenate(
            [jnp.concatenate([y_ref[b, l] for b in range(b0, b1)], axis=1) for l in range(2)], axis=0)
    t0 = dot3(*split(cat(0, 2)), eh[...], el[...])
    t1 = dot3(*split(cat(2, 4)), oh[...], ol[...])
    d = dot3(*split(cat(4, 8)), dh[...], dl[...])
    s = jnp.concatenate([t0 + t1, t0 - t1], axis=1)
    for half, slope in ((0, s + d), (1, s - d)):
        cols = slice(half * 512, (half + 1) * 512)
        for l in range(2):
            level = base_ref[0] + 2 * step + l
            solid = level < roof_ref[:, cols]
            out_ref[l, :, cols] = jnp.where(solid, 0.0, w_ref[l, :, cols] - slope[l * 128:(l + 1) * 128])


def x_inverse(base, y, w, roof):
    return pl.pallas_call(
        x_inverse_kernel, grid=(4,),
        out_shape=jax.ShapeDtypeStruct((LEV, ROWS, N), F32),
        in_specs=[SM, pl.BlockSpec((NPX, 2, ROWS, 128), lambda g: (0, g, 0, 0)),
                  pl.BlockSpec((2, ROWS, N), lambda g: (g, 0, 0)),
                  pl.BlockSpec((ROWS, N), lambda g: (0, 0))] + table_specs(),
        out_specs=pl.BlockSpec((2, ROWS, N), lambda g: (g, 0, 0)),
        compiler_params=params(40), name="x_inverse",
    )(base, y, w, roof, *tables(True))


def swap(x, axes):
    return lax.all_to_all(x, axes, split_axis=0, concat_axis=0, tiled=True)


def body(horiz_div, w_star, air_temp, roof_level, facet_cells, facet_temp, net_radiation,
         heat_capacity, drag_coef, heat_coef):
    ix, iy = lax.axis_index("px"), lax.axis_index("py")
    owner = jnp.concatenate(
        [v.reshape(OWNERS, 1, SLOT) for v in (facet_temp, drag_coef, heat_coef, jnp.zeros_like(heat_coef))],
        axis=2)
    arrived = swap(owner, ("px", "py")).reshape(OWNERS, 128)
    cells = facet_cells[0]
    safe = jnp.maximum(cells, 0)
    row = safe >> 10
    addr = (row >> 3) * 64 + ((safe >> 7) & 7) * 8 + (row & 7)
    ids = facet_cells.reshape(OWNERS, SLOT)
    w2, a2 = w_star.reshape(1024, 1024), air_temp.reshape(1024, 1024)
    wc, tc = gather_cells(addr, ids, w2, a2)
    w_corr, theta, flux = scatter_fluxes(addr, ids, wc, tc, arrived, w2, a2)
    flux_back = swap(flux.reshape(OWNERS, 1, SLOT), ("px", "py")).reshape(1, OWNERS * SLOT)
    temp_new = facet_temp + (net_radiation - flux_back - 0.5 * facet_temp) / heat_capacity
    w_corr = w_corr.reshape(LEV, ROWS, N)
    halo = lax.ppermute(w_corr[:1], "py", [(j, j - 1) for j in range(1, NPY)])

    eig = jnp.asarray(EIGEN.astype(np.float32))
    eig_x = lax.dynamic_slice_in_dim(eig, ix * 128, 128)
    eig_y = lax.dynamic_slice_in_dim(eig, iy * 64, 64)
    lam = eig[:, None] + eig_x[None, :]
    lam_mine = eig_y[:, None] + eig_x[None, :]

    xs = swap(x_forward(horiz_div, w_corr, halo), "px")
    r, al = y_forward(xs, lam)
    pu = swap(ladder(swap(al, "py"), lam_mine), "py")
    ys = swap(y_inverse(r, pu, lam), "px")
    base = (iy * LEV).astype(jnp.int32).reshape(1)
    w_new = x_inverse(base, ys, w_corr, roof_level)
    return w_new, theta.reshape(LEV, ROWS, N), temp_new


def solution(mesh):
    field, facet = P("py", "px", None), P(("px", "py"), None)
    return jax.shard_map(
        body, mesh=mesh,
        in_specs=(field, field, field, P("px", None)) + (facet,) * 6,
        out_specs=(field, field, facet), check_vma=False)
```

time: 975 us -> 293 us (0.30); the launches traced: 962 us -> 291 us
  local copies, waits for them, and re-layouts: 268 us -> 28 us
  matrix products: 239 us -> 0 us
  other arithmetic: 103 us -> 8.06 us
  blocking collectives: 98.1 us -> 18.3 us
  waiting for transfers between devices: 196 us -> 124 us
  Pallas kernels: 0 us -> 70.6 us
  starting transfers between devices: 55.8 us -> 41.2 us
    dot_general x6 -> x0, matrix products: 239 us -> none  [the longest x1 90.6 us: body(): modes_x = jnp.einsum('fzyx,xk->fzky', fields, basis_x, precision=highest)]
    gather x2 -> x0, local copies, waits for them, and re-layouts: 179 us -> none  [the longest x1 89.7 us: body(): w_flat[safe_ids]]
    all_to_all x5, waiting for transfers between devices: 196 us -> 111 us  [swap(): return lax.all_to_all(x, axes, split_axis=0, concat_axis=0, tiled=True)]
    all_to_all x1, blocking collectives: 98.1 us -> 18.3 us  [swap(): return lax.all_to_all(x, axes, split_axis=0, concat_axis=0, tiled=True)]
    pallas_call x0 -> x7, Pallas kernels: none -> 70.6 us  [the longest x1 31.6 us: scatter_fluxes(): pl.pallas_call(scatter_kernel, out_shape=(jax.ShapeDtypeStruct((1024, 102...]
    scatter-add x2 -> x0, other arithmetic: 52 us -> none  [the longest x1 26.3 us: body(): w_corr = w_flat.at[safe_ids].add(-momentum_sink).reshape(w_star.shape)]
    dot_general x3 -> x0, other arithmetic: 41 us -> none  [the longest x1 18.4 us: body(): jnp.einsum('fzmk,ym->fzky', returned_z, basis_y, precision=highest)]
    all_to_all x5 -> x0, local copies, waits for them, and re-layouts: 33 us -> none  [the longest x2 17.4 us: body(): lax.all_to_all(modes_x, 'px', split_axis=2, concat_axis=3, tiled=True)]
  transfers between devices with their start and end apart: 5 -> 6, of which waited for: 4 -> 4; matrix products, arithmetic and copies ran while one was open for 8% -> 1% of each run, Pallas kernels for 0% -> 7%
where the time goes in v1:
time: 293 us; the launch traced here: 291 us
  waiting for transfers between devices  124 us (42%)
  Pallas kernels  70.6 us (24%)
  starting transfers between devices  41.2 us (14%)
  local copies, waits for them, and re-layouts  28 us (10%)
  blocking collectives  18.3 us (6%)
  other arithmetic  8.06 us (3%)
    all_to_all x5, waiting for transfers between devices, swap(): return lax.all_to_all(x, axes, split_axis=0, concat_axis=0, tiled=True)  111 us
    all_to_all x5, starting transfers between devices, swap(): return lax.all_to_all(x, axes, split_axis=0, concat_axis=0, tiled=True)  40 us
    pallas_call x1, Pallas kernels, scatter_fluxes(): pl.pallas_call(scatter_kernel, out_shape=(jax.ShapeDtypeStruct((1024, 102...  31.6 us
    unnamed x78, local copies, waits for them, and re-layouts  26.3 us
    all_to_all x1, blocking collectives, swap(): return lax.all_to_all(x, axes, split_axis=0, concat_axis=0, tiled=True)  18.3 us
    ppermute x1, waiting for transfers between devices, body(): halo = lax.ppermute(w_corr[:1], 'py', [(j, j - 1) for j in range(1, NPY)])  12.9 us
    pallas_call x1, Pallas kernels, gather_cells(): pl.pallas_call(gather_kernel, out_shape=(out, out), in_specs=[SM, VM, VM,...  10.5 us
    pallas_call x1, Pallas kernels, y_inverse(): pl.pallas_call(y_inverse_kernel, grid=(4,), out_shape=jax.ShapeDtypeStruc...  8.48 us
  transfers between devices with their start and end apart: 6, of which 4 were waited for; matrix products, arithmetic and copies ran while one was open for 1% of the time, Pallas kernels for 7%

profile of v1, /device:TPU:1, one launch (start us, length us, event | category | flops | bytes accessed | tf_op | source)
XLA Modules:
  0.0 291.4 jit_solution(236843616851885949)
XLA Ops:
  1.2 1.4 reduce.17
  2.6 1.4 reduce.16
  4.0 1.4 reduce.18
  6.4 11.5 %all-to-all-start = ((f32[128,1,128]{2,1,0:T(1,128)}), f32[128,1,128]{2,1,0:T(1,128)S(1)}, u32[]{:S(2)}, u32[]{:S(2)}) async-start(f32[128,1,128]{2,1,0:T(1,128)} %bitcast.4), calls=%async_computation | async-start | bytes 131072 | tf_op jit(solution)/shard_map/all_to_all | solution.py:405
  18.5 1.4 fusion
  20.0 2.2 copy-done.1
  22.2 1.6 copy-done.4
  23.8 10.5 %facet_gather.1 = (f32[128,32]{1,0:T(8,128)S(1)}, f32[128,32]{1,0:T(8,128)S(1)}) custom-call(s32[4096]{0:T(1024)S(1)} %bitcast.21, s32[128,32]{1,0:T(8,128)S(1)} %reshape.66.ids_ref, f32[1024,1024]{1,0:T(8,128)S(1)} %bitcast.17, bf16[1024,1024]{1,0:T(8,128)(2,1)S(1)} %bitcast.18), custom_call_target="tpu_custom_call" | custom-call | tf_op jit(solution)/shard_map/facet_gather/pallas_call | solution.py:115
  36.6 1.3 copy-done.33
  37.9 31.6 %facet_scatter.1 = (f32[1024,1024]{1,0:T(8,128)}, bf16[1024,1024]{1,0:T(8,128)(2,1)}, f32[128,32]{1,0:T(8,128)}) custom-call(s32[4096]{0:T(1024)S(1)} %bitcast.22, s32[128,32]{1,0:T(8,128)S(1)} %reshape.66.ids_ref, f32[128,32]{1,0:T(8,128)S(1)} %copy-done.31, f32[128,32]{1,0:T(8,128)S(1)} %copy-done.33, f32[128,128]{1,0:T(8,128)S(1)} %bitcast.20, ...), custom_call_target="tpu_custom_call" | custom-call | tf_op jit(solution)/shard_map/facet_scatter/pallas_call | solution.py:165
  69.5 1.1 slice_bitcast_fusion
  70.6 1.3 collective-permute-start
  71.9 12.9 %collective-permute-done.halo_ref = f32[1,128,1024]{2,1,0:T(8,128)S(1)} collective-permute-done((f32[1,128,1024]{2,1,0:T(8,128)S(1)}, f32[1,128,1024]{2,1,0:T(8,128)S(1)}, u32[]{:S(2)}, u32[]{:S(2)}) %collective-permute-start) | collective-permute-done | bytes 524320 | tf_op jit(solution)/shard_map/ppermute | solution.py:426
  84.9 5.8 %x_forward.1 = f32[8,8,128,128]{3,2,1,0:T(8,128)S(1)} custom-call(f32[8,128,1024]{2,1,0:T(8,128)S(1)} %copy-done.6, f32[8,128,1024]{2,1,0:T(8,128)} %bitcast.13, f32[8,128,1024]{2,1,0:T(8,128)} %bitcast.14, f32[1,128,1024]{2,1,0:T(8,128)S(1)} %collective-permute-done.halo_ref, bf16[256,256]{1,0:T(8,128)(2,1)S(1)} %copy-done.19, ...), custom_call_target="tpu_custom_call" | custom-call | tf_op jit(solution)/shard_map/x_forward/pallas_call | solution.py:208
  90.8 2.0 copy-done.3
  92.8 6.6 %all-to-all-start.1 = ((f32[8,8,128,128]{3,2,1,0:T(8,128)}), f32[8,8,128,128]{3,2,1,0:T(8,128)}, u32[]{:S(2)}, u32[]{:S(2)}) async-start(f32[8,8,128,128]{3,2,1,0:T(8,128)} %copy-done.3), calls=%async_computation.1 | async-start | bytes 8388608 | tf_op jit(solution)/shard_map/all_to_all | solution.py:405
  99.6 48.6 %all-to-all-done.1.x_ref = f32[8,8,128,128]{3,2,1,0:T(8,128)} async-done(((f32[8,8,128,128]{3,2,1,0:T(8,128)}), f32[8,8,128,128]{3,2,1,0:T(8,128)}, u32[]{:S(2)}, u32[]{:S(2)}) %all-to-all-start.1) | async-done | bytes 4194336 | tf_op jit(solution)/shard_map/all_to_all | solution.py:405
  151.9 7.3 %y_forward.1 = (f32[8,1024,128]{2,1,0:T(8,128)S(1)}, f32[16,2,64,128]{3,2,1,0:T(8,128)S(1)}) custom-call(f32[8,8,128,128]{3,2,1,0:T(8,128)} %all-to-all-done.1.x_ref, f32[1024,128]{1,0:T(8,128)S(1)} %broadcast_add_fusion.lam_ref, bf16[256,256]{1,0:T(8,128)(2,1)S(1)} %copy-done.27, bf16[256,256]{1,0:T(8,128)(2,1)S(1)} %copy-done.25, ...), custom_call_target="tpu_custom_call" | custom-call | tf_op jit(solution)/shard_map/y_forward/pallas_call | solution.py:273
  159.2 2.0 copy-done.7
  161.2 1.0 copy-done.14
  162.2 9.2 %all-to-all-start.2 = ((f32[16,2,64,128]{3,2,1,0:T(8,128)}), f32[16,2,64,128]{3,2,1,0:T(8,128)S(1)}, u32[]{:S(2)}, u32[]{:S(2)}) async-start(f32[16,2,64,128]{3,2,1,0:T(8,128)} %copy-done.14), calls=%async_computation.2 | async-start | bytes 2097152 | tf_op jit(solution)/shard_map/all_to_all | solution.py:405
  171.5 15.2 %all-to-all-done.2.al_ref = f32[16,2,64,128]{3,2,1,0:T(8,128)S(1)} async-done(((f32[16,2,64,128]{3,2,1,0:T(8,128)}), f32[16,2,64,128]{3,2,1,0:T(8,128)S(1)}, u32[]{:S(2)}, u32[]{:S(2)}) %all-to-all-start.2) | async-done | bytes 1048608 | tf_op jit(solution)/shard_map/all_to_all | solution.py:405
  187.2 18.3 %all_to_all.30.pu_ref = f32[16,2,64,128]{3,2,1,0:T(8,128)S(1)} all-to-all(f32[16,2,64,128]{3,2,1,0:T(8,128)S(1)} %ladder.1), channel_id=1, replica_groups=mesh['px'=8,'py'=16] {'py'}, dimensions={0} | all-to-all | bytes 2097152 | tf_op jit(solution)/shard_map/all_to_all | solution.py:405
  205.5 7.1 %all-to-all-start.5 = ((f32[128,1,32]{2,1,0:T(1,128)}), f32[128,1,32]{2,1,0:T(1,128)S(1)}, u32[]{:S(2)}, u32[]{:S(2)}) async-start(f32[128,1,32]{2,1,0:T(1,128)} %bitcast.10), calls=%async_computation.5 | async-start | bytes 131072 | tf_op jit(solution)/shard_map/all_to_all | solution.py:405
  212.6 2.2 copy-done.8
  214.8 1.0 copy-done.13
  217.6 8.5 %y_inverse.1 = f32[8,8,128,128]{3,2,1,0:T(8,128)S(1)} custom-call(f32[8,1024,128]{2,1,0:T(8,128)S(1)} %copy-done.8, f32[16,2,64,128]{3,2,1,0:T(8,128)S(1)} %all_to_all.30.pu_ref, f32[1024,128]{1,0:T(8,128)S(1)} %broadcast_add_fusion.lam_ref, bf16[256,256]{1,0:T(8,128)(2,1)S(1)} %copy-done.20, bf16[256,256]{1,0:T(8,128)(2,1)S(1)} %copy-done.18, ...), custom_call_target="tpu_custom_call" | custom-call | tf_op jit(solution)/shard_map/y_inverse/pallas_call | solution.py:362
  226.1 2.0 copy-done.2
  228.1 5.6 %all-to-all-start.4 = ((f32[8,8,128,128]{3,2,1,0:T(8,128)}), f32[8,8,128,128]{3,2,1,0:T(8,128)}, u32[]{:S(2)}, u32[]{:S(2)}) async-start(f32[8,8,128,128]{3,2,1,0:T(8,128)} %copy-done.2), calls=%async_computation.4 | async-start | bytes 8388608 | tf_op jit(solution)/shard_map/all_to_all | solution.py:405
  235.4 47.4 %all-to-all-done.4.y_ref = f32[8,8,128,128]{3,2,1,0:T(8,128)} async-done(((f32[8,8,128,128]{3,2,1,0:T(8,128)}), f32[8,8,128,128]{3,2,1,0:T(8,128)}, u32[]{:S(2)}, u32[]{:S(2)}) %all-to-all-start.4) | async-done | bytes 4194336 | tf_op jit(solution)/shard_map/all_to_all | solution.py:405
  282.8 2.2 copy-done
  284.9 6.5 %x_inverse.1 = f32[8,128,1024]{2,1,0:T(8,128)} custom-call(s32[1]{0:T(128)} %bitcast.base_ref, f32[8,8,128,128]{3,2,1,0:T(8,128)} %all-to-all-done.4.y_ref, f32[8,128,1024]{2,1,0:T(8,128)S(1)} %bitcast.15, s32[128,1024]{1,0:T(8,128)S(1)} %copy-done.29, bf16[256,256]{1,0:T(8,128)(2,1)S(1)} %copy-done.28, bf16[256,256]{1,0:T(8,128)(2,1)S(1)} %copy-done.26, ...), custom_call_target="tpu_custom_call" | custom-call | tf_op jit(solution)/shard_map/x_inverse/pallas_call | solution.py:393
  (85 shorter events, 12.4 us)
Async XLA Ops:
  6.4 29.1 %all-to-all-start = ((f32[128,1,128]{2,1,0:T(1,128)}), f32[128,1,128]{2,1,0:T(1,128)S(1)}, u32[]{:S(2)}, u32[]{:S(2)}) async-start(f32[128,1,128]{2,1,0:T(1,128)} %bitcast.4), calls=%async_computation | async-start | bytes 131072 | tf_op jit(solution)/shard_map/all_to_all | solution.py:405
  20.0 2.2 copy-start.1
  22.2 1.6 copy-start.4
  23.8 11.8 %copy-start.5 = (bf16[8,128,1024]{2,1,0:T(8,128)(2,1)S(1)}, bf16[8,128,1024]{2,1,0:T(8,128)(2,1)}, u32[]{:S(2)}) copy-start(bf16[8,128,1024]{2,1,0:T(8,128)(2,1)} %param.37) | copy-start | bytes 6291460
  35.5 49.3 %copy-start.11 = (bf16[512,512]{1,0:T(8,128)(2,1)S(1)}, bf16[512,512]{1,0:T(8,128)(2,1)}, u32[]{:S(2)}) copy-start(bf16[512,512]{1,0:T(8,128)(2,1)} %constant.64.clone.dl) | copy-start | bytes 1572868
  35.5 49.3 %copy-start.12 = (bf16[512,512]{1,0:T(8,128)(2,1)S(1)}, bf16[512,512]{1,0:T(8,128)(2,1)}, u32[]{:S(2)}) copy-start(bf16[512,512]{1,0:T(8,128)(2,1)} %constant.63.clone.dh) | copy-start | bytes 1572868
  35.5 49.3 %copy-start.15 = (bf16[256,256]{1,0:T(8,128)(2,1)S(1)}, bf16[256,256]{1,0:T(8,128)(2,1)}, u32[]{:S(2)}) copy-start(bf16[256,256]{1,0:T(8,128)(2,1)} %constant.62.clone.ol) | copy-start | bytes 393220
  35.5 49.3 %copy-start.16 = (bf16[256,256]{1,0:T(8,128)(2,1)S(1)}, bf16[256,256]{1,0:T(8,128)(2,1)}, u32[]{:S(2)}) copy-start(bf16[256,256]{1,0:T(8,128)(2,1)} %constant.61.clone.oh) | copy-start | bytes 393220
  35.6 49.3 %copy-start.6 = (f32[8,128,1024]{2,1,0:T(8,128)S(1)}, f32[8,128,1024]{2,1,0:T(8,128)}, u32[]{:S(2)}) copy-start(f32[8,128,1024]{2,1,0:T(8,128)} %h_ref.1) | copy-start | bytes 12582916
  35.6 49.3 %copy-start.17 = (bf16[256,256]{1,0:T(8,128)(2,1)S(1)}, bf16[256,256]{1,0:T(8,128)(2,1)}, u32[]{:S(2)}) copy-start(bf16[256,256]{1,0:T(8,128)(2,1)} %constant.60.clone.el) | copy-start | bytes 393220
  35.6 49.3 %copy-start.19 = (bf16[256,256]{1,0:T(8,128)(2,1)S(1)}, bf16[256,256]{1,0:T(8,128)(2,1)}, u32[]{:S(2)}) copy-start(bf16[256,256]{1,0:T(8,128)(2,1)} %constant.59.clone.eh) | copy-start | bytes 393220
  70.6 14.2 %collective-permute-start = (f32[1,128,1024]{2,1,0:T(8,128)S(1)}, f32[1,128,1024]{2,1,0:T(8,128)S(1)}, u32[]{:S(2)}, u32[]{:S(2)}) collective-permute-start(f32[1,128,1024]{2,1,0:T(8,128)S(1)} %slice_bitcast_fusion), channel_id=1, source_target_pairs={{1,0},{2,1},{3,2},{4,3},{5,4},{6,5},{7,6},{8,7},{9,8},{10,9},{11,1... | collective-permute-start | bytes 1572872 | tf_op jit(solution)/shard_map/ppermute | solution.py:426
  90.7 2.0 copy-start.3
  92.8 6.6 %copy-start.37 = (f32[1024]{0:T(1024)S(1)}, f32[1024]{0:T(1024)}, u32[]{:S(2)}) copy-start(f32[1024]{0:T(1024)} %constant.58.clone) | copy-start | bytes 12292
  92.8 55.5 %copy-start.9 = (bf16[512,512]{1,0:T(8,128)(2,1)S(1)}, bf16[512,512]{1,0:T(8,128)(2,1)}, u32[]{:S(2)}) copy-start(bf16[512,512]{1,0:T(8,128)(2,1)} %constant.70.clone.dl) | copy-start | bytes 1572868
  92.8 55.5 %copy-start.10 = (bf16[512,512]{1,0:T(8,128)(2,1)S(1)}, bf16[512,512]{1,0:T(8,128)(2,1)}, u32[]{:S(2)}) copy-start(bf16[512,512]{1,0:T(8,128)(2,1)} %constant.69.clone.dh) | copy-start | bytes 1572868
  92.8 55.5 %all-to-all-start.1 = ((f32[8,8,128,128]{3,2,1,0:T(8,128)}), f32[8,8,128,128]{3,2,1,0:T(8,128)}, u32[]{:S(2)}, u32[]{:S(2)}) async-start(f32[8,8,128,128]{3,2,1,0:T(8,128)} %copy-done.3), calls=%async_computation.1 | async-start | bytes 8388608 | tf_op jit(solution)/shard_map/all_to_all | solution.py:405
  159.2 2.0 copy-start.7
  162.2 24.5 %all-to-all-start.2 = ((f32[16,2,64,128]{3,2,1,0:T(8,128)}), f32[16,2,64,128]{3,2,1,0:T(8,128)S(1)}, u32[]{:S(2)}, u32[]{:S(2)}) async-start(f32[16,2,64,128]{3,2,1,0:T(8,128)} %copy-done.14), calls=%async_computation.2 | async-start | bytes 2097152 | tf_op jit(solution)/shard_map/all_to_all | solution.py:405
  205.5 22.6 %all-to-all-start.5 = ((f32[128,1,32]{2,1,0:T(1,128)}), f32[128,1,32]{2,1,0:T(1,128)S(1)}, u32[]{:S(2)}, u32[]{:S(2)}) async-start(f32[128,1,32]{2,1,0:T(1,128)} %bitcast.10), calls=%async_computation.5 | async-start | bytes 131072 | tf_op jit(solution)/shard_map/all_to_all | solution.py:405
  212.6 2.2 copy-start.8
  226.1 2.0 copy-start.2
  228.1 6.6 %copy-start.34 = (f32[1,4096]{1,0:T(1,128)S(1)}, f32[1,4096]{1,0:T(1,128)}, u32[]{:S(2)}) copy-start(f32[1,4096]{1,0:T(1,128)} %param.40) | copy-start | bytes 49156
  228.1 6.6 %copy-start.35 = (f32[1,4096]{1,0:T(1,128)S(1)}, f32[1,4096]{1,0:T(1,128)}, u32[]{:S(2)}) copy-start(f32[1,4096]{1,0:T(1,128)} %param.42) | copy-start | bytes 49156
  228.1 6.6 %copy-start.36 = (f32[1,4096]{1,0:T(1,128)S(1)}, f32[1,4096]{1,0:T(1,128)}, u32[]{:S(2)}) copy-start(f32[1,4096]{1,0:T(1,128)} %param.41) | copy-start | bytes 49156
  228.1 54.6 %copy-start.22 = (bf16[256,256]{1,0:T(8,128)(2,1)S(1)}, bf16[256,256]{1,0:T(8,128)(2,1)}, u32[]{:S(2)}) copy-start(bf16[256,256]{1,0:T(8,128)(2,1)} %constant.68.clone.ol) | copy-start | bytes 393220
  228.1 54.6 %copy-start.24 = (bf16[256,256]{1,0:T(8,128)(2,1)S(1)}, bf16[256,256]{1,0:T(8,128)(2,1)}, u32[]{:S(2)}) copy-start(bf16[256,256]{1,0:T(8,128)(2,1)} %constant.67.clone.oh) | copy-start | bytes 393220
  228.1 54.6 %copy-start.26 = (bf16[256,256]{1,0:T(8,128)(2,1)S(1)}, bf16[256,256]{1,0:T(8,128)(2,1)}, u32[]{:S(2)}) copy-start(bf16[256,256]{1,0:T(8,128)(2,1)} %constant.66.clone.el) | copy-start | bytes 393220
  228.1 54.6 %copy-start.28 = (bf16[256,256]{1,0:T(8,128)(2,1)S(1)}, bf16[256,256]{1,0:T(8,128)(2,1)}, u32[]{:S(2)}) copy-start(bf16[256,256]{1,0:T(8,128)(2,1)} %constant.65.clone.eh) | copy-start | bytes 393220
  228.1 54.6 %copy-start.29 = (s32[128,1024]{1,0:T(8,128)S(1)}, s32[128,1024]{1,0:T(8,128)}, u32[]{:S(2)}) copy-start(s32[128,1024]{1,0:T(8,128)} %roof_ref.1) | copy-start | bytes 1572868
  228.1 54.6 %all-to-all-start.4 = ((f32[8,8,128,128]{3,2,1,0:T(8,128)}), f32[8,8,128,128]{3,2,1,0:T(8,128)}, u32[]{:S(2)}, u32[]{:S(2)}) async-start(f32[8,8,128,128]{3,2,1,0:T(8,128)} %copy-done.2), calls=%async_computation.4 | async-start | bytes 8388608 | tf_op jit(solution)/shard_map/all_to_all | solution.py:405
  282.8 2.2 copy-start
  (12 other events, 11.1 us)

commit v2 on v1

--- a/solution.py
+++ b/solution.py
@@ -173,7 +173,61 @@
     )(addr, ids, wc, tc, od, w2, a2)
 
 
-def x_forward_kernel(h_ref, w_ref, wn_ref, halo_ref, eh, el, oh, ol, dh, dl, out_ref):
+BLK = 2 * ROWS + 2 * LEV
+
+
+def z_basis():
+    k, m = np.arange(LEV)[:, None], np.arange(LEV)[None, :]
+    q = math.sqrt(4 / 17) * np.sin(np.pi * (2 * m + 1) * (k + 1) / 17)
+    theta = -4.0 * np.sin(np.pi * (2 * np.arange(LEV) + 1) / 34) ** 2
+    return q, theta
+
+
+def y_basis():
+    i = np.arange(ROWS) + 1
+    s = math.sqrt(2 / 129) * np.sin(np.pi * (np.outer(i, i) % 258) / 129)
+    mu = -4.0 * np.sin(np.pi * i / 258) ** 2
+    return s, mu
+
+
+Q, THETA = z_basis()
+DQ = Q - np.concatenate([np.zeros((1, LEV)), Q[:-1]])
+SINE, MU = y_basis()
+EDGE = np.concatenate([TABLE[0::ROWS], TABLE[ROWS - 1::ROWS]])
+
+
+def pack(transposed):
+    parts = [split_np(t.T if transposed else t) for t in (T_EE, T_EO, T_OD)]
+    (eh, el), (oh, ol), (dh, dl) = parts
+    return np.concatenate([dh, dl, np.concatenate([np.concatenate([eh, oh], 1), np.concatenate([el, ol], 1)])])
+
+
+TAB, TAB_T = pack(False), pack(True)
+SINE2 = np.concatenate(split_np(SINE))
+EDGE_F = np.concatenate(split_np(EDGE.T))
+EDGE_B = np.concatenate(split_np(EDGE))
+LAM_X = np.broadcast_to(EIGEN.astype(np.float32), (8, N)).copy()
+COLS = np.stack([np.broadcast_to(v[:, None], (ROWS, 128)) for v in (MU, SINE[:, 0], SINE[:, 127])]).astype(np.float32)
+
+
+def tab_parts(t):
+    return ((t[1024:1280, :256], t[1280:1536, :256]), (t[1024:1280, 256:], t[1280:1536, 256:]),
+            (t[:512], t[512:1024]))
+
+
+def combine(coefs, vs):
+    out = None
+    for c, v in zip(coefs, vs):
+        t = float(c) * v
+        out = t if out is None else out + t
+    return out
+
+
+def tile(i, size=8):
+    return pl.ds(pl.multiple_of(i * size, size), size)
+
+
+def block_forward_kernel(h_ref, w_ref, wn_ref, halo_ref, tab, sine, lx, cols, out_ref, g_ref, r2, a0, a7):
     step = pl.program_id(0)
     up = jnp.where(step == 3, halo_ref[0], wn_ref[0])
     r0 = h_ref[0] + w_ref[1] - w_ref[0]
@@ -181,40 +235,62 @@
     r = jnp.concatenate([r0, r1], axis=0)
     s, d = r[:, :512] + r[:, 512:], r[:, :512] - r[:, 512:]
     ee, eo = s[:, :256] + s[:, 256:], s[:, :256] - s[:, 256:]
-
-    def put(res, b0):
-        for b in range(res.shape[1] // 128):
-            for l in range(2):
-                out_ref[b0 + b, l] = res[l * 128:(l + 1) * 128, b * 128:(b + 1) * 128]
-    put(dot3(*split(ee), eh[...], el[...]), 0)
-    put(dot3(*split(eo), oh[...], ol[...]), 2)
-    put(dot3(*split(d), dh[...], dl[...]), 4)
-
-
-def table_specs():
-    small = pl.BlockSpec((256, 256), lambda g: (0, 0))
-    big = pl.BlockSpec((512, 512), lambda g: (0, 0))
-    return [small] * 4 + [big] * 2
-
-
-def tables(transposed):
-    out = []
-    for t in (T_EE, T_EO, T_OD):
-        out += [jnp.asarray(v) for v in split_np(t.T if transposed else t)]
-    return out
-
-
-def x_forward(h, w, halo):
-    return pl.pallas_call(
-        x_forward_kernel, grid=(4,),
-        out_shape=jax.ShapeDtypeStruct((NPX, LEV, ROWS, 128), F32),
+    te, to, td = tab_parts(tab)
+    sh, sl = sine[:128, :], sine[128:, :]
+    for v, t, c0 in ((ee, te, 0), (eo, to, 256), (d, td, 512)):
+        res = dot3(*split(v), t[0], t[1])
+        for l in range(2):
+            r2[2 * step + l, :, c0:c0 + res.shape[1]] = dot3(sh, sl, *split(res[l * 128:(l + 1) * 128]))
+
+    @pl.when(step == 3)
+    def _():
+        def lanes(lt, c):
+            ln = tile(lt, 128)
+            lam = lx[:, ln]
+
+            def inner(bt, acc):
+                rows = tile(bt)
+                rs = [r2[k, rows, ln] for k in range(LEV)]
+                mu, s0, s1 = cols[0, rows, :], cols[1, rows, :], cols[2, rows, :]
+                base = lam + mu
+                ps = []
+                for m in range(LEV):
+                    p = combine(Q[:, m], rs) / (base + float(THETA[m]))
+                    g_ref[m, rows, ln] = p
+                    ps.append(p)
+                a0[rows, ln] = combine(Q[0], ps)
+                a7[rows, ln] = combine(Q[7], ps)
+                return tuple(acc[m] + s0 * ps[m] for m in range(LEV)) + tuple(
+                    acc[LEV + m] + s1 * ps[m] for m in range(LEV))
+            acc = lax.fori_loop(0, ROWS // 8, inner, tuple(jnp.zeros((8, 128), F32) for _ in range(16)))
+            for e in range(2):
+                sums = [jnp.sum(acc[e * LEV + m], axis=0, keepdims=True) for m in range(LEV)]
+                out_ref[lt, 2 * ROWS + e * LEV:2 * ROWS + (e + 1) * LEV, :] = jnp.concatenate(
+                    [combine(Q[k], sums) for k in range(LEV)], axis=0)
+            return c
+        lax.fori_loop(0, NPX, lanes, 0)
+        for f, a in ((0, a0), (1, a7)):
+            res = dot3(sh, sl, *split(a[...]))
+            for b in range(NPX):
+                out_ref[b, f * ROWS:(f + 1) * ROWS, :] = res[:, b * 128:(b + 1) * 128]
+
+
+def fixed(shape):
+    return pl.BlockSpec(shape, lambda g: (0,) * len(shape))
+
+
+def block_forward(h, w, halo):
+    return pl.pallas_call(
+        block_forward_kernel, grid=(4,),
+        out_shape=(jax.ShapeDtypeStruct((NPX, BLK, 128), F32), jax.ShapeDtypeStruct((LEV, ROWS, N), F32)),
         in_specs=[pl.BlockSpec((2, 128, 1024), lambda g: (g, 0, 0)),
                   pl.BlockSpec((2, 128, 1024), lambda g: (g, 0, 0)),
                   pl.BlockSpec((1, 128, 1024), lambda g: (jnp.minimum(2 * g + 2, 7), 0, 0)),
-                  pl.BlockSpec((1, 128, 1024), lambda g: (0, 0, 0))] + table_specs(),
-        out_specs=pl.BlockSpec((NPX, 2, ROWS, 128), lambda g: (0, g, 0, 0)),
-        compiler_params=params(40), name="x_forward",
-    )(h, w, w, halo, *tables(False))
+                  fixed((1, 128, 1024)), fixed((1536, 512)), fixed((256, 128)), fixed((8, N)), fixed((3, ROWS, 128))],
+        out_specs=(fixed((NPX, BLK, 128)), fixed((LEV, ROWS, N))),
+        scratch_shapes=[pltpu.VMEM((LEV, ROWS, N), F32), pltpu.VMEM((ROWS, N), F32), pltpu.VMEM((ROWS, N), F32)],
+        compiler_params=params(48), name="block_forward",
+    )(h, w, w, halo, jnp.asarray(TAB), jnp.asarray(SINE2), jnp.asarray(LAM_X), jnp.asarray(COLS))
 
 
 def slab_polys(lam):
@@ -231,54 +307,50 @@
     return phi, theta, delta
 
 
-def y_forward_kernel(x_ref, lam_ref, eh, el, oh, ol, dh, dl, r_ref, al_ref, keep):
-    step = pl.program_id(0)
-    x = jnp.concatenate([x_ref[:, 0], x_ref[:, 1]], axis=-1).reshape(1024, 256)
+def y_forward_kernel(x_ref, lam_ref, tab, edge, s_ref, al_ref, pp, sr):
+    x = jnp.concatenate([x_ref[:, :ROWS], x_ref[:, ROWS:2 * ROWS]], axis=-1).reshape(N, 256)
     s, d = x[:512] + x[512:], x[:512] - x[512:]
     ee, eo = s[:256] + s[256:], s[:256] - s[256:]
-
-    def left(th, tl, v):
-        vh, vl = split(v)
-        return dot3(th, tl, vh, vl)
-
-    def put(res, k0):
-        for l in range(2):
-            part = res[:, l * 128:(l + 1) * 128]
-            r_ref[l, k0:k0 + res.shape[0], :] = part
-            keep[2 * step + l, k0:k0 + res.shape[0], :] = part
-    put(left(eh[...], el[...], ee), 0)
-    put(left(oh[...], ol[...], eo), 256)
-    put(left(dh[...], dl[...], d), 512)
-
-    @pl.when(step == 3)
-    def _():
-        def one(t, c):
-            rows = pl.ds(pl.multiple_of(t * 16, 16), 16)
-            phi, theta, _ = slab_polys(lam_ref[rows, :])
-            inv = -1.0 / phi[0]
-            a0 = phi[1] * keep[0, rows, :]
-            a7 = keep[0, rows, :]
-            for k in range(1, 8):
-                a0 = a0 + phi[k + 1] * keep[k, rows, :]
-                a7 = a7 + theta[k] * keep[k, rows, :]
-            inner = pl.ds(pl.multiple_of((t % 4) * 16, 16), 16)
-            al_ref[t // 4, 0, inner, :] = a0 * inv
-            al_ref[t // 4, 1, inner, :] = a7 * inv
-            return c
-        lax.fori_loop(0, 64, one, 0)
+    te, to, td = tab_parts(tab)
+    for v, t, k0 in ((ee, te, 0), (eo, to, 256), (d, td, 512)):
+        res = dot3(t[0], t[1], *split(v))
+        pp[k0:k0 + res.shape[0], :] = res
+    for i in range(NPX):
+        for k in range(LEV):
+            sr[i:i + 1, k * 128:(k + 1) * 128] = x_ref[(i + 7) % 8, 2 * ROWS + LEV + k:2 * ROWS + LEV + k + 1, :]
+            sr[8 + i:9 + i, k * 128:(k + 1) * 128] = x_ref[(i + 1) % 8, 2 * ROWS + k:2 * ROWS + k + 1, :]
+    sh, sl = split(sr[...])
+
+    def spread(i, c):
+        lo = tile(i, 256)
+        s_ref[lo, :] = dot3(edge[lo, :], edge[pl.ds(pl.multiple_of(N + i * 256, 256), 256), :], sh, sl)
+        return c
+    lax.fori_loop(0, 4, spread, 0)
+
+    def one(t, c):
+        rows = tile(t, 16)
+        phi, theta, _ = slab_polys(lam_ref[rows, :])
+        inv = 1.0 / phi[0]
+        b0 = b7 = None
+        for k in range(LEV):
+            sk = s_ref[rows, k * 128:(k + 1) * 128]
+            b0 = phi[k + 1] * sk if k == 0 else b0 + phi[k + 1] * sk
+            b7 = sk if k == 0 else b7 + theta[k] * sk
+        inner = tile(t % 4, 16)
+        al_ref[t // 4, 0, inner, :] = pp[rows, :128] + b0 * inv
+        al_ref[t // 4, 1, inner, :] = pp[rows, 128:] + b7 * inv
+        return c
+    lax.fori_loop(0, 64, one, 0)
 
 
 def y_forward(x, lam):
-    whole = pl.BlockSpec((N, 128), lambda g: (0, 0))
-    return pl.pallas_call(
-        y_forward_kernel, grid=(4,),
-        out_shape=(jax.ShapeDtypeStruct((LEV, N, 128), F32), jax.ShapeDtypeStruct((NPY, 2, 64, 128), F32)),
-        in_specs=[pl.BlockSpec((NPX, 2, ROWS, 128), lambda g: (0, g, 0, 0)), whole] + table_specs(),
-        out_specs=(pl.BlockSpec((2, N, 128), lambda g: (g, 0, 0)),
-                   pl.BlockSpec((NPY, 2, 64, 128), lambda g: (0, 0, 0, 0))),
-        scratch_shapes=[pltpu.VMEM((LEV, N, 128), F32)],
+    return pl.pallas_call(
+        y_forward_kernel,
+        out_shape=(jax.ShapeDtypeStruct((N, N), F32), jax.ShapeDtypeStruct((NPY, 2, 64, 128), F32)),
+        in_specs=[VM] * 4, out_specs=(VM, VM),
+        scratch_shapes=[pltpu.VMEM((N, 256), F32), pltpu.VMEM((16, N), F32)],
         compiler_params=params(40), name="y_forward",
-    )(x, lam, *tables(True))
+    )(x, lam, jnp.asarray(TAB_T), jnp.asarray(EDGE_F))
 
 
 def ladder_kernel(al_ref, lam_ref, out_ref):
@@ -312,93 +384,119 @@
     )(al, lam)
 
 
-def y_inverse_kernel(r_ref, pu_ref, lam_ref, eh, el, oh, ol, dh, dl, out_ref, sh, sl):
-    step = pl.program_id(0)
-
-    @pl.when(step == 0)
-    def _():
-        def one(t, c):
-            rows = pl.ds(pl.multiple_of(t * 16, 16), 16)
-            inner = pl.ds(pl.multiple_of((t % 4) * 16, 16), 16)
-            low = pu_ref[t // 4, 0, inner, :]
-            top = pu_ref[t // 4, 1, inner, :]
-            lam = lam_ref[rows, :]
-            cs = [None] * 8
-            fs = [None] * 8
-            cs[7] = 1.0 / (1.0 - lam)
-            fs[7] = top_f = -r_ref[7, rows, :] - (-top)
-            for k in range(6, -1, -1):
-                cs[k] = 1.0 / (2.0 - lam - cs[k + 1])
-                f = -r_ref[k, rows, :]
-                if k == 0:
-                    f = f + low
-                fs[k] = f + cs[k + 1] * fs[k + 1]
-            prev = low
-            for k in range(8):
-                p = cs[k] * (fs[k] + prev) if k else cs[k] * fs[k]
-                hi, lo = split(p - prev)
-                sh[k // 2, rows, (k % 2) * 128:(k % 2 + 1) * 128] = hi
-                sl[k // 2, rows, (k % 2) * 128:(k % 2 + 1) * 128] = lo
-                prev = p
-            return c
-        lax.fori_loop(0, 64, one, 0)
-
-    def left(th, tl, lo, hi):
-        return dot3(th, tl, sh[step, lo:hi, :], sl[step, lo:hi, :])
-    t0 = left(eh[...], el[...], 0, 256)
-    t1 = left(oh[...], ol[...], 256, 512)
-    d = left(dh[...], dl[...], 512, 1024)
+def y_inverse_kernel(s_ref, pu_ref, lam_ref, x_ref, tab, edge, out_ref, ph, pl_):
+    def one(t, c):
+        rows = tile(t, 16)
+        inner = tile(t % 4, 16)
+        low, top = pu_ref[t // 4, 0, inner, :], pu_ref[t // 4, 1, inner, :]
+        lam = lam_ref[rows, :]
+        cs = [None] * 8
+        fs = [None] * 8
+        cs[7] = 1.0 / (1.0 - lam)
+        fs[7] = s_ref[rows, 7 * 128:] + top
+        for k in range(6, -1, -1):
+            cs[k] = 1.0 / (2.0 - lam - cs[k + 1])
+            fs[k] = s_ref[rows, k * 128:(k + 1) * 128] + cs[k + 1] * fs[k + 1]
+        prev = low
+        for k in range(8):
+            prev = cs[k] * (fs[k] + prev)
+            ph[rows, k * 128:(k + 1) * 128], pl_[rows, k * 128:(k + 1) * 128] = split(prev)
+        return c
+    lax.fori_loop(0, 64, one, 0)
+    edges = dot3(edge[:16, :], edge[16:, :], ph[...], pl_[...])
+    for i in range(NPX):
+        below, above = (i + 7) % 8, (i + 1) % 8
+        for k in range(LEV):
+            cols = slice(k * 128, (k + 1) * 128)
+            lo = 2 * ROWS + k
+            hi = 2 * ROWS + LEV + k
+            out_ref[i, lo:lo + 1, :] = edges[8 + below:9 + below, cols] + x_ref[below, hi:hi + 1, :]
+            out_ref[i, hi:hi + 1, :] = edges[above:above + 1, cols] + x_ref[above, lo:lo + 1, :]
+    pu = jnp.concatenate([pu_ref[:, 0], pu_ref[:, 1]], axis=-1).reshape(N, 256)
+    te, to, td = tab_parts(tab)
+    t0 = dot3(te[0], te[1], *split(pu[:256]))
+    t1 = dot3(to[0], to[1], *split(pu[256:512]))
+    d = dot3(td[0], td[1], *split(pu[512:]))
     ev = (t0 + t1, t0 - t1)
     for i in range(4):
         base = ev[i // 2][(i % 2) * 128:(i % 2 + 1) * 128]
         odd = d[i * 128:(i + 1) * 128]
         for l in range(2):
             cols = slice(l * 128, (l + 1) * 128)
-            out_ref[i, l] = base[:, cols] + odd[:, cols]
-            out_ref[i + 4, l] = base[:, cols] - odd[:, cols]
-
-
-def y_inverse(r, pu, lam):
-    return pl.pallas_call(
-        y_inverse_kernel, grid=(4,),
-        out_shape=jax.ShapeDtypeStruct((NPX, LEV, ROWS, 128), F32),
-        in_specs=[pl.BlockSpec((LEV, N, 128), lambda g: (0, 0, 0)),
-                  pl.BlockSpec((NPY, 2, 64, 128), lambda g: (0, 0, 0, 0)),
-                  pl.BlockSpec((N, 128), lambda g: (0, 0))] + table_specs(),
-        out_specs=pl.BlockSpec((NPX, 2, ROWS, 128), lambda g: (0, g, 0, 0)),
-        scratch_shapes=[pltpu.VMEM((4, N, 256), BF16), pltpu.VMEM((4, N, 256), BF16)],
+            out_ref[i, l * ROWS:(l + 1) * ROWS, :] = base[:, cols] + odd[:, cols]
+            out_ref[i + 4, l * ROWS:(l + 1) * ROWS, :] = base[:, cols] - odd[:, cols]
+
+
+def y_inverse(s, pu, lam, x):
+    return pl.pallas_call(
+        y_inverse_kernel, out_shape=jax.ShapeDtypeStruct((NPX, BLK, 128), F32),
+        in_specs=[VM] * 6, out_specs=VM,
+        scratch_shapes=[pltpu.VMEM((N, N), BF16), pltpu.VMEM((N, N), BF16)],
         compiler_params=params(40), name="y_inverse",
-    )(r, pu, lam, *tables(False))
-
-
-def x_inverse_kernel(base_ref, y_ref, w_ref, roof_ref, eh, el, oh, ol, dh, dl, out_ref):
+    )(s, pu, lam, x, jnp.asarray(TAB), jnp.asarray(EDGE_B))
+
+
+def block_inverse_kernel(base_ref, y_ref, g_ref, w_ref, roof_ref, tab, sine, lx, cols, out_ref, slope, sp, su):
     step = pl.program_id(0)
-
-    def cat(b0, b1):
-        return jnp.concatenate(
-            [jnp.concatenate([y_ref[b, l] for b in range(b0, b1)], axis=1) for l in range(2)], axis=0)
-    t0 = dot3(*split(cat(0, 2)), eh[...], el[...])
-    t1 = dot3(*split(cat(2, 4)), oh[...], ol[...])
-    d = dot3(*split(cat(4, 8)), dh[...], dl[...])
+    sh, sl = sine[:128, :], sine[128:, :]
+
+    @pl.when(step == 0)
+    def _():
+        for f, dst in ((0, sp), (1, su)):
+            v = jnp.concatenate([y_ref[b, f * ROWS:(f + 1) * ROWS] for b in range(NPX)], axis=1)
+            dst[...] = dot3(sh, sl, *split(v))
+
+        def lanes(lt, c):
+            ln = tile(lt, 128)
+            lam = lx[:, ln]
+            ql, qh = [], []
+            for e, dst in ((0, ql), (1, qh)):
+                rows = [y_ref[lt, 2 * ROWS + e * LEV + k:2 * ROWS + e * LEV + k + 1, :] for k in range(LEV)]
+                for m in range(LEV):
+                    dst.append(jnp.broadcast_to(combine(Q[:, m], rows), (8, 128)))
+
+            def inner(bt, cc):
+                rows = tile(bt)
+                mu, s0, s1 = cols[0, rows, :], cols[1, rows, :], cols[2, rows, :]
+                base = lam + mu
+                low, top = sp[rows, ln], su[rows, ln]
+                ps = []
+                for m in range(LEV):
+                    f = (float(Q[0, m]) * low + float(Q[7, m]) * top) + (s0 * ql[m] + s1 * qh[m])
+                    ps.append(g_ref[m, rows, ln] - f / (base + float(THETA[m])))
+                for k in range(LEV):
+                    v = combine(DQ[k], ps)
+                    slope[k, rows, ln] = v - low if k == 0 else v
+                return cc
+            lax.fori_loop(0, ROWS // 8, inner, 0)
+            return c
+        lax.fori_loop(0, NPX, lanes, 0)
+
+    v = jnp.concatenate([dot3(sh, sl, *split(slope[2 * step + l])) for l in range(2)], axis=0)
+    te, to, td = tab_parts(tab)
+    t0 = dot3(*split(v[:, :256]), te[0], te[1])
+    t1 = dot3(*split(v[:, 256:512]), to[0], to[1])
+    d = dot3(*split(v[:, 512:]), td[0], td[1])
     s = jnp.concatenate([t0 + t1, t0 - t1], axis=1)
-    for half, slope in ((0, s + d), (1, s - d)):
-        cols = slice(half * 512, (half + 1) * 512)
+    for half, res in ((0, s + d), (1, s - d)):
+        cs = slice(half * 512, (half + 1) * 512)
         for l in range(2):
             level = base_ref[0] + 2 * step + l
-            solid = level < roof_ref[:, cols]
-            out_ref[l, :, cols] = jnp.where(solid, 0.0, w_ref[l, :, cols] - slope[l * 128:(l + 1) * 128])
-
-
-def x_inverse(base, y, w, roof):
-    return pl.pallas_call(
-        x_inverse_kernel, grid=(4,),
+            solid = level < roof_ref[:, cs]
+            out_ref[l, :, cs] = jnp.where(solid, 0.0, w_ref[l, :, cs] - res[l * 128:(l + 1) * 128])
+
+
+def block_inverse(base, y, g, w, roof):
+    return pl.pallas_call(
+        block_inverse_kernel, grid=(4,),
         out_shape=jax.ShapeDtypeStruct((LEV, ROWS, N), F32),
-        in_specs=[SM, pl.BlockSpec((NPX, 2, ROWS, 128), lambda g: (0, g, 0, 0)),
-                  pl.BlockSpec((2, ROWS, N), lambda g: (g, 0, 0)),
-                  pl.BlockSpec((ROWS, N), lambda g: (0, 0))] + table_specs(),
+        in_specs=[SM, fixed((NPX, BLK, 128)), fixed((LEV, ROWS, N)),
+                  pl.BlockSpec((2, ROWS, N), lambda g: (g, 0, 0)), fixed((ROWS, N)),
+                  fixed((1536, 512)), fixed((256, 128)), fixed((8, N)), fixed((3, ROWS, 128))],
         out_specs=pl.BlockSpec((2, ROWS, N), lambda g: (g, 0, 0)),
-        compiler_params=params(40), name="x_inverse",
-    )(base, y, w, roof, *tables(True))
+        scratch_shapes=[pltpu.VMEM((LEV, ROWS, N), F32), pltpu.VMEM((ROWS, N), F32), pltpu.VMEM((ROWS, N), F32)],
+        compiler_params=params(48), name="block_inverse",
+    )(base, y, g, w, roof, jnp.asarray(TAB_T), jnp.asarray(SINE2), jnp.asarray(LAM_X), jnp.asarray(COLS))
 
 
 def swap(x, axes):
@@ -431,12 +529,13 @@
     lam = eig[:, None] + eig_x[None, :]
     lam_mine = eig_y[:, None] + eig_x[None, :]
 
-    xs = swap(x_forward(horiz_div, w_corr, halo), "px")
-    r, al = y_forward(xs, lam)
+    sent, g = block_forward(horiz_div, w_corr, halo)
+    xs = swap(sent, "px")
+    s, al = y_forward(xs, lam)
     pu = swap(ladder(swap(al, "py"), lam_mine), "py")
-    ys = swap(y_inverse(r, pu, lam), "px")
+    ys = swap(y_inverse(s, pu, lam, xs), "px")
     base = (iy * LEV).astype(jnp.int32).reshape(1)
-    w_new = x_inverse(base, ys, w_corr, roof_level)
+    w_new = block_inverse(base, ys, g, w_corr, roof_level)
     return w_new, theta.reshape(LEV, ROWS, N), temp_new
 
 

time: 293 us -> 234 us (0.80)
  waiting for transfers between devices: 124 us -> 55.2 us
  Pallas kernels: 70.6 us -> 87.8 us
  local copies, waits for them, and re-layouts: 28 us -> 19.7 us
    all_to_all x5, waiting for transfers between devices: 111 us -> 42 us  [swap(): return lax.all_to_all(x, axes, split_axis=0, concat_axis=0, tiled=True)]
    pallas_call x4, Pallas kernels: 28.1 us -> 43.6 us  [the longest x1 17.4 us: block_forward(): pl.pallas_call(block_forward_kernel, grid=(4,), out_shape=(jax.ShapeDtype...]
    unnamed x78 -> x46, local copies, waits for them, and re-layouts: 26.3 us -> 17.2 us
  transfers between devices with their start and end apart: 6 -> 6, of which waited for: 4 -> 4; matrix products, arithmetic and copies ran while one was open for 1% -> 3% of each run, Pallas kernels for 7% -> 7%
where the time goes in v2:
time: 234 us; the launch traced here: 233 us
  Pallas kernels  87.8 us (38%)
  waiting for transfers between devices  55.2 us (24%)
  starting transfers between devices  41.6 us (18%)
  local copies, waits for them, and re-layouts  19.7 us (8%)
  blocking collectives  17.7 us (8%)
  other arithmetic  10.2 us (4%)
    all_to_all x5, waiting for transfers between devices, swap(): return lax.all_to_all(x, axes, split_axis=0, concat_axis=0, tiled=True)  42 us
    all_to_all x5, starting transfers between devices, swap(): return lax.all_to_all(x, axes, split_axis=0, concat_axis=0, tiled=True)  40.3 us
    pallas_call x1, Pallas kernels, scatter_fluxes(): pl.pallas_call(scatter_kernel, out_shape=(jax.ShapeDtypeStruct((1024, 102...  32 us
    all_to_all x1, blocking collectives, swap(): return lax.all_to_all(x, axes, split_axis=0, concat_axis=0, tiled=True)  17.7 us
    pallas_call x1, Pallas kernels, block_forward(): pl.pallas_call(block_forward_kernel, grid=(4,), out_shape=(jax.ShapeDtype...  17.4 us
    unnamed x46, local copies, waits for them, and re-layouts  17.2 us
    pallas_call x1, Pallas kernels, block_inverse(): pl.pallas_call(block_inverse_kernel, grid=(4,), out_shape=jax.ShapeDtypeS...  14.5 us
    ppermute x1, waiting for transfers between devices, body(): halo = lax.ppermute(w_corr[:1], 'py', [(j, j - 1) for j in range(1, NPY)])  13.2 us
  transfers between devices with their start and end apart: 6, of which 4 were waited for; matrix products, arithmetic and copies ran while one was open for 3% of the time, Pallas kernels for 7%

profile of v2, /device:TPU:1, one launch (start us, length us, event | category | flops | bytes accessed | tf_op | source)
XLA Modules:
  0.0 233.1 jit_solution(6271319770231716498)
XLA Ops:
  1.1 1.4 reduce.17
  2.5 1.4 reduce.16
  3.9 1.4 reduce.18
  6.3 11.5 %all-to-all-start = ((f32[128,1,128]{2,1,0:T(1,128)}), f32[128,1,128]{2,1,0:T(1,128)S(1)}, u32[]{:S(2)}, u32[]{:S(2)}) async-start(f32[128,1,128]{2,1,0:T(1,128)} %bitcast.4), calls=%async_computation | async-start | bytes 131072 | tf_op jit(solution)/shard_map/all_to_all | solution.py:503
  18.3 1.4 fusion
  19.9 2.2 copy-done
  22.1 1.6 copy-done.1
  23.7 10.5 %facet_gather.1 = (f32[128,32]{1,0:T(8,128)S(1)}, f32[128,32]{1,0:T(8,128)S(1)}) custom-call(s32[4096]{0:T(1024)S(1)} %bitcast.18, s32[128,32]{1,0:T(8,128)S(1)} %reshape.66.ids_ref, f32[1024,1024]{1,0:T(8,128)S(1)} %bitcast.14, bf16[1024,1024]{1,0:T(8,128)(2,1)S(1)} %bitcast.15), custom_call_target="tpu_custom_call" | custom-call | tf_op jit(solution)/shard_map/facet_gather/pallas_call | solution.py:115
  34.3 32.0 %facet_scatter.1 = (f32[1024,1024]{1,0:T(8,128)}, bf16[1024,1024]{1,0:T(8,128)(2,1)}, f32[128,32]{1,0:T(8,128)S(1)}) custom-call(s32[4096]{0:T(1024)S(1)} %bitcast.19, s32[128,32]{1,0:T(8,128)S(1)} %reshape.66.ids_ref, f32[128,32]{1,0:T(8,128)S(1)} %get-tuple-element.12.wc_ref, f32[128,32]{1,0:T(8,128)S(1)} %get-tuple-element.13.tc_ref, ...), custom_call_target="tpu_custom_call" | custom-call | tf_op jit(solution)/shard_map/facet_scatter/pallas_call | solution.py:165
  66.9 1.1 slice_bitcast_fusion
  68.0 1.3 collective-permute-start
  69.3 13.2 %collective-permute-done.halo_ref = f32[1,128,1024]{2,1,0:T(8,128)S(1)} collective-permute-done((f32[1,128,1024]{2,1,0:T(8,128)S(1)}, f32[1,128,1024]{2,1,0:T(8,128)S(1)}, u32[]{:S(2)}, u32[]{:S(2)}) %collective-permute-start) | collective-permute-done | bytes 524320 | tf_op jit(solution)/shard_map/ppermute | solution.py:524
  82.5 17.4 %block_forward.1 = (f32[8,272,128]{2,1,0:T(8,128)S(1)}, f32[8,128,1024]{2,1,0:T(8,128)}) custom-call(f32[8,128,1024]{2,1,0:T(8,128)} %h_ref.1, f32[8,128,1024]{2,1,0:T(8,128)} %bitcast.21, f32[8,128,1024]{2,1,0:T(8,128)} %bitcast.22, f32[1,128,1024]{2,1,0:T(8,128)S(1)} %collective-permute-done.halo_ref, bf16[1536,512]{1,0:T(8,128)(2,1)S(1)} %copy-done.4, ...), custom_call_target="tpu_custom_call" | custom-call | tf_op jit(solution)/shard_map/block_forward/pallas_call | solution.py:283
  100.8 6.1 %all-to-all-start.1 = ((f32[8,272,128]{2,1,0:T(8,128)}), f32[8,272,128]{2,1,0:T(8,128)S(1)}, u32[]{:S(2)}, u32[]{:S(2)}) async-start(f32[8,272,128]{2,1,0:T(8,128)} %copy-done.10), calls=%async_computation.1 | async-start | bytes 2228224 | tf_op jit(solution)/shard_map/all_to_all | solution.py:503
  107.2 15.5 %all-to-all-done.1.x_ref = f32[8,272,128]{2,1,0:T(8,128)S(1)} async-done(((f32[8,272,128]{2,1,0:T(8,128)}), f32[8,272,128]{2,1,0:T(8,128)S(1)}, u32[]{:S(2)}, u32[]{:S(2)}) %all-to-all-start.1) | async-done | bytes 1114144 | tf_op jit(solution)/shard_map/all_to_all | solution.py:503
  122.7 1.0 copy-done.14
  123.8 5.2 %y_forward.1 = (f32[1024,1024]{1,0:T(8,128)S(1)}, f32[16,2,64,128]{3,2,1,0:T(8,128)S(1)}) custom-call(f32[8,272,128]{2,1,0:T(8,128)S(1)} %all-to-all-done.1.x_ref, f32[1024,128]{1,0:T(8,128)S(1)} %broadcast_add_fusion.lam_ref, bf16[1536,512]{1,0:T(8,128)(2,1)S(1)} %copy-done.3, bf16[2048,16]{1,0:T(8,128)(2,1)S(1)} %copy-done.14), custom_call_target="tpu_custom_call" | custom-call | tf_op jit(solution)/shard_map/y_forward/pallas_call | solution.py:347
  128.9 2.0 copy-done.7
  131.9 9.1 %all-to-all-start.2 = ((f32[16,2,64,128]{3,2,1,0:T(8,128)}), f32[16,2,64,128]{3,2,1,0:T(8,128)}, u32[]{:S(2)}, u32[]{:S(2)}) async-start(f32[16,2,64,128]{3,2,1,0:T(8,128)} %copy-done.11), calls=%async_computation.2 | async-start | bytes 2097152 | tf_op jit(solution)/shard_map/all_to_all | solution.py:503
  141.2 15.2 %all-to-all-done.2.al_ref = f32[16,2,64,128]{3,2,1,0:T(8,128)} async-done(((f32[16,2,64,128]{3,2,1,0:T(8,128)}), f32[16,2,64,128]{3,2,1,0:T(8,128)}, u32[]{:S(2)}, u32[]{:S(2)}) %all-to-all-start.2) | async-done | bytes 1048608 | tf_op jit(solution)/shard_map/all_to_all | solution.py:503
  156.5 1.7 ladder.1
  158.2 17.7 %all_to_all.30.pu_ref = f32[16,2,64,128]{3,2,1,0:T(8,128)} all-to-all(f32[16,2,64,128]{3,2,1,0:T(8,128)S(1)} %ladder.1), channel_id=1, replica_groups=mesh['px'=8,'py'=16] {'py'}, dimensions={0} | all-to-all | bytes 2097152 | tf_op jit(solution)/shard_map/all_to_all | solution.py:503
  175.9 8.5 %all-to-all-start.5 = ((f32[128,1,32]{2,1,0:T(1,128)}), f32[128,1,32]{2,1,0:T(1,128)}, u32[]{:S(2)}, u32[]{:S(2)}) async-start(f32[128,1,32]{2,1,0:T(1,128)} %bitcast.20), calls=%async_computation.5 | async-start | bytes 131072 | tf_op jit(solution)/shard_map/all_to_all | solution.py:503
  184.5 1.4 copy-done.5
  185.9 2.2 copy-done.8
  188.0 1.2 copy-done.9
  190.1 6.6 %y_inverse.1 = f32[8,272,128]{2,1,0:T(8,128)S(1)} custom-call(f32[1024,1024]{1,0:T(8,128)S(1)} %copy-done.8, f32[16,2,64,128]{3,2,1,0:T(8,128)S(1)} %copy-done.9, f32[1024,128]{1,0:T(8,128)S(1)} %broadcast_add_fusion.lam_ref, f32[8,272,128]{2,1,0:T(8,128)S(1)} %all-to-all-done.1.x_ref, bf16[1536,512]{1,0:T(8,128)(2,1)S(1)} %copy-done.5, ...), custom_call_target="tpu_custom_call" | custom-call | tf_op jit(solution)/shard_map/y_inverse/pallas_call | solution.py:431
  197.7 5.1 %all-to-all-start.4 = ((f32[8,272,128]{2,1,0:T(8,128)}), f32[8,272,128]{2,1,0:T(8,128)S(1)}, u32[]{:S(2)}, u32[]{:S(2)}) async-start(f32[8,272,128]{2,1,0:T(8,128)} %copy-done.6), calls=%async_computation.4 | async-start | bytes 2228224 | tf_op jit(solution)/shard_map/all_to_all | solution.py:503
  202.8 2.2 reduce.19
  206.0 1.4 divide_add_fusion
  207.3 11.3 %all-to-all-done.4.y_ref = f32[8,272,128]{2,1,0:T(8,128)S(1)} async-done(((f32[8,272,128]{2,1,0:T(8,128)}), f32[8,272,128]{2,1,0:T(8,128)S(1)}, u32[]{:S(2)}, u32[]{:S(2)}) %all-to-all-start.4) | async-done | bytes 1114144 | tf_op jit(solution)/shard_map/all_to_all | solution.py:503
  218.6 14.5 %block_inverse.1 = f32[8,128,1024]{2,1,0:T(8,128)} custom-call(s32[1]{0:T(128)} %bitcast.base_ref, f32[8,272,128]{2,1,0:T(8,128)S(1)} %all-to-all-done.4.y_ref, f32[8,128,1024]{2,1,0:T(8,128)} %get-tuple-element.18.g_ref, f32[8,128,1024]{2,1,0:T(8,128)} %bitcast.23, s32[128,1024]{1,0:T(8,128)S(1)} %copy-done.13, bf16[1536,512]{1,0:T(8,128)(2,1)S(1)} %copy-done.3, ...), custom_call_target="tpu_custom_call" | custom-call | tf_op jit(solution)/shard_map/block_inverse/pallas_call | solution.py:490
  (53 shorter events, 8.0 us)
Async XLA Ops:
  6.3 27.9 %all-to-all-start = ((f32[128,1,128]{2,1,0:T(1,128)}), f32[128,1,128]{2,1,0:T(1,128)S(1)}, u32[]{:S(2)}, u32[]{:S(2)}) async-start(f32[128,1,128]{2,1,0:T(1,128)} %bitcast.4), calls=%async_computation | async-start | bytes 131072 | tf_op jit(solution)/shard_map/all_to_all | solution.py:503
  19.9 2.2 copy-start
  22.1 1.6 copy-start.1
  23.7 10.5 %copy-start.2 = (bf16[8,128,1024]{2,1,0:T(8,128)(2,1)S(1)}, bf16[8,128,1024]{2,1,0:T(8,128)(2,1)}, u32[]{:S(2)}) copy-start(bf16[8,128,1024]{2,1,0:T(8,128)(2,1)} %param.20) | copy-start | bytes 6291460
  34.2 48.2 %copy-start.4 = (bf16[1536,512]{1,0:T(8,128)(2,1)S(1)}, bf16[1536,512]{1,0:T(8,128)(2,1)}, u32[]{:S(2)}) copy-start(bf16[1536,512]{1,0:T(8,128)(2,1)} %constant.49.clone.tab) | copy-start | bytes 4718596
  34.2 48.2 %copy-start.12 = (f32[3,128,128]{2,1,0:T(8,128)S(1)}, f32[3,128,128]{2,1,0:T(8,128)}, u32[]{:S(2)}) copy-start(f32[3,128,128]{2,1,0:T(8,128)} %constant.52.clone.cols) | copy-start | bytes 589828
  34.2 48.2 %copy-start.15 = (bf16[256,128]{1,0:T(8,128)(2,1)S(1)}, bf16[256,128]{1,0:T(8,128)(2,1)}, u32[]{:S(2)}) copy-start(bf16[256,128]{1,0:T(8,128)(2,1)} %constant.50.clone.sine) | copy-start | bytes 196612
  34.2 48.2 %copy-start.16 = (f32[8,1024]{1,0:T(8,128)S(1)}, f32[8,1024]{1,0:T(8,128)}, u32[]{:S(2)}) copy-start(f32[8,1024]{1,0:T(8,128)} %constant.51.clone.lx) | copy-start | bytes 98308
  66.3 0.6 copy-start.18
  68.0 14.5 %collective-permute-start = (f32[1,128,1024]{2,1,0:T(8,128)S(1)}, f32[1,128,1024]{2,1,0:T(8,128)S(1)}, u32[]{:S(2)}, u32[]{:S(2)}) collective-permute-start(f32[1,128,1024]{2,1,0:T(8,128)S(1)} %slice_bitcast_fusion), channel_id=1, source_target_pairs={{1,0},{2,1},{3,2},{4,3},{5,4},{6,5},{7,6},{8,7},{9,8},{10,9},{11,1... | collective-permute-start | bytes 1572872 | tf_op jit(solution)/shard_map/ppermute | solution.py:524
  99.8 1.0 copy-start.10
  100.8 6.1 %copy-start.21 = (f32[1024]{0:T(1024)S(1)}, f32[1024]{0:T(1024)}, u32[]{:S(2)}) copy-start(f32[1024]{0:T(1024)} %constant.48.clone) | copy-start | bytes 12292
  100.8 21.9 %copy-start.3 = (bf16[1536,512]{1,0:T(8,128)(2,1)S(1)}, bf16[1536,512]{1,0:T(8,128)(2,1)}, u32[]{:S(2)}) copy-start(bf16[1536,512]{1,0:T(8,128)(2,1)} %constant.53.clone.tab) | copy-start | bytes 4718596
  100.8 21.9 %all-to-all-start.1 = ((f32[8,272,128]{2,1,0:T(8,128)}), f32[8,272,128]{2,1,0:T(8,128)S(1)}, u32[]{:S(2)}, u32[]{:S(2)}) async-start(f32[8,272,128]{2,1,0:T(8,128)} %copy-done.10), calls=%async_computation.1 | async-start | bytes 2228224 | tf_op jit(solution)/shard_map/all_to_all | solution.py:503
  122.7 1.0 copy-start.14
  128.9 2.0 copy-start.7
  130.9 1.0 copy-start.11
  131.9 24.5 %all-to-all-start.2 = ((f32[16,2,64,128]{3,2,1,0:T(8,128)}), f32[16,2,64,128]{3,2,1,0:T(8,128)}, u32[]{:S(2)}, u32[]{:S(2)}) async-start(f32[16,2,64,128]{3,2,1,0:T(8,128)} %copy-done.11), calls=%async_computation.2 | async-start | bytes 2097152 | tf_op jit(solution)/shard_map/all_to_all | solution.py:503
  175.9 21.8 %all-to-all-start.5 = ((f32[128,1,32]{2,1,0:T(1,128)}), f32[128,1,32]{2,1,0:T(1,128)}, u32[]{:S(2)}, u32[]{:S(2)}) async-start(f32[128,1,32]{2,1,0:T(1,128)} %bitcast.20), calls=%async_computation.5 | async-start | bytes 131072 | tf_op jit(solution)/shard_map/all_to_all | solution.py:503
  184.4 1.4 copy-start.5
  185.9 2.2 copy-start.8
  188.0 1.2 copy-start.9
  189.3 0.8 copy-start.17
  196.7 1.0 copy-start.6
  197.7 8.2 %copy-start.19 = (f32[1,4096]{1,0:T(1,128)S(1)}, f32[1,4096]{1,0:T(1,128)}, u32[]{:S(2)}) copy-start(f32[1,4096]{1,0:T(1,128)} %param.23) | copy-start | bytes 49156
  197.7 8.2 %copy-start.20 = (f32[1,4096]{1,0:T(1,128)S(1)}, f32[1,4096]{1,0:T(1,128)}, u32[]{:S(2)}) copy-start(f32[1,4096]{1,0:T(1,128)} %param.25) | copy-start | bytes 49156
  197.7 20.9 %copy-start.13 = (s32[128,1024]{1,0:T(8,128)S(1)}, s32[128,1024]{1,0:T(8,128)}, u32[]{:S(2)}) copy-start(s32[128,1024]{1,0:T(8,128)} %roof_ref.1) | copy-start | bytes 1572868
  197.7 20.9 %all-to-all-start.4 = ((f32[8,272,128]{2,1,0:T(8,128)}), f32[8,272,128]{2,1,0:T(8,128)S(1)}, u32[]{:S(2)}, u32[]{:S(2)}) async-start(f32[8,272,128]{2,1,0:T(8,128)} %copy-done.6), calls=%async_computation.4 | async-start | bytes 2228224 | tf_op jit(solution)/shard_map/all_to_all | solution.py:503

commit v3 on v2

v3 whole, which is shorter than its diff:
```python
import functools
import math

import jax
import jax.numpy as jnp
import numpy as np
from jax import lax
from jax.experimental import pallas as pl
from jax.experimental.pallas import tpu as pltpu
from jax.sharding import PartitionSpec as P

N = 1024
NPX, NPY = 8, 16
LEV, ROWS = 8, 128
OWNERS, SLOT = 128, 32
MIB = 1 << 20
F32, BF16 = jnp.float32, jnp.bfloat16


def mode_table():
    classes = [np.arange(0, 513, 4), np.arange(2, 513, 4), np.arange(1, 512, 2)]
    n = np.arange(N)
    cols, waves = [], []
    for ks in classes:
        for k in ks:
            edge = k == 0 or k == N // 2
            norm = math.sqrt((1.0 if edge else 2.0) / N)
            cols.append(norm * np.cos(2 * np.pi * ((n * k) % N) / N))
            waves.append(k)
        for k in ks:
            if k == 0 or k == N // 2:
                continue
            cols.append(math.sqrt(2.0 / N) * np.sin(2 * np.pi * ((n * k) % N) / N))
            waves.append(k)
    table = np.stack(cols, axis=1)
    eigen = -4.0 * np.sin(np.pi * np.array(waves) / N) ** 2
    return table, eigen


def split_np(a):
    a = a.astype(np.float32)
    hi = a.astype(jnp.bfloat16)
    lo = (a - hi.astype(np.float32)).astype(jnp.bfloat16)
    return hi, lo


TABLE, EIGEN = mode_table()
T_EE = TABLE[:256, :256]
T_EO = TABLE[:256, 256:512]
T_OD = TABLE[:512, 512:]


def split(v):
    hi = v.astype(BF16)
    return hi, (v - hi.astype(F32)).astype(BF16)


def dot3(ah, al, bh, bl):
    d = functools.partial(jnp.dot, preferred_element_type=F32)
    return d(ah, bh) + (d(al, bh) + d(ah, bl))


def params(mb, sem=None):
    return pltpu.CompilerParams(vmem_limit_bytes=mb * MIB)


VM = pl.BlockSpec(memory_space=pltpu.VMEM)
SM = pl.BlockSpec(memory_space=pltpu.SMEM)


def pack_kernel(ft, dr, he, ce, od, ids, addr):
    zero = jnp.zeros((32, 32), F32)
    none = jnp.zeros((32, 96), jnp.int32)
    for q in range(4):
        c = slice(q * 32, (q + 1) * 32)
        od[pl.ds(q, 32, stride=4), :] = jnp.concatenate([ft[:, c], dr[:, c], he[:, c], zero], axis=1)
        ids[pl.ds(q, 32, stride=4), :] = jnp.concatenate([ce[:, c], none], axis=1)
    safe = jnp.maximum(ce[...], 0)
    row = safe >> 10
    addr[...] = (row >> 3) * 64 + ((safe >> 7) & 7) * 8 + (row & 7)


def pack_owner(ft, dr, he, ce):
    full = jax.ShapeDtypeStruct((OWNERS, 128), F32)
    return pl.pallas_call(
        pack_kernel, out_shape=(full, jax.ShapeDtypeStruct((OWNERS, 128), jnp.int32),
                                jax.ShapeDtypeStruct((32, 128), jnp.int32)),
        in_specs=[VM] * 4, out_specs=(VM,) * 3, compiler_params=params(16), name="pack_owner",
    )(ft, dr, he, ce)


def load_w(w_ref, wt):
    def one(tr, c):
        for ct in range(8):
            wt[tile(tr * 8 + ct), :] = w_ref[tile(tr), ct * 128:(ct + 1) * 128]
        return c
    lax.fori_loop(0, 128, one, 0)


def load_temp(a_ref, tt):
    def one(i, c):
        for ct in range(8):
            v = a_ref[tile(i, 16), ct * 128:(ct + 1) * 128].astype(F32)
            tt[tile(i * 16 + ct), :] = v[:8]
            tt[tile(i * 16 + 8 + ct), :] = v[8:]
        return c
    lax.fori_loop(0, 64, one, 0)


def gather_rows(addr, src, buf):
    def one(o, c):
        for s in range(SLOT):
            buf[pl.ds(s * OWNERS + o, 1), :] = src[pl.ds(addr[o * SLOT + s], 1), :]
        return c
    lax.fori_loop(0, OWNERS, one, 0)


def hits(ids, s, lane):
    col = ids[:, s:s + 1]
    return lane == jnp.where(col >= 0, col & 127, -1)


def pick(ids, buf):
    lane = lax.broadcasted_iota(jnp.int32, (OWNERS, 128), 1)
    out = jnp.zeros((OWNERS, 128), F32)
    for s in range(SLOT):
        v = jnp.where(hits(ids, s, lane), buf[s * OWNERS:(s + 1) * OWNERS, :], 0.0)
        out = jnp.where(lane == s, jnp.sum(v, axis=1, keepdims=True), out)
    return out


def spread_rows(ids, vals, buf):
    lane = lax.broadcasted_iota(jnp.int32, (OWNERS, 128), 1)
    for s in range(SLOT):
        buf[s * OWNERS:(s + 1) * OWNERS, :] = jnp.where(hits(ids, s, lane), vals[:, s:s + 1], 0.0)


def clear(accs):
    def one(i, c):
        for a in accs:
            for j in range(8):
                a[tile(i * 8 + j), :] = jnp.zeros((8, 128), F32)
        return c
    lax.fori_loop(0, 128, one, 0)


def add_rows(addr, accs, buf):
    width = len(accs)

    def one(o, c):
        for s in range(0, SLOT, width):
            at = [addr[o * SLOT + s + j] for j in range(width)]
            new = [accs[j][pl.ds(at[j], 1), :] + buf[pl.ds((s + j) * OWNERS + o, 1), :] for j in range(width)]
            for j in range(width):
                accs[j][pl.ds(at[j], 1), :] = new[j]
        return c
    lax.fori_loop(0, OWNERS, one, 0)


def total(accs, rows):
    return (accs[0][rows, :] + accs[1][rows, :]) + (accs[2][rows, :] + accs[3][rows, :])


def gather_kernel(addr, ids_ref, w_ref, wc_ref, wt, buf):
    load_w(w_ref, wt)
    gather_rows(addr, wt, buf)
    wc_ref[...] = pick(ids_ref[...], buf)


def gather_w(addr, ids, w2):
    return pl.pallas_call(
        gather_kernel, out_shape=jax.ShapeDtypeStruct((OWNERS, 128), F32), in_specs=[SM, VM, VM], out_specs=VM,
        scratch_shapes=[pltpu.VMEM((8192, 128), F32), pltpu.VMEM((4096, 128), F32)],
        compiler_params=params(32), name="facet_gather",
    )(addr, ids, w2)


def scatter_w_kernel(addr, ids_ref, wc_ref, od_ref, w_ref, wo_ref, acc0, acc1, acc2, acc3, buf):
    accs = (acc0, acc1, acc2, acc3)
    load_w(w_ref, acc0)
    clear(accs[1:])
    wc = wc_ref[:, :SLOT]
    stress = od_ref[:, 32:64] * jnp.sqrt(wc * wc + 0.25) * wc
    spread_rows(ids_ref[...], -stress, buf)
    add_rows(addr, accs, buf)

    def put(tr, c):
        for ct in range(8):
            wo_ref[tile(tr), ct * 128:(ct + 1) * 128] = total(accs, tile(tr * 8 + ct))
        return c
    lax.fori_loop(0, 128, put, 0)


FOUR = [pltpu.VMEM((8192, 128), F32)] * 4 + [pltpu.VMEM((4096, 128), F32)]


def scatter_w(addr, ids, wc, od, w2):
    return pl.pallas_call(
        scatter_w_kernel, out_shape=jax.ShapeDtypeStruct((1024, 1024), F32),
        in_specs=[SM, VM, VM, VM, VM], out_specs=VM, scratch_shapes=FOUR,
        compiler_params=params(40), name="scatter_w",
    )(addr, ids, wc, od, w2)


def heat_kernel(addr, shift, after, ids_ref, wc_ref, od_ref, a_ref, th_ref, fl_ref, acc0, acc1, acc2, acc3, buf, turned):
    accs = (acc0, acc1, acc2, acc3)
    load_temp(a_ref, acc0)
    gather_rows(addr, acc0, buf)
    ids = ids_ref[...]
    tc = pick(ids, buf)[:, :SLOT]
    clear(accs[1:])
    wc = wc_ref[:, :SLOT]
    flux = od_ref[:, 64:96] * jnp.sqrt(wc * wc + 0.25) * (od_ref[:, :32] - tc)
    spread_rows(ids, flux, buf)
    wide = jnp.concatenate([flux, jnp.zeros((OWNERS, 96), F32)], axis=1)
    turned[...] = pltpu.roll(wide, shift[0], 1)
    for j in range(NPY):
        fl_ref[j] = turned[pl.ds(j, 8, stride=16), :]
    add_rows(addr, accs, buf)

    def put(i, c):
        for ct in range(8):
            v0 = total(accs, tile(i * 16 + ct))
            v1 = total(accs, tile(i * 16 + 8 + ct))
            th_ref[tile(i, 16), ct * 128:(ct + 1) * 128] = jnp.concatenate([v0, v1], axis=0).astype(BF16)
        return c
    lax.fori_loop(0, 64, put, 0)


def heat_cells(addr, shift, after, ids, wc, od, a2):
    return pl.pallas_call(
        heat_kernel,
        out_shape=(jax.ShapeDtypeStruct((1024, 1024), BF16), jax.ShapeDtypeStruct((NPY, 8, 128), F32)),
        in_specs=[SM, SM, pl.BlockSpec(memory_space=pl.ANY), VM, VM, VM, VM], out_specs=(VM, VM),
        scratch_shapes=FOUR + [pltpu.VMEM((OWNERS, 128), F32)],
        cost_estimate=pl.CostEstimate(flops=0, bytes_accessed=60 * MIB, transcendentals=0),
        compiler_params=params(40), name="heat_cells",
    )(addr, shift, after, ids, wc, od, a2)


BLK = 2 * ROWS + 2 * LEV
BACK = BLK + 8


def z_basis():
    k, m = np.arange(LEV)[:, None], np.arange(LEV)[None, :]
    q = math.sqrt(4 / 17) * np.sin(np.pi * (2 * m + 1) * (k + 1) / 17)
    theta = -4.0 * np.sin(np.pi * (2 * np.arange(LEV) + 1) / 34) ** 2
    return q, theta


def y_basis():
    i = np.arange(ROWS) + 1
    s = math.sqrt(2 / 129) * np.sin(np.pi * (np.outer(i, i) % 258) / 129)
    mu = -4.0 * np.sin(np.pi * i / 258) ** 2
    return s, mu


Q, THETA = z_basis()
DQ = Q - np.concatenate([np.zeros((1, LEV)), Q[:-1]])
SINE, MU = y_basis()
EDGE = np.concatenate([TABLE[0::ROWS], TABLE[ROWS - 1::ROWS]])


def pack(transposed):
    parts = [split_np(t.T if transposed else t) for t in (T_EE, T_EO, T_OD)]
    (eh, el), (oh, ol), (dh, dl) = parts
    return np.concatenate([dh, dl, np.concatenate([np.concatenate([eh, oh], 1), np.concatenate([el, ol], 1)])])


TAB, TAB_T = pack(False), pack(True)
SINE2 = np.concatenate(split_np(SINE))
EDGE_F = np.concatenate(split_np(EDGE.T))
EDGE_B = np.concatenate(split_np(EDGE))
LAM_X = np.broadcast_to(EIGEN.astype(np.float32), (8, N)).copy()
COLS = np.stack([np.broadcast_to(v[:, None], (ROWS, 128)) for v in (MU, SINE[:, 0], SINE[:, 127])]).astype(np.float32)


def tab_parts(t):
    return ((t[1024:1280, :256], t[1280:1536, :256]), (t[1024:1280, 256:], t[1280:1536, 256:]),
            (t[:512], t[512:1024]))


def combine(coefs, vs):
    out = None
    for c, v in zip(coefs, vs):
        t = float(c) * v
        out = t if out is None else out + t
    return out


def tile(i, size=8):
    return pl.ds(pl.multiple_of(i * size, size), size)


def fixed(shape):
    return pl.BlockSpec(shape, lambda g: (0,) * len(shape))


def slab_polys(lam):
    phi = [None] * 9
    phi[8] = jnp.ones_like(lam)
    delta = -lam
    phi[7] = phi[8] + delta
    for k in range(6, -1, -1):
        delta = delta - lam * phi[k + 1]
        phi[k] = phi[k + 1] + delta
    theta = [jnp.ones_like(lam), 2.0 - lam]
    for k in range(2, 8):
        theta.append((2.0 - lam) * theta[k - 1] - theta[k - 2])
    return phi, theta, delta


def inverse_of(v):
    r = pl.reciprocal(v, approx=True)
    r = r * (2.0 - v * r)
    return r * (2.0 - v * r)


def x_modes(v, tab):
    s, d = v[:, :512] + v[:, 512:], v[:, :512] - v[:, 512:]
    te, to, td = tab_parts(tab)
    return ((0, dot3(*split(s[:, :256] + s[:, 256:]), *te)), (256, dot3(*split(s[:, :256] - s[:, 256:]), *to)),
            (512, dot3(*split(d), *td)))


def block_modes_kernel(h_ref, w_ref, wn_ref, tab, sine, out_ref):
    up = jnp.where(pl.program_id(0) == 3, 0.0, wn_ref[0])
    r = jnp.concatenate([h_ref[0] + w_ref[1] - w_ref[0], h_ref[1] + up - w_ref[1]], axis=0)
    for c0, res in x_modes(r, tab):
        for l in range(2):
            out_ref[l, :, c0:c0 + res.shape[1]] = dot3(
                sine[:128, :], sine[128:, :], *split(res[l * 128:(l + 1) * 128]))


def block_modes(h, w):
    two = pl.BlockSpec((2, ROWS, N), lambda g: (g, 0, 0))
    return pl.pallas_call(
        block_modes_kernel, grid=(4,), out_shape=jax.ShapeDtypeStruct((LEV, ROWS, N), F32),
        in_specs=[two, two, pl.BlockSpec((1, ROWS, N), lambda g: (jnp.minimum(2 * g + 2, 7), 0, 0)),
                  fixed((1536, 512)), fixed((256, 128))],
        out_specs=two, compiler_params=params(32), name="block_modes",
        cost_estimate=pl.CostEstimate(flops=0, bytes_accessed=25 * MIB, transcendentals=0),
    )(h, w, w, jnp.asarray(TAB), jnp.asarray(SINE2))


def block_solve_kernel(r_ref, halo_ref, tab, sine, lx, cols, out_ref, g_ref, hx, a07):
    lt = pl.program_id(0)
    sh, sl = sine[:128, :], sine[128:, :]

    @pl.when(lt == 0)
    def _():
        for c0, res in x_modes(halo_ref[...], tab):
            res = dot3(sh, sl, *split(res))
            for b in range(res.shape[1] // 128):
                hx[c0 // 128 + b] = res[:, b * 128:(b + 1) * 128]
    lam = lx[...]

    def inner(bt, acc):
        rows = tile(bt)
        rs = [r_ref[k, rows, :] for k in range(LEV)]
        rs[7] = rs[7] + hx[lt, rows, :]
        mu, s0, s1 = cols[0, rows, :], cols[1, rows, :], cols[2, rows, :]
        base = lam + mu
        ps = []
        for m in range(LEV):
            p = combine(Q[:, m], rs) * inverse_of(base + float(THETA[m]))
            g_ref[m, rows, :] = p
            ps.append(p)
        a07[rows, :128] = combine(Q[0], ps)
        a07[rows, 128:] = combine(Q[7], ps)
        return tuple(acc[m] + s0 * ps[m] for m in range(LEV)) + tuple(
            acc[LEV + m] + s1 * ps[m] for m in range(LEV))
    acc = lax.fori_loop(0, ROWS // 8, inner, tuple(jnp.zeros((8, 128), F32) for _ in range(16)))
    for e in range(2):
        sums = [jnp.sum(acc[e * LEV + m], axis=0, keepdims=True) for m in range(LEV)]
        out_ref[0, 2 * ROWS + e * LEV:2 * ROWS + (e + 1) * LEV, :] = jnp.concatenate(
            [combine(Q[k], sums) for k in range(LEV)], axis=0)
    res = dot3(sh, sl, *split(a07[...]))
    out_ref[0, :ROWS, :] = res[:, :128]
    out_ref[0, ROWS:2 * ROWS, :] = res[:, 128:]


def block_solve(r, halo):
    col = pl.BlockSpec((LEV, ROWS, 128), lambda g: (0, 0, g))
    return pl.pallas_call(
        block_solve_kernel, grid=(NPX,),
        out_shape=(jax.ShapeDtypeStruct((NPX, BLK, 128), F32), jax.ShapeDtypeStruct((LEV, ROWS, N), F32)),
        in_specs=[col, fixed((ROWS, N)), fixed((1536, 512)), fixed((256, 128)),
                  pl.BlockSpec((8, 128), lambda g: (0, g)), fixed((3, ROWS, 128))],
        out_specs=(pl.BlockSpec((1, BLK, 128), lambda g: (g, 0, 0)), col),
        scratch_shapes=[pltpu.VMEM((NPX, ROWS, 128), F32), pltpu.VMEM((ROWS, 256), F32)],
        compiler_params=params(32), name="block_solve",
    )(r, halo, jnp.asarray(TAB), jnp.asarray(SINE2), jnp.asarray(LAM_X), jnp.asarray(COLS))


def edge_rows(x_ref, sr):
    for i in range(NPX):
        for k in range(LEV):
            cs = slice(k * 128, (k + 1) * 128)
            sr[i:i + 1, cs] = x_ref[(i + 7) % 8, 2 * ROWS + LEV + k:2 * ROWS + LEV + k + 1, :]
            sr[8 + i:9 + i, cs] = x_ref[(i + 1) % 8, 2 * ROWS + k:2 * ROWS + k + 1, :]
    return split(sr[...])


def edge_modes(edge, t, sh, sl):
    return dot3(edge[tile(t, 128), :], edge[pl.ds(pl.multiple_of(N + t * 128, 128), 128), :], sh, sl)


def y_forward_kernel(x_ref, lam_ref, tab, edge, al_ref, pp, sr, st):
    x = jnp.concatenate([x_ref[:, :ROWS], x_ref[:, ROWS:2 * ROWS]], axis=-1).reshape(N, 256)
    s, d = x[:512] + x[512:], x[:512] - x[512:]
    ee, eo = s[:256] + s[256:], s[:256] - s[256:]
    te, to, td = tab_parts(tab)
    for v, t, k0 in ((ee, te, 0), (eo, to, 256), (d, td, 512)):
        res = dot3(*t, *split(v))
        pp[k0:k0 + res.shape[0], :] = res
    sh, sl = edge_rows(x_ref, sr)

    def some(t, c):
        st[...] = edge_modes(edge, t, sh, sl)
        for q in range(8):
            part = slice(q * 16, (q + 1) * 16)
            rows = pl.ds(pl.multiple_of(t * 128 + q * 16, 16), 16)
            phi, theta, _ = slab_polys(lam_ref[rows, :])
            inv = inverse_of(phi[0])
            b0 = b7 = None
            for k in range(LEV):
                sk = st[part, k * 128:(k + 1) * 128]
                b0 = phi[k + 1] * sk if k == 0 else b0 + phi[k + 1] * sk
                b7 = sk if k == 0 else b7 + theta[k] * sk
            j, at = 2 * t + q // 4, (q % 4) * 16
            al_ref[j, at:at + 16, :] = pp[rows, :128] + b0 * inv
            al_ref[j, 64 + at:80 + at, :] = pp[rows, 128:] + b7 * inv
        return c
    lax.fori_loop(0, 8, some, 0)


def y_forward(x, lam):
    return pl.pallas_call(
        y_forward_kernel, grid=(1,),
        out_shape=jax.ShapeDtypeStruct((NPY, 128, 128), F32),
        in_specs=[fixed((NPX, BLK, 128)), fixed((N, 128)), fixed((1536, 512)), fixed((2 * N, 16))],
        out_specs=fixed((NPY, 128, 128)),
        scratch_shapes=[pltpu.VMEM((N, 256), F32), pltpu.VMEM((16, N), F32), pltpu.VMEM((128, N), F32)],
        compiler_params=params(40), name="y_forward",
    )(x, lam, jnp.asarray(TAB_T), jnp.asarray(EDGE_F))


def ladder_kernel(al_ref, lam_ref, fl_ref, out_ref):
    for j in range(NPY):
        out_ref[j, 128:, :] = fl_ref[j]

    def some(t, c):
        rows, tops = tile(t), pl.ds(pl.multiple_of(64 + t * 8, 8), 8)
        phi, theta, delta = slab_polys(lam_ref[rows, :])
        inv = 1.0 / phi[0]
        n07, n77, cc = inv, theta[7] * inv, delta * inv
        A = [None] * 17
        B = [None] * 17
        e = [None] * 17
        A[16] = jnp.zeros_like(inv)
        B[16] = jnp.full_like(inv, -2.0)
        for j in range(15, -1, -1):
            g, q = al_ref[j, rows, :], al_ref[j, tops, :]
            e[j + 1] = inverse_of(1.0 - n77 * B[j + 1])
            be = B[j + 1] * e[j + 1]
            A[j] = g + n07 * (A[j + 1] + be * (q + n77 * A[j + 1]))
            B[j] = n07 * n07 * be - cc
        p = -A[0] / B[0]
        for j in range(16):
            out_ref[j, rows, :] = p
            p = (al_ref[j, tops, :] + n77 * A[j + 1] + n07 * p) * e[j + 1]
            out_ref[j, tops, :] = A[j + 1] + B[j + 1] * p
        return c
    lax.fori_loop(0, 8, some, 0)


def ladder(al, lam, fl):
    return pl.pallas_call(
        ladder_kernel, grid=(1,), out_shape=jax.ShapeDtypeStruct((NPY, 136, 128), F32),
        in_specs=[fixed((NPY, 128, 128)), fixed((64, 128)), fixed((NPY, 8, 128))],
        out_specs=fixed((NPY, 136, 128)), compiler_params=params(16), name="ladder",
    )(al, lam, fl)


def y_inverse_kernel(x_ref, pu_ref, lam_ref, tab, edge_f, edge_b, out_ref, sr, st, ph, pl_):
    sh, sl = edge_rows(x_ref, sr)

    def some(t, c):
        st[...] = edge_modes(edge_f, t, sh, sl)
        for q in range(8):
            part = slice(q * 16, (q + 1) * 16)
            rows = pl.ds(pl.multiple_of(t * 128 + q * 16, 16), 16)
            j, at = 2 * t + q // 4, (q % 4) * 16
            low, top = pu_ref[j, at:at + 16, :], pu_ref[j, 64 + at:80 + at, :]
            lam = lam_ref[rows, :]
            cs = [None] * 8
            fs = [None] * 8
            cs[7] = inverse_of(1.0 - lam)
            fs[7] = st[part, 7 * 128:] + top
            for k in range(6, -1, -1):
                cs[k] = inverse_of(2.0 - lam - cs[k + 1])
                fs[k] = st[part, k * 128:(k + 1) * 128] + cs[k + 1] * fs[k + 1]
            prev = low
            for k in range(8):
                prev = cs[k] * (fs[k] + prev)
                ph[rows, k * 128:(k + 1) * 128], pl_[rows, k * 128:(k + 1) * 128] = split(prev)
        return c
    lax.fori_loop(0, 8, some, 0)
    edges = dot3(edge_b[:16, :], edge_b[16:, :], ph[...], pl_[...])
    for i in range(NPX):
        below, above = (i + 7) % 8, (i + 1) % 8
        for k in range(LEV):
            cols = slice(k * 128, (k + 1) * 128)
            lo = 2 * ROWS + k
            hi = 2 * ROWS + LEV + k
            out_ref[i, lo:lo + 1, :] = edges[8 + below:9 + below, cols] + x_ref[below, hi:hi + 1, :]
            out_ref[i, hi:hi + 1, :] = edges[above:above + 1, cols] + x_ref[above, lo:lo + 1, :]
    for q in range(4):
        flux = (pu_ref[4 * q, 128:, :] + pu_ref[4 * q + 1, 128:, :]) + (
            pu_ref[4 * q + 2, 128:, :] + pu_ref[4 * q + 3, 128:, :])
        for i in range(NPX):
            out_ref[i, BLK + q:BLK + q + 1, :] = flux[i:i + 1, :]
            out_ref[i, BLK + 4 + q:BLK + 5 + q, :] = jnp.zeros((1, 128), F32)
    pu = jnp.concatenate([pu_ref[:, :64], pu_ref[:, 64:128]], axis=-1).reshape(N, 256)
    te, to, td = tab_parts(tab)
    t0 = dot3(*te, *split(pu[:256]))
    t1 = dot3(*to, *split(pu[256:512]))
    d = dot3(*td, *split(pu[512:]))
    ev = (t0 + t1, t0 - t1)
    for i in range(4):
        base = ev[i // 2][(i % 2) * 128:(i % 2 + 1) * 128]
        odd = d[i * 128:(i + 1) * 128]
        for l in range(2):
            cols = slice(l * 128, (l + 1) * 128)
            out_ref[i, l * ROWS:(l + 1) * ROWS, :] = base[:, cols] + odd[:, cols]
            out_ref[i + 4, l * ROWS:(l + 1) * ROWS, :] = base[:, cols] - odd[:, cols]


def y_inverse(x, pu, lam):
    return pl.pallas_call(
        y_inverse_kernel, grid=(1,), out_shape=jax.ShapeDtypeStruct((NPX, BACK, 128), F32),
        in_specs=[fixed((NPX, BLK, 128)), fixed((NPY, 136, 128)), fixed((N, 128)), fixed((1536, 512)),
                  fixed((2 * N, 16)), fixed((32, N))],
        out_specs=fixed((NPX, BACK, 128)),
        scratch_shapes=[pltpu.VMEM((16, N), F32), pltpu.VMEM((128, N), F32),
                        pltpu.VMEM((N, N), BF16), pltpu.VMEM((N, N), BF16)],
        compiler_params=params(40), name="y_inverse",
    )(x, pu, lam, jnp.asarray(TAB), jnp.asarray(EDGE_F), jnp.asarray(EDGE_B))


def block_inverse_kernel(base_ref, y_ref, g_ref, w_ref, roof_ref, tab, sine, lx, cols, ft, nr, hc,
                         out_ref, nt_ref, field, wv, spu, fb):
    step = pl.program_id(0)
    sh, sl = sine[:128, :], sine[128:, :]

    @pl.when(step < NPX)
    def _():
        fb[step] = y_ref[0, BLK:, :]
        spu[...] = dot3(sh, sl, *split(jnp.concatenate([y_ref[0, :ROWS, :], y_ref[0, ROWS:2 * ROWS, :]], axis=1)))
        lam = lx[...]
        ql, qh = [], []
        for e, dst in ((0, ql), (1, qh)):
            rows = [y_ref[0, 2 * ROWS + e * LEV + k:2 * ROWS + e * LEV + k + 1, :] for k in range(LEV)]
            for m in range(LEV):
                dst.append(jnp.broadcast_to(combine(Q[:, m], rows), (8, 128)))

        def inner(bt, c):
            rows = tile(bt)
            mu, s0, s1 = cols[0, rows, :], cols[1, rows, :], cols[2, rows, :]
            base = lam + mu
            low, top = spu[rows, :128], spu[rows, 128:]
            ps = []
            for m in range(LEV):
                f = (float(Q[0, m]) * low + float(Q[7, m]) * top) + (s0 * ql[m] + s1 * qh[m])
                ps.append(g_ref[m, rows, :] - f * inverse_of(base + float(THETA[m])))
            for k in range(LEV):
                v = combine(DQ[k], ps)
                wv[rows, k * 128:(k + 1) * 128] = v - low if k == 0 else v
            return c
        lax.fori_loop(0, ROWS // 8, inner, 0)
        res = dot3(sh, sl, *split(wv[...]))
        for k in range(LEV):
            field[k, :, tile(step, 128)] = res[:, k * 128:(k + 1) * 128]

    @pl.when(step >= NPX)
    def _():
        pair = step - NPX
        v = jnp.concatenate([field[2 * pair], field[2 * pair + 1]], axis=0)
        te, to, td = tab_parts(tab)
        t0 = dot3(*split(v[:, :256]), *te)
        t1 = dot3(*split(v[:, 256:512]), *to)
        d = dot3(*split(v[:, 512:]), *td)
        s = jnp.concatenate([t0 + t1, t0 - t1], axis=1)
        for half, res in ((0, s + d), (1, s - d)):
            cs = slice(half * 512, (half + 1) * 512)
            for l in range(2):
                solid = base_ref[0] + 2 * pair + l < roof_ref[:, cs]
                out_ref[l, :, cs] = jnp.where(solid, 0.0, w_ref[l, :, cs] - res[l * 128:(l + 1) * 128])

    @pl.when(step == NPX + 3)
    def _():
        flux = jnp.concatenate([fb[i, :4, :] for i in range(NPX)], axis=0)
        nt_ref[...] = ft[...] + (nr[...] - flux - 0.5 * ft[...]) / hc[...]


def block_inverse(base, y, g, w, roof, ft, nr, hc):
    late = pl.BlockSpec((2, ROWS, N), lambda t: (jnp.maximum(t - NPX, 0), 0, 0))
    return pl.pallas_call(
        block_inverse_kernel, grid=(NPX + 4,),
        out_shape=(jax.ShapeDtypeStruct((LEV, ROWS, N), F32), jax.ShapeDtypeStruct((32, 128), F32)),
        in_specs=[SM, pl.BlockSpec((1, BACK, 128), lambda t: (jnp.minimum(t, NPX - 1), 0, 0)),
                  pl.BlockSpec((LEV, ROWS, 128), lambda t: (0, 0, jnp.minimum(t, NPX - 1))),
                  late, fixed((ROWS, N)), fixed((1536, 512)), fixed((256, 128)),
                  pl.BlockSpec((8, 128), lambda t: (0, jnp.minimum(t, NPX - 1))), fixed((3, ROWS, 128)),
                  fixed((32, 128)), fixed((32, 128)), fixed((32, 128))],
        out_specs=(late, fixed((32, 128))),
        scratch_shapes=[pltpu.VMEM((LEV, ROWS, N), F32), pltpu.VMEM((ROWS, N), F32), pltpu.VMEM((ROWS, 256), F32),
                        pltpu.VMEM((NPX, 8, 128), F32)],
        compiler_params=params(40), name="block_inverse",
    )(base, y, g, w, roof, jnp.asarray(TAB_T), jnp.asarray(SINE2), jnp.asarray(LAM_X), jnp.asarray(COLS), ft, nr, hc)


def swap(x, axes):
    return lax.all_to_all(x, axes, split_axis=0, concat_axis=0, tiled=True)


def body(horiz_div, w_star, air_temp, roof_level, facet_cells, facet_temp, net_radiation,
         heat_capacity, drag_coef, heat_coef):
    ix, iy = lax.axis_index("px"), lax.axis_index("py")
    ft, nr, hc, dr, he, ce = [
        v.reshape(32, 128) for v in (facet_temp, net_radiation, heat_capacity, drag_coef, heat_coef, facet_cells)]
    owner, ids, addr = pack_owner(ft, dr, he, ce)
    od = swap(owner.reshape(OWNERS, 1, 128), ("px", "py")).reshape(OWNERS, 128)
    addr = addr.reshape(OWNERS * SLOT)
    w2, a2 = w_star.reshape(1024, 1024), air_temp.reshape(1024, 1024)
    wc = gather_w(addr, ids, w2)
    w_corr = scatter_w(addr, ids, wc, od, w2)
    halo = lax.ppermute(w_corr[:ROWS], "py", [(j, j - 1) for j in range(1, NPY)])
    w_corr = w_corr.reshape(LEV, ROWS, N)

    eig = jnp.asarray(EIGEN.astype(np.float32))
    eig_x = lax.dynamic_slice_in_dim(eig, ix * 128, 128)
    eig_y = lax.dynamic_slice_in_dim(eig, iy * 64, 64)
    lam = eig[:, None] + eig_x[None, :]
    lam_mine = eig_y[:, None] + eig_x[None, :]

    sent, g = block_solve(block_modes(horiz_div, w_corr), halo)
    xs = swap(sent, "px")
    shift = ((iy % 4) * SLOT).astype(jnp.int32).reshape(1)
    theta, fl = heat_cells(addr, shift, sent, ids, wc, od, a2)
    al = y_forward(xs, lam)
    pu = swap(ladder(swap(al, "py"), lam_mine, fl), "py")
    ys = swap(y_inverse(xs, pu, lam), "px")
    base = (iy * LEV).astype(jnp.int32).reshape(1)
    w_new, temp_new = block_inverse(base, ys, g, w_corr, roof_level, ft, nr, hc)
    return w_new, theta.reshape(LEV, ROWS, N), temp_new.reshape(1, OWNERS * SLOT)


def solution(mesh):
    field, facet = P("py", "px", None), P(("px", "py"), None)
    return jax.shard_map(
        body, mesh=mesh,
        in_specs=(field, field, field, P("px", None)) + (facet,) * 6,
        out_specs=(field, field, facet), check_vma=False)
```

time: 234 us -> 213 us (0.910)
  waiting for transfers between devices: 55.2 us -> 37.6 us
  local copies, waits for them, and re-layouts: 19.7 us -> 29.5 us
  other arithmetic: 10.2 us -> 2.22 us
  starting transfers between devices: 41.6 us -> 34.7 us
  blocking collectives: 17.7 us -> 22.3 us
  Pallas kernels: 87.8 us -> 84.6 us
    all_to_all x5 -> x4, waiting for transfers between devices: 42 us -> 29.8 us  [swap(): return lax.all_to_all(x, axes, split_axis=0, concat_axis=0, tiled=True)]
    unnamed x46 -> x76, local copies, waits for them, and re-layouts: 17.2 us -> 27.4 us
    all_to_all x5 -> x4, starting transfers between devices: 40.3 us -> 33.4 us  [swap(): return lax.all_to_all(x, axes, split_axis=0, concat_axis=0, tiled=True)]
    unnamed x4 -> x0, other arithmetic: 5.57 us -> none
    ppermute x1, waiting for transfers between devices: 13.2 us -> 7.81 us  [body(): lax.ppermute(w_corr[:ROWS], 'py', [(j, j - 1) for j in range(1, NPY)])]
    all_to_all x1, blocking collectives: 17.7 us -> 22.3 us  [swap(): return lax.all_to_all(x, axes, split_axis=0, concat_axis=0, tiled=True)]
    pallas_call x7 -> x10, Pallas kernels: 87.8 us -> 84.6 us  [the longest x1 18.7 us: heat_cells(): pl.pallas_call(heat_kernel, out_shape=(jax.ShapeDtypeStruct((1024, 1024),...]
  transfers between devices with their start and end apart: 6 -> 5, of which waited for: 4 -> 3; matrix products, arithmetic and copies ran while one was open for 3% -> 2% of each run, Pallas kernels for 7% -> 15%
where the time goes in v3:
time: 213 us; the launch traced here: 212 us
  Pallas kernels  84.6 us (40%)
  waiting for transfers between devices  37.6 us (18%)
  starting transfers between devices  34.7 us (16%)
  local copies, waits for them, and re-layouts  29.5 us (14%)
  blocking collectives  22.3 us (10%)
  other arithmetic  2.22 us (1%)
    all_to_all x4, starting transfers between devices, swap(): return lax.all_to_all(x, axes, split_axis=0, concat_axis=0, tiled=True)  33.4 us
    all_to_all x4, waiting for transfers between devices, swap(): return lax.all_to_all(x, axes, split_axis=0, concat_axis=0, tiled=True)  29.8 us
    unnamed x76, local copies, waits for them, and re-layouts  27.4 us
    all_to_all x1, blocking collectives, swap(): return lax.all_to_all(x, axes, split_axis=0, concat_axis=0, tiled=True)  22.3 us
    pallas_call x1, Pallas kernels, heat_cells(): pl.pallas_call(heat_kernel, out_shape=(jax.ShapeDtypeStruct((1024, 1024),...  18.7 us
    pallas_call x1, Pallas kernels, block_inverse(): pl.pallas_call(block_inverse_kernel, grid=(NPX + 4,), out_shape=(jax.Shap...  16.4 us
    pallas_call x1, Pallas kernels, scatter_w(): pl.pallas_call(scatter_w_kernel, out_shape=jax.ShapeDtypeStruct((1024, 10...  11.3 us
    pallas_call x1, Pallas kernels, block_solve(): pl.pallas_call(block_solve_kernel, grid=(NPX,), out_shape=(jax.ShapeDtype...  9.55 us
  transfers between devices with their start and end apart: 5, of which 3 were waited for; matrix products, arithmetic and copies ran while one was open for 2% of the time, Pallas kernels for 15%

profile of v3, /device:TPU:1, one launch (start us, length us, event | category | flops | bytes accessed | tf_op | source)
XLA Modules:
  0.0 212.0 jit_solution(11952234451595582487)
XLA Ops:
  4.2 11.5 %all-to-all-start = ((f32[128,1,128]{2,1,0:T(1,128)}), f32[128,1,128]{2,1,0:T(1,128)S(1)}, u32[]{:S(2)}, u32[]{:S(2)}) async-start(f32[128,1,128]{2,1,0:T(1,128)} %bitcast.8), calls=%async_computation | async-start | bytes 131072 | tf_op jit(solution)/shard_map/all_to_all | solution.py:626
  15.8 2.2 %copy-done.2 = f32[8,128,1024]{2,1,0:T(8,128)S(1)} copy-done((f32[8,128,1024]{2,1,0:T(8,128)S(1)}, f32[8,128,1024]{2,1,0:T(8,128)}, u32[]{:S(2)}) %copy-start.2) | copy-done | bytes 4194328
  17.9 8.6 %facet_gather.1.wc_ref = f32[128,128]{1,0:T(8,128)S(1)} custom-call(s32[4096]{0:T(1024)S(1)} %bitcast.26, s32[128,128]{1,0:T(8,128)S(1)} %get-tuple-element.13.ids_ref, f32[1024,1024]{1,0:T(8,128)S(1)} %bitcast.21), custom_call_target="tpu_custom_call" | custom-call | tf_op jit(solution)/shard_map/facet_gather/pallas_call | solution.py:171
  26.6 2.2 %copy-done.3 = f32[8,128,1024]{2,1,0:T(8,128)S(1)} copy-done((f32[8,128,1024]{2,1,0:T(8,128)S(1)}, f32[8,128,1024]{2,1,0:T(8,128)}, u32[]{:S(2)}) %copy-start.3) | copy-done | bytes 4194328
  28.9 11.3 %scatter_w.1 = f32[1024,1024]{1,0:T(8,128)S(1)} custom-call(s32[4096]{0:T(1024)S(1)} %bitcast.27, s32[128,128]{1,0:T(8,128)S(1)} %get-tuple-element.13.ids_ref, f32[128,128]{1,0:T(8,128)S(1)} %facet_gather.1.wc_ref, f32[128,128]{1,0:T(8,128)S(1)} %bitcast.24, f32[1024,1024]{1,0:T(8,128)S(1)} %bitcast.22), custom_call_target="tpu_custom_call" | custom-call | tf_op jit(solution)/shard_map/scatter_w/pallas_call | solution.py:198
  40.3 1.3 collective-permute-start
  41.6 5.2 %block_modes.1.r_ref = f32[8,128,1024]{2,1,0:T(8,128)S(1)} custom-call(f32[8,128,1024]{2,1,0:T(8,128)S(1)} %copy-done.13, f32[8,128,1024]{2,1,0:T(8,128)S(1)} %bitcast.18, f32[8,128,1024]{2,1,0:T(8,128)S(1)} %bitcast.19, bf16[1536,512]{1,0:T(8,128)(2,1)S(1)} %copy-done.4, bf16[256,128]{1,0:T(8,128)(2,1)S(1)} %copy-done.18), custom_call_target="tpu_custom_call" | custom-call | bytes 26214400 | tf_op jit(solution)/shard_map/block_modes/pallas_call | solution.py:338
  46.9 7.8 %collective-permute-done.halo_ref = f32[128,1024]{1,0:T(8,128)S(1)} collective-permute-done((f32[128,1024]{1,0:T(8,128)S(1)}, f32[128,1024]{1,0:T(8,128)S(1)}, u32[]{:S(2)}, u32[]{:S(2)}) %collective-permute-start) | collective-permute-done | bytes 524320 | tf_op jit(solution)/shard_map/ppermute | solution.py:640
  54.7 9.5 %block_solve.1 = (f32[8,272,128]{2,1,0:T(8,128)S(1)}, f32[8,128,1024]{2,1,0:T(8,128)S(1)}) custom-call(f32[8,128,1024]{2,1,0:T(8,128)S(1)} %block_modes.1.r_ref, f32[128,1024]{1,0:T(8,128)S(1)} %collective-permute-done.halo_ref, bf16[1536,512]{1,0:T(8,128)(2,1)S(1)} %copy-done.4, bf16[256,128]{1,0:T(8,128)(2,1)S(1)} %copy-done.18, f32[8,1024]{1,0:T(8,128)S(1)} %copy-done.24, ...), custom_call_target="tpu_custom_call" | custom-call | tf_op jit(solution)/shard_map/block_solve/pallas_call | solution.py:386
  64.2 1.0 copy-done.8
  65.2 2.0 copy-done.10
  67.2 6.3 %all-to-all-start.1 = ((f32[8,272,128]{2,1,0:T(8,128)}), f32[8,272,128]{2,1,0:T(8,128)S(1)}, u32[]{:S(2)}, u32[]{:S(2)}) async-start(f32[8,272,128]{2,1,0:T(8,128)} %copy-done.8), calls=%async_computation.1 | async-start | bytes 2228224 | tf_op jit(solution)/shard_map/all_to_all | solution.py:626
  75.7 13.6 %all-to-all-done.1.x_ref = f32[8,272,128]{2,1,0:T(8,128)S(1)} async-done(((f32[8,272,128]{2,1,0:T(8,128)}), f32[8,272,128]{2,1,0:T(8,128)S(1)}, u32[]{:S(2)}, u32[]{:S(2)}) %all-to-all-start.1) | async-done | bytes 1114144 | tf_op jit(solution)/shard_map/all_to_all | solution.py:626
  89.3 1.4 copy-done.5
  90.7 1.0 copy-done.14
  91.8 3.7 %y_forward.1 = f32[16,128,128]{2,1,0:T(8,128)S(1)} custom-call(f32[8,272,128]{2,1,0:T(8,128)S(1)} %all-to-all-done.1.x_ref, f32[1024,128]{1,0:T(8,128)S(1)} %broadcast_add_fusion.lam_ref, bf16[1536,512]{1,0:T(8,128)(2,1)S(1)} %copy-done.5, bf16[2048,16]{1,0:T(8,128)(2,1)S(1)} %copy-done.14), custom_call_target="tpu_custom_call" | custom-call | tf_op jit(solution)/shard_map/y_forward/pallas_call | solution.py:440
  96.5 9.2 %all-to-all-start.2 = ((f32[16,128,128]{2,1,0:T(8,128)}), f32[16,128,128]{2,1,0:T(8,128)}, u32[]{:S(2)}, u32[]{:S(2)}) async-start(f32[16,128,128]{2,1,0:T(8,128)} %copy-done.12), calls=%async_computation.2 | async-start | bytes 2097152 | tf_op jit(solution)/shard_map/all_to_all | solution.py:626
  105.7 1.3 dynamic_slice.7
  107.0 1.3 broadcast_add_fusion.1.lam_ref
  108.3 1.2 copy-done.9
  109.6 1.6 copy-done.16
  112.9 18.7 %heat_cells.1 = (bf16[1024,1024]{1,0:T(8,128)(2,1)}, f32[16,8,128]{2,1,0:T(8,128)S(1)}) custom-call(s32[4096]{0:T(1024)S(1)} %bitcast.28, s32[1]{0:T(128)} %bitcast.11.shift, f32[8,272,128]{2,1,0:T(8,128)S(1)} %copy-done.9, s32[128,128]{1,0:T(8,128)S(1)} %get-tuple-element.13.ids_ref, f32[128,128]{1,0:T(8,128)S(1)} %copy-done.20, f32[128,128]{1,0:T(8,128)S(1)} %bitcast.25, ...), custom_call_target="tpu_custom_call" | custom-call | bytes 62914560 | tf_op jit(solution)/shard_map/heat_cells/pallas_call | solution.py:231
  133.8 4.2 %ladder.1 = f32[16,136,128]{2,1,0:T(8,128)S(1)} custom-call(f32[16,128,128]{2,1,0:T(8,128)} %all-to-all-done.2.al_ref, f32[64,128]{1,0:T(8,128)S(1)} %copy-done.26, f32[16,8,128]{2,1,0:T(8,128)S(1)} %copy-done.31), custom_call_target="tpu_custom_call" | custom-call | tf_op jit(solution)/shard_map/ladder/pallas_call | solution.py:480
  138.0 22.3 %all_to_all.25.pu_ref = f32[16,136,128]{2,1,0:T(8,128)S(1)} all-to-all(f32[16,136,128]{2,1,0:T(8,128)S(1)} %ladder.1), channel_id=1, replica_groups=mesh['px'=8,'py'=16] {'py'}, dimensions={0} | all-to-all | bytes 2228224 | tf_op jit(solution)/shard_map/all_to_all | solution.py:626
  160.3 6.1 %y_inverse.1 = f32[8,280,128]{2,1,0:T(8,128)S(1)} custom-call(f32[8,272,128]{2,1,0:T(8,128)S(1)} %all-to-all-done.1.x_ref, f32[16,136,128]{2,1,0:T(8,128)S(1)} %all_to_all.25.pu_ref, f32[1024,128]{1,0:T(8,128)S(1)} %broadcast_add_fusion.lam_ref, bf16[1536,512]{1,0:T(8,128)(2,1)S(1)} %copy-done.4, bf16[2048,16]{1,0:T(8,128)(2,1)S(1)} %copy-done.15, ...), custom_call_target="tpu_custom_call" | custom-call | tf_op jit(solution)/shard_map/y_inverse/pallas_call | solution.py:542
  166.4 1.0 copy-done.7
  167.5 6.5 %all-to-all-start.4 = ((f32[8,280,128]{2,1,0:T(8,128)}), f32[8,280,128]{2,1,0:T(8,128)S(1)}, u32[]{:S(2)}, u32[]{:S(2)}) async-start(f32[8,280,128]{2,1,0:T(8,128)} %copy-done.7), calls=%async_computation.4 | async-start | bytes 2293760 | tf_op jit(solution)/shard_map/all_to_all | solution.py:626
  174.0 16.2 %all-to-all-done.4.y_ref = f32[8,280,128]{2,1,0:T(8,128)S(1)} async-done(((f32[8,280,128]{2,1,0:T(8,128)}), f32[8,280,128]{2,1,0:T(8,128)S(1)}, u32[]{:S(2)}, u32[]{:S(2)}) %all-to-all-start.4) | async-done | bytes 1146912 | tf_op jit(solution)/shard_map/all_to_all | solution.py:626
  190.2 2.2 %copy-done.1 = f32[1024,1024]{1,0:T(8,128)S(1)} copy-done((f32[1024,1024]{1,0:T(8,128)S(1)}, f32[1024,1024]{1,0:T(8,128)}, u32[]{:S(2)}) %copy-start.1) | copy-done | bytes 4194328
  192.4 2.2 %copy-done.11 = f32[8,128,1024]{2,1,0:T(8,128)S(1)} copy-done((f32[8,128,1024]{2,1,0:T(8,128)S(1)}, f32[8,128,1024]{2,1,0:T(8,128)}, u32[]{:S(2)}) %copy-start.11) | copy-done | bytes 4194328
  194.5 1.0 copy-done.23
  195.6 16.4 %block_inverse.1 = (f32[8,128,1024]{2,1,0:T(8,128)}, f32[32,128]{1,0:T(8,128)}) custom-call(s32[1]{0:T(128)} %bitcast.base_ref, f32[8,280,128]{2,1,0:T(8,128)S(1)} %all-to-all-done.4.y_ref, f32[8,128,1024]{2,1,0:T(8,128)S(1)} %copy-done.11, f32[8,128,1024]{2,1,0:T(8,128)S(1)} %bitcast.20, s32[128,1024]{1,0:T(8,128)S(1)} %copy-done.23, ...), custom_call_target="tpu_custom_call" | custom-call | tf_op jit(solution)/shard_map/block_inverse/pallas_call | solution.py:610
  (70 shorter events, 10.8 us)
Async XLA Ops:
  4.2 22.4 %all-to-all-start = ((f32[128,1,128]{2,1,0:T(1,128)}), f32[128,1,128]{2,1,0:T(1,128)S(1)}, u32[]{:S(2)}, u32[]{:S(2)}) async-start(f32[128,1,128]{2,1,0:T(1,128)} %bitcast.8), calls=%async_computation | async-start | bytes 131072 | tf_op jit(solution)/shard_map/all_to_all | solution.py:626
  15.7 2.2 %copy-start.2 = (f32[8,128,1024]{2,1,0:T(8,128)S(1)}, f32[8,128,1024]{2,1,0:T(8,128)}, u32[]{:S(2)}) copy-start(f32[8,128,1024]{2,1,0:T(8,128)} %param.19) | copy-start | bytes 12582916
  26.6 13.6 %copy-start.19 = (f32[128,128]{1,0:T(8,128)}, f32[128,128]{1,0:T(8,128)S(1)}, u32[]{:S(2)}) copy-start(f32[128,128]{1,0:T(8,128)S(1)} %facet_gather.1.wc_ref) | copy-start | bytes 196612
  26.6 13.6 %copy-start.21 = (f32[128,1,128]{2,1,0:T(1,128)}, f32[128,1,128]{2,1,0:T(1,128)S(1)}, u32[]{:S(2)}) copy-start(f32[128,1,128]{2,1,0:T(1,128)S(1)} %all-to-all-done) | copy-start | bytes 196612
  26.6 2.2 %copy-start.3 = (f32[8,128,1024]{2,1,0:T(8,128)S(1)}, f32[8,128,1024]{2,1,0:T(8,128)}, u32[]{:S(2)}) copy-start(f32[8,128,1024]{2,1,0:T(8,128)} %param.19) | copy-start | bytes 12582916
  28.8 12.7 %copy-start.4 = (bf16[1536,512]{1,0:T(8,128)(2,1)S(1)}, bf16[1536,512]{1,0:T(8,128)(2,1)}, u32[]{:S(2)}) copy-start(bf16[1536,512]{1,0:T(8,128)(2,1)} %constant.50.clone.tab) | copy-start | bytes 4718596
  28.9 12.7 %copy-start.13 = (f32[8,128,1024]{2,1,0:T(8,128)S(1)}, f32[8,128,1024]{2,1,0:T(8,128)}, u32[]{:S(2)}) copy-start(f32[8,128,1024]{2,1,0:T(8,128)} %h_ref.1) | copy-start | bytes 12582916
  28.9 12.8 %copy-start.18 = (bf16[256,128]{1,0:T(8,128)(2,1)S(1)}, bf16[256,128]{1,0:T(8,128)(2,1)}, u32[]{:S(2)}) copy-start(bf16[256,128]{1,0:T(8,128)(2,1)} %constant.51.clone.sine) | copy-start | bytes 196612
  40.2 6.6 %copy-start = (f32[1024,1024]{1,0:T(8,128)}, f32[1024,1024]{1,0:T(8,128)S(1)}, u32[]{:S(2)}) copy-start(f32[1024,1024]{1,0:T(8,128)S(1)} %scatter_w.1) | copy-start | bytes 12582916
  40.3 14.4 %collective-permute-start = (f32[128,1024]{1,0:T(8,128)S(1)}, f32[128,1024]{1,0:T(8,128)S(1)}, u32[]{:S(2)}, u32[]{:S(2)}) collective-permute-start(f32[128,1024]{1,0:T(8,128)S(1)} %slice.4), channel_id=1, source_target_pairs={{1,0},{2,1},{3,2},{4,3},{5,4},{6,5},{7,6},{8,7},{9,8},{10,9},{11,1... | collective-permute-start | bytes 1572872 | tf_op jit(solution)/shard_map/ppermute | solution.py:640
  41.6 13.1 %copy-start.17 = (f32[3,128,128]{2,1,0:T(8,128)S(1)}, f32[3,128,128]{2,1,0:T(8,128)}, u32[]{:S(2)}) copy-start(f32[3,128,128]{2,1,0:T(8,128)} %constant.53.clone.cols) | copy-start | bytes 589828
  41.6 13.0 %copy-start.24 = (f32[8,1024]{1,0:T(8,128)S(1)}, f32[8,1024]{1,0:T(8,128)}, u32[]{:S(2)}) copy-start(f32[8,1024]{1,0:T(8,128)} %constant.52.clone.lx) | copy-start | bytes 98308
  64.2 1.0 copy-start.8
  65.2 2.0 copy-start.10
  67.2 22.1 %all-to-all-start.1 = ((f32[8,272,128]{2,1,0:T(8,128)}), f32[8,272,128]{2,1,0:T(8,128)S(1)}, u32[]{:S(2)}, u32[]{:S(2)}) async-start(f32[8,272,128]{2,1,0:T(8,128)} %copy-done.8), calls=%async_computation.1 | async-start | bytes 2228224 | tf_op jit(solution)/shard_map/all_to_all | solution.py:626
  89.3 1.4 copy-start.5
  90.7 1.0 copy-start.14
  96.5 35.7 %all-to-all-start.2 = ((f32[16,128,128]{2,1,0:T(8,128)}), f32[16,128,128]{2,1,0:T(8,128)}, u32[]{:S(2)}, u32[]{:S(2)}) async-start(f32[16,128,128]{2,1,0:T(8,128)} %copy-done.12), calls=%async_computation.2 | async-start | bytes 2097152 | tf_op jit(solution)/shard_map/all_to_all | solution.py:626
  108.3 1.2 copy-start.9
  109.6 1.6 copy-start.16
  133.8 26.6 %copy-start.15 = (bf16[2048,16]{1,0:T(8,128)(2,1)S(1)}, bf16[2048,16]{1,0:T(8,128)(2,1)}, u32[]{:S(2)}) copy-start(bf16[2048,16]{1,0:T(8,128)(2,1)} %constant.55.clone.edge.edge_f) | copy-start | bytes 196612
  133.8 26.6 %copy-start.27 = (bf16[32,1024]{1,0:T(8,128)(2,1)S(1)}, bf16[32,1024]{1,0:T(8,128)(2,1)}, u32[]{:S(2)}) copy-start(bf16[32,1024]{1,0:T(8,128)(2,1)} %constant.56.clone.edge_b) | copy-start | bytes 196612
  166.4 1.0 copy-start.7
  167.5 22.7 %copy-start.6 = (bf16[1536,512]{1,0:T(8,128)(2,1)S(1)}, bf16[1536,512]{1,0:T(8,128)(2,1)}, u32[]{:S(2)}) copy-start(bf16[1536,512]{1,0:T(8,128)(2,1)} %constant.54.clone.tab) | copy-start | bytes 4718596
  167.5 22.7 %copy-start.25 = (f32[8,1024]{1,0:T(8,128)S(1)}, f32[8,1024]{1,0:T(8,128)}, u32[]{:S(2)}) copy-start(f32[8,1024]{1,0:T(8,128)} %constant.52.clone.lx) | copy-start | bytes 98308
  167.5 22.7 %copy-start.29 = (f32[1,4096]{1,0:T(1,128)S(1)}, f32[1,4096]{1,0:T(1,128)}, u32[]{:S(2)}) copy-start(f32[1,4096]{1,0:T(1,128)} %param.23) | copy-start | bytes 49156
  167.5 22.7 %copy-start.32 = (f32[1,4096]{1,0:T(1,128)S(1)}, f32[1,4096]{1,0:T(1,128)}, u32[]{:S(2)}) copy-start(f32[1,4096]{1,0:T(1,128)} %param.24) | copy-start | bytes 49156
  167.5 22.7 %copy-start.33 = (f32[1,4096]{1,0:T(1,128)S(1)}, f32[1,4096]{1,0:T(1,128)}, u32[]{:S(2)}) copy-start(f32[1,4096]{1,0:T(1,128)} %param.25) | copy-start | bytes 49156
  167.5 22.6 %all-to-all-start.4 = ((f32[8,280,128]{2,1,0:T(8,128)}), f32[8,280,128]{2,1,0:T(8,128)S(1)}, u32[]{:S(2)}, u32[]{:S(2)}) async-start(f32[8,280,128]{2,1,0:T(8,128)} %copy-done.7), calls=%async_computation.4 | async-start | bytes 2293760 | tf_op jit(solution)/shard_map/all_to_all | solution.py:626
  190.2 2.2 %copy-start.1 = (f32[1024,1024]{1,0:T(8,128)S(1)}, f32[1024,1024]{1,0:T(8,128)}, u32[]{:S(2)}) copy-start(f32[1024,1024]{1,0:T(8,128)} %copy-done) | copy-start | bytes 12582916
  192.4 2.2 %copy-start.11 = (f32[8,128,1024]{2,1,0:T(8,128)S(1)}, f32[8,128,1024]{2,1,0:T(8,128)}, u32[]{:S(2)}) copy-start(f32[8,128,1024]{2,1,0:T(8,128)} %copy-done.10) | copy-start | bytes 12582916
  194.5 1.0 copy-start.23
  (11 other events, 8.3 us)

commit v4 on v3

--- a/solution.py
+++ b/solution.py
@@ -14,6 +14,7 @@
 LEV, ROWS = 8, 128
 OWNERS, SLOT = 128, 32
 MIB = 1 << 20
+VMEM_MIB = 58
 F32, BF16 = jnp.float32, jnp.bfloat16
 
 
@@ -64,6 +65,7 @@
     return pltpu.CompilerParams(vmem_limit_bytes=mb * MIB)
 
 
+TOKEN = jax.ShapeDtypeStruct((8, 128), F32)
 VM = pl.BlockSpec(memory_space=pltpu.VMEM)
 SM = pl.BlockSpec(memory_space=pltpu.SMEM)
 
@@ -85,7 +87,7 @@
     return pl.pallas_call(
         pack_kernel, out_shape=(full, jax.ShapeDtypeStruct((OWNERS, 128), jnp.int32),
                                 jax.ShapeDtypeStruct((32, 128), jnp.int32)),
-        in_specs=[VM] * 4, out_specs=(VM,) * 3, compiler_params=params(16), name="pack_owner",
+        in_specs=[VM] * 4, out_specs=(VM,) * 3, compiler_params=params(VMEM_MIB), name="pack_owner",
     )(ft, dr, he, ce)
 
 
@@ -171,7 +173,7 @@
     return pl.pallas_call(
         gather_kernel, out_shape=jax.ShapeDtypeStruct((OWNERS, 128), F32), in_specs=[SM, VM, VM], out_specs=VM,
         scratch_shapes=[pltpu.VMEM((8192, 128), F32), pltpu.VMEM((4096, 128), F32)],
-        compiler_params=params(32), name="facet_gather",
+        compiler_params=params(VMEM_MIB), name="facet_gather",
     )(addr, ids, w2)
 
 
@@ -198,24 +200,40 @@
     return pl.pallas_call(
         scatter_w_kernel, out_shape=jax.ShapeDtypeStruct((1024, 1024), F32),
         in_specs=[SM, VM, VM, VM, VM], out_specs=VM, scratch_shapes=FOUR,
-        compiler_params=params(40), name="scatter_w",
+        compiler_params=params(VMEM_MIB), name="scatter_w",
     )(addr, ids, wc, od, w2)
 
 
-def heat_kernel(addr, shift, after, ids_ref, wc_ref, od_ref, a_ref, th_ref, fl_ref, acc0, acc1, acc2, acc3, buf, turned):
+def flux_kernel(addr, tok_in, ids_ref, wc_ref, od_ref, a_ref, flux_ref, fl_ref, tok_ref, tt, buf, turned):
+    load_temp(a_ref, tt)
+    gather_rows(addr, tt, buf)
+    tc = pick(ids_ref[...], buf)[:, :SLOT]
+    wc = wc_ref[:, :SLOT]
+    flux = od_ref[:, 64:96] * jnp.sqrt(wc * wc + 0.25) * (od_ref[:, :32] - tc)
+    wide = jnp.concatenate([flux, jnp.zeros((OWNERS, 96), F32)], axis=1)
+    flux_ref[...] = wide
+    turned[...] = pltpu.roll(wide, (lax.axis_index("py") % 4) * SLOT, 1)
+    for j in range(NPY):
+        fl_ref[j] = turned[pl.ds(j, 8, stride=16), :]
+    tok_ref[...] = tok_in[...]
+
+
+def heat_flux(addr, tok, ids, wc, od, a2):
+    return pl.pallas_call(
+        flux_kernel,
+        out_shape=(jax.ShapeDtypeStruct((OWNERS, 128), F32), jax.ShapeDtypeStruct((NPY, 8, 128), F32), TOKEN),
+        in_specs=[SM] + [VM] * 5, out_specs=(VM,) * 3,
+        scratch_shapes=[pltpu.VMEM((8192, 128), F32), pltpu.VMEM((4096, 128), F32), pltpu.VMEM((OWNERS, 128), F32)],
+        cost_estimate=pl.CostEstimate(flops=0, bytes_accessed=25 * MIB, transcendentals=0),
+        compiler_params=params(VMEM_MIB), name="heat_flux",
+    )(addr, tok, ids, wc, od, a2)
+
+
+def theta_kernel(addr, tok_in, ids_ref, flux_ref, a_ref, th_ref, tok_ref, acc0, acc1, acc2, acc3, buf):
     accs = (acc0, acc1, acc2, acc3)
     load_temp(a_ref, acc0)
-    gather_rows(addr, acc0, buf)
-    ids = ids_ref[...]
-    tc = pick(ids, buf)[:, :SLOT]
     clear(accs[1:])
-    wc = wc_ref[:, :SLOT]
-    flux = od_ref[:, 64:96] * jnp.sqrt(wc * wc + 0.25) * (od_ref[:, :32] - tc)
-    spread_rows(ids, flux, buf)
-    wide = jnp.concatenate([flux, jnp.zeros((OWNERS, 96), F32)], axis=1)
-    turned[...] = pltpu.roll(wide, shift[0], 1)
-    for j in range(NPY):
-        fl_ref[j] = turned[pl.ds(j, 8, stride=16), :]
+    spread_rows(ids_ref[...], flux_ref[...], buf)
     add_rows(addr, accs, buf)
 
     def put(i, c):
@@ -225,17 +243,16 @@
             th_ref[tile(i, 16), ct * 128:(ct + 1) * 128] = jnp.concatenate([v0, v1], axis=0).astype(BF16)
         return c
     lax.fori_loop(0, 64, put, 0)
-
-
-def heat_cells(addr, shift, after, ids, wc, od, a2):
-    return pl.pallas_call(
-        heat_kernel,
-        out_shape=(jax.ShapeDtypeStruct((1024, 1024), BF16), jax.ShapeDtypeStruct((NPY, 8, 128), F32)),
-        in_specs=[SM, SM, pl.BlockSpec(memory_space=pl.ANY), VM, VM, VM, VM], out_specs=(VM, VM),
-        scratch_shapes=FOUR + [pltpu.VMEM((OWNERS, 128), F32)],
-        cost_estimate=pl.CostEstimate(flops=0, bytes_accessed=60 * MIB, transcendentals=0),
-        compiler_params=params(40), name="heat_cells",
-    )(addr, shift, after, ids, wc, od, a2)
+    tok_ref[...] = tok_in[...]
+
+
+def new_theta(addr, tok, ids, flux, a2):
+    return pl.pallas_call(
+        theta_kernel, out_shape=(jax.ShapeDtypeStruct((1024, 1024), BF16), TOKEN),
+        in_specs=[SM] + [VM] * 4, out_specs=(VM, VM), scratch_shapes=FOUR,
+        cost_estimate=pl.CostEstimate(flops=0, bytes_accessed=40 * MIB, transcendentals=0),
+        compiler_params=params(VMEM_MIB), name="new_theta",
+    )(addr, tok, ids, flux, a2)
 
 
 BLK = 2 * ROWS + 2 * LEV
@@ -272,6 +289,7 @@
 SINE2 = np.concatenate(split_np(SINE))
 EDGE_F = np.concatenate(split_np(EDGE.T))
 EDGE_B = np.concatenate(split_np(EDGE))
+LAM_Y = np.broadcast_to(EIGEN.astype(np.float32)[:, None], (N, 128)).copy()
 LAM_X = np.broadcast_to(EIGEN.astype(np.float32), (8, N)).copy()
 COLS = np.stack([np.broadcast_to(v[:, None], (ROWS, 128)) for v in (MU, SINE[:, 0], SINE[:, 127])]).astype(np.float32)
 
@@ -324,74 +342,75 @@
             (512, dot3(*split(d), *td)))
 
 
-def block_modes_kernel(h_ref, w_ref, wn_ref, tab, sine, out_ref):
-    up = jnp.where(pl.program_id(0) == 3, 0.0, wn_ref[0])
-    r = jnp.concatenate([h_ref[0] + w_ref[1] - w_ref[0], h_ref[1] + up - w_ref[1]], axis=0)
-    for c0, res in x_modes(r, tab):
-        for l in range(2):
-            out_ref[l, :, c0:c0 + res.shape[1]] = dot3(
-                sine[:128, :], sine[128:, :], *split(res[l * 128:(l + 1) * 128]))
-
-
-def block_modes(h, w):
-    two = pl.BlockSpec((2, ROWS, N), lambda g: (g, 0, 0))
-    return pl.pallas_call(
-        block_modes_kernel, grid=(4,), out_shape=jax.ShapeDtypeStruct((LEV, ROWS, N), F32),
-        in_specs=[two, two, pl.BlockSpec((1, ROWS, N), lambda g: (jnp.minimum(2 * g + 2, 7), 0, 0)),
-                  fixed((1536, 512)), fixed((256, 128))],
-        out_specs=two, compiler_params=params(32), name="block_modes",
-        cost_estimate=pl.CostEstimate(flops=0, bytes_accessed=25 * MIB, transcendentals=0),
-    )(h, w, w, jnp.asarray(TAB), jnp.asarray(SINE2))
-
-
-def block_solve_kernel(r_ref, halo_ref, tab, sine, lx, cols, out_ref, g_ref, hx, a07):
-    lt = pl.program_id(0)
+def block_forward_kernel(h_ref, w_ref, wn_ref, tab, sine, lx, cols, out_ref, g_ref, tok_ref, r2, hx, a07):
+    step = pl.program_id(0)
     sh, sl = sine[:128, :], sine[128:, :]
 
-    @pl.when(lt == 0)
+    @pl.when(step == 0)
     def _():
-        for c0, res in x_modes(halo_ref[...], tab):
-            res = dot3(sh, sl, *split(res))
+        tok_ref[...] = jnp.zeros((8, 128), F32)
+        lifted = (lax.axis_index("py") > 0).astype(F32)
+        for c0, res in x_modes(w_ref[0] * lifted, tab):
             for b in range(res.shape[1] // 128):
                 hx[c0 // 128 + b] = res[:, b * 128:(b + 1) * 128]
-    lam = lx[...]
-
-    def inner(bt, acc):
-        rows = tile(bt)
-        rs = [r_ref[k, rows, :] for k in range(LEV)]
-        rs[7] = rs[7] + hx[lt, rows, :]
-        mu, s0, s1 = cols[0, rows, :], cols[1, rows, :], cols[2, rows, :]
-        base = lam + mu
-        ps = []
-        for m in range(LEV):
-            p = combine(Q[:, m], rs) * inverse_of(base + float(THETA[m]))
-            g_ref[m, rows, :] = p
-            ps.append(p)
-        a07[rows, :128] = combine(Q[0], ps)
-        a07[rows, 128:] = combine(Q[7], ps)
-        return tuple(acc[m] + s0 * ps[m] for m in range(LEV)) + tuple(
-            acc[LEV + m] + s1 * ps[m] for m in range(LEV))
-    acc = lax.fori_loop(0, ROWS // 8, inner, tuple(jnp.zeros((8, 128), F32) for _ in range(16)))
-    for e in range(2):
-        sums = [jnp.sum(acc[e * LEV + m], axis=0, keepdims=True) for m in range(LEV)]
-        out_ref[0, 2 * ROWS + e * LEV:2 * ROWS + (e + 1) * LEV, :] = jnp.concatenate(
-            [combine(Q[k], sums) for k in range(LEV)], axis=0)
-    res = dot3(sh, sl, *split(a07[...]))
-    out_ref[0, :ROWS, :] = res[:, :128]
-    out_ref[0, ROWS:2 * ROWS, :] = res[:, 128:]
-
-
-def block_solve(r, halo):
-    col = pl.BlockSpec((LEV, ROWS, 128), lambda g: (0, 0, g))
-    return pl.pallas_call(
-        block_solve_kernel, grid=(NPX,),
-        out_shape=(jax.ShapeDtypeStruct((NPX, BLK, 128), F32), jax.ShapeDtypeStruct((LEV, ROWS, N), F32)),
-        in_specs=[col, fixed((ROWS, N)), fixed((1536, 512)), fixed((256, 128)),
-                  pl.BlockSpec((8, 128), lambda g: (0, g)), fixed((3, ROWS, 128))],
-        out_specs=(pl.BlockSpec((1, BLK, 128), lambda g: (g, 0, 0)), col),
-        scratch_shapes=[pltpu.VMEM((NPX, ROWS, 128), F32), pltpu.VMEM((ROWS, 256), F32)],
-        compiler_params=params(32), name="block_solve",
-    )(r, halo, jnp.asarray(TAB), jnp.asarray(SINE2), jnp.asarray(LAM_X), jnp.asarray(COLS))
+
+    @pl.when(step < 4)
+    def _():
+        up = jnp.where(step == 3, 0.0, wn_ref[0])
+        r = jnp.concatenate([h_ref[0] + w_ref[1] - w_ref[0], h_ref[1] + up - w_ref[1]], axis=0)
+        for c0, res in x_modes(r, tab):
+            for l in range(2):
+                v = dot3(sh, sl, *split(res[l * 128:(l + 1) * 128]))
+                for b in range(res.shape[1] // 128):
+                    r2[c0 // 128 + b, 2 * step + l] = v[:, b * 128:(b + 1) * 128]
+
+    @pl.when(step >= 4)
+    def _():
+        lt = step - 4
+        lam = lx[...]
+
+        def inner(bt, acc):
+            rows = tile(bt)
+            rs = [r2[lt, k, rows, :] for k in range(LEV)]
+            mu, s0, s1 = cols[0, rows, :], cols[1, rows, :], cols[2, rows, :]
+            base = lam + mu
+            ps = []
+            for m in range(LEV):
+                p = combine(Q[:, m], rs) * inverse_of(base + float(THETA[m]))
+                g_ref[m, rows, :] = p
+                ps.append(p)
+            a07[rows, :128] = combine(Q[0], ps)
+            a07[rows, 128:] = combine(Q[7], ps)
+            return tuple(acc[m] + s0 * ps[m] for m in range(LEV)) + tuple(
+                acc[LEV + m] + s1 * ps[m] for m in range(LEV))
+        acc = lax.fori_loop(0, ROWS // 8, inner, tuple(jnp.zeros((8, 128), F32) for _ in range(16)))
+        for e in range(2):
+            sums = [jnp.sum(acc[e * LEV + m], axis=0, keepdims=True) for m in range(LEV)]
+            out_ref[0, 2 * ROWS + e * LEV:2 * ROWS + (e + 1) * LEV, :] = jnp.concatenate(
+                [combine(Q[k], sums) for k in range(LEV)], axis=0)
+        res = dot3(sh, sl, *split(a07[...]))
+        out_ref[0, :ROWS, :] = res[:, :128] - hx[lt]
+        out_ref[0, ROWS:2 * ROWS, :] = res[:, 128:]
+
+
+def block_forward(h, w):
+    two = pl.BlockSpec((2, ROWS, N), lambda g: (jnp.minimum(g, 3), 0, 0))
+    return pl.pallas_call(
+        block_forward_kernel, grid=(4 + NPX,),
+        out_shape=(jax.ShapeDtypeStruct((NPX, BLK, 128), F32), jax.ShapeDtypeStruct((LEV, ROWS, N), F32), TOKEN),
+        in_specs=[two, two, pl.BlockSpec((1, ROWS, N), lambda g: (jnp.minimum(2 * g + 2, 7), 0, 0)),
+                  fixed((1536, 512)), fixed((256, 128)),
+                  pl.BlockSpec((8, 128), lambda g: (0, jnp.maximum(g - 4, 0))), fixed((3, ROWS, 128))],
+        out_specs=(pl.BlockSpec((1, BLK, 128), lambda g: (jnp.maximum(g - 4, 0), 0, 0)),
+                   pl.BlockSpec((LEV, ROWS, 128), lambda g: (0, 0, jnp.maximum(g - 4, 0))), fixed((8, 128))),
+        scratch_shapes=[pltpu.VMEM((NPX, LEV, ROWS, 128), F32), pltpu.VMEM((NPX, ROWS, 128), F32),
+                        pltpu.VMEM((ROWS, 256), F32)],
+        compiler_params=params(VMEM_MIB), name="block_forward",
+    )(h, w, w, jnp.asarray(TAB), jnp.asarray(SINE2), jnp.asarray(LAM_X), jnp.asarray(COLS))
+
+
+def lam_row(lx):
+    return lx[0:1, pl.ds(pl.multiple_of(lax.axis_index("px") * 128, 128), 128)]
 
 
 def edge_rows(x_ref, sr):
@@ -407,7 +426,7 @@
     return dot3(edge[tile(t, 128), :], edge[pl.ds(pl.multiple_of(N + t * 128, 128), 128), :], sh, sl)
 
 
-def y_forward_kernel(x_ref, lam_ref, tab, edge, al_ref, pp, sr, st):
+def y_forward_kernel(x_ref, tok, lx, ly, tab, edge, al_ref, pp, sr, st):
     x = jnp.concatenate([x_ref[:, :ROWS], x_ref[:, ROWS:2 * ROWS]], axis=-1).reshape(N, 256)
     s, d = x[:512] + x[512:], x[:512] - x[512:]
     ee, eo = s[:256] + s[256:], s[:256] - s[256:]
@@ -416,13 +435,14 @@
         res = dot3(*t, *split(v))
         pp[k0:k0 + res.shape[0], :] = res
     sh, sl = edge_rows(x_ref, sr)
+    lam_x = lam_row(lx)
 
     def some(t, c):
         st[...] = edge_modes(edge, t, sh, sl)
         for q in range(8):
             part = slice(q * 16, (q + 1) * 16)
             rows = pl.ds(pl.multiple_of(t * 128 + q * 16, 16), 16)
-            phi, theta, _ = slab_polys(lam_ref[rows, :])
+            phi, theta, _ = slab_polys(ly[rows, :] + lam_x)
             inv = inverse_of(phi[0])
             b0 = b7 = None
             for k in range(LEV):
@@ -436,24 +456,27 @@
     lax.fori_loop(0, 8, some, 0)
 
 
-def y_forward(x, lam):
+def y_forward(x, tok):
     return pl.pallas_call(
         y_forward_kernel, grid=(1,),
         out_shape=jax.ShapeDtypeStruct((NPY, 128, 128), F32),
-        in_specs=[fixed((NPX, BLK, 128)), fixed((N, 128)), fixed((1536, 512)), fixed((2 * N, 16))],
+        in_specs=[fixed((NPX, BLK, 128)), fixed((8, 128)), fixed((8, N)), fixed((N, 128)), fixed((1536, 512)),
+                  fixed((2 * N, 16))],
         out_specs=fixed((NPY, 128, 128)),
         scratch_shapes=[pltpu.VMEM((N, 256), F32), pltpu.VMEM((16, N), F32), pltpu.VMEM((128, N), F32)],
-        compiler_params=params(40), name="y_forward",
-    )(x, lam, jnp.asarray(TAB_T), jnp.asarray(EDGE_F))
-
-
-def ladder_kernel(al_ref, lam_ref, fl_ref, out_ref):
+        compiler_params=params(VMEM_MIB), name="y_forward",
+    )(x, tok, jnp.asarray(LAM_X), jnp.asarray(LAM_Y), jnp.asarray(TAB_T), jnp.asarray(EDGE_F))
+
+
+def ladder_kernel(al_ref, lx, ly, fl_ref, out_ref):
     for j in range(NPY):
         out_ref[j, 128:, :] = fl_ref[j]
 
-    def some(t, c):
-        rows, tops = tile(t), pl.ds(pl.multiple_of(64 + t * 8, 8), 8)
-        phi, theta, delta = slab_polys(lam_ref[rows, :])
+    lam_x = lam_row(lx)
+    mine = lax.axis_index("py") * 64
+    for t in range(8):
+        rows, tops = slice(t * 8, (t + 1) * 8), slice(64 + t * 8, 72 + t * 8)
+        phi, theta, delta = slab_polys(ly[pl.ds(pl.multiple_of(mine + t * 8, 8), 8), :] + lam_x)
         inv = 1.0 / phi[0]
         n07, n77, cc = inv, theta[7] * inv, delta * inv
         A = [None] * 17
@@ -472,20 +495,20 @@
             out_ref[j, rows, :] = p
             p = (al_ref[j, tops, :] + n77 * A[j + 1] + n07 * p) * e[j + 1]
             out_ref[j, tops, :] = A[j + 1] + B[j + 1] * p
-        return c
-    lax.fori_loop(0, 8, some, 0)
-
-
-def ladder(al, lam, fl):
+
+
+def ladder(al, fl):
     return pl.pallas_call(
         ladder_kernel, grid=(1,), out_shape=jax.ShapeDtypeStruct((NPY, 136, 128), F32),
-        in_specs=[fixed((NPY, 128, 128)), fixed((64, 128)), fixed((NPY, 8, 128))],
-        out_specs=fixed((NPY, 136, 128)), compiler_params=params(16), name="ladder",
-    )(al, lam, fl)
-
-
-def y_inverse_kernel(x_ref, pu_ref, lam_ref, tab, edge_f, edge_b, out_ref, sr, st, ph, pl_):
+        in_specs=[fixed((NPY, 128, 128)), fixed((8, N)), fixed((N, 128)), fixed((NPY, 8, 128))],
+        out_specs=fixed((NPY, 136, 128)), compiler_params=params(VMEM_MIB), name="ladder",
+    )(al, jnp.asarray(LAM_X), jnp.asarray(LAM_Y), fl)
+
+
+def y_inverse_kernel(x_ref, pu_ref, lx, ly, tab, edge_f, edge_b, out_ref, tok_ref, sr, st, ph, pl_):
+    tok_ref[...] = jnp.zeros((8, 128), F32)
     sh, sl = edge_rows(x_ref, sr)
+    lam_x = lam_row(lx)
 
     def some(t, c):
         st[...] = edge_modes(edge_f, t, sh, sl)
@@ -494,7 +517,7 @@
             rows = pl.ds(pl.multiple_of(t * 128 + q * 16, 16), 16)
             j, at = 2 * t + q // 4, (q % 4) * 16
             low, top = pu_ref[j, at:at + 16, :], pu_ref[j, 64 + at:80 + at, :]
-            lam = lam_ref[rows, :]
+            lam = ly[rows, :] + lam_x
             cs = [None] * 8
             fs = [None] * 8
             cs[7] = inverse_of(1.0 - lam)
@@ -538,19 +561,19 @@
             out_ref[i + 4, l * ROWS:(l + 1) * ROWS, :] = base[:, cols] - odd[:, cols]
 
 
-def y_inverse(x, pu, lam):
-    return pl.pallas_call(
-        y_inverse_kernel, grid=(1,), out_shape=jax.ShapeDtypeStruct((NPX, BACK, 128), F32),
-        in_specs=[fixed((NPX, BLK, 128)), fixed((NPY, 136, 128)), fixed((N, 128)), fixed((1536, 512)),
+def y_inverse(x, pu):
+    return pl.pallas_call(
+        y_inverse_kernel, grid=(1,), out_shape=(jax.ShapeDtypeStruct((NPX, BACK, 128), F32), TOKEN),
+        in_specs=[fixed((NPX, BLK, 128)), fixed((NPY, 136, 128)), fixed((8, N)), fixed((N, 128)), fixed((1536, 512)),
                   fixed((2 * N, 16)), fixed((32, N))],
-        out_specs=fixed((NPX, BACK, 128)),
+        out_specs=(fixed((NPX, BACK, 128)), fixed((8, 128))),
         scratch_shapes=[pltpu.VMEM((16, N), F32), pltpu.VMEM((128, N), F32),
                         pltpu.VMEM((N, N), BF16), pltpu.VMEM((N, N), BF16)],
-        compiler_params=params(40), name="y_inverse",
-    )(x, pu, lam, jnp.asarray(TAB), jnp.asarray(EDGE_F), jnp.asarray(EDGE_B))
-
-
-def block_inverse_kernel(base_ref, y_ref, g_ref, w_ref, roof_ref, tab, sine, lx, cols, ft, nr, hc,
+        compiler_params=params(VMEM_MIB), name="y_inverse",
+    )(x, pu, jnp.asarray(LAM_X), jnp.asarray(LAM_Y), jnp.asarray(TAB), jnp.asarray(EDGE_F), jnp.asarray(EDGE_B))
+
+
+def block_inverse_kernel(y_ref, g_ref, w_ref, roof_ref, tab, sine, lx, cols, ft, nr, hc, tok,
                          out_ref, nt_ref, field, wv, spu, fb):
     step = pl.program_id(0)
     sh, sl = sine[:128, :], sine[128:, :]
@@ -596,7 +619,7 @@
         for half, res in ((0, s + d), (1, s - d)):
             cs = slice(half * 512, (half + 1) * 512)
             for l in range(2):
-                solid = base_ref[0] + 2 * pair + l < roof_ref[:, cs]
+                solid = lax.axis_index("py") * LEV + 2 * pair + l < roof_ref[:, cs]
                 out_ref[l, :, cs] = jnp.where(solid, 0.0, w_ref[l, :, cs] - res[l * 128:(l + 1) * 128])
 
     @pl.when(step == NPX + 3)
@@ -605,21 +628,21 @@
         nt_ref[...] = ft[...] + (nr[...] - flux - 0.5 * ft[...]) / hc[...]
 
 
-def block_inverse(base, y, g, w, roof, ft, nr, hc):
+def block_inverse(y, g, w, roof, ft, nr, hc, tok):
     late = pl.BlockSpec((2, ROWS, N), lambda t: (jnp.maximum(t - NPX, 0), 0, 0))
     return pl.pallas_call(
         block_inverse_kernel, grid=(NPX + 4,),
         out_shape=(jax.ShapeDtypeStruct((LEV, ROWS, N), F32), jax.ShapeDtypeStruct((32, 128), F32)),
-        in_specs=[SM, pl.BlockSpec((1, BACK, 128), lambda t: (jnp.minimum(t, NPX - 1), 0, 0)),
+        in_specs=[pl.BlockSpec((1, BACK, 128), lambda t: (jnp.minimum(t, NPX - 1), 0, 0)),
                   pl.BlockSpec((LEV, ROWS, 128), lambda t: (0, 0, jnp.minimum(t, NPX - 1))),
                   late, fixed((ROWS, N)), fixed((1536, 512)), fixed((256, 128)),
                   pl.BlockSpec((8, 128), lambda t: (0, jnp.minimum(t, NPX - 1))), fixed((3, ROWS, 128)),
-                  fixed((32, 128)), fixed((32, 128)), fixed((32, 128))],
+                  fixed((32, 128)), fixed((32, 128)), fixed((32, 128)), fixed((8, 128))],
         out_specs=(late, fixed((32, 128))),
         scratch_shapes=[pltpu.VMEM((LEV, ROWS, N), F32), pltpu.VMEM((ROWS, N), F32), pltpu.VMEM((ROWS, 256), F32),
                         pltpu.VMEM((NPX, 8, 128), F32)],
-        compiler_params=params(40), name="block_inverse",
-    )(base, y, g, w, roof, jnp.asarray(TAB_T), jnp.asarray(SINE2), jnp.asarray(LAM_X), jnp.asarray(COLS), ft, nr, hc)
+        compiler_params=params(VMEM_MIB), name="block_inverse",
+    )(y, g, w, roof, jnp.asarray(TAB_T), jnp.asarray(SINE2), jnp.asarray(LAM_X), jnp.asarray(COLS), ft, nr, hc, tok)
 
 
 def swap(x, axes):
@@ -628,7 +651,6 @@
 
 def body(horiz_div, w_star, air_temp, roof_level, facet_cells, facet_temp, net_radiation,
          heat_capacity, drag_coef, heat_coef):
-    ix, iy = lax.axis_index("px"), lax.axis_index("py")
     ft, nr, hc, dr, he, ce = [
         v.reshape(32, 128) for v in (facet_temp, net_radiation, heat_capacity, drag_coef, heat_coef, facet_cells)]
     owner, ids, addr = pack_owner(ft, dr, he, ce)
@@ -636,25 +658,15 @@
     addr = addr.reshape(OWNERS * SLOT)
     w2, a2 = w_star.reshape(1024, 1024), air_temp.reshape(1024, 1024)
     wc = gather_w(addr, ids, w2)
-    w_corr = scatter_w(addr, ids, wc, od, w2)
-    halo = lax.ppermute(w_corr[:ROWS], "py", [(j, j - 1) for j in range(1, NPY)])
-    w_corr = w_corr.reshape(LEV, ROWS, N)
-
-    eig = jnp.asarray(EIGEN.astype(np.float32))
-    eig_x = lax.dynamic_slice_in_dim(eig, ix * 128, 128)
-    eig_y = lax.dynamic_slice_in_dim(eig, iy * 64, 64)
-    lam = eig[:, None] + eig_x[None, :]
-    lam_mine = eig_y[:, None] + eig_x[None, :]
-
-    sent, g = block_solve(block_modes(horiz_div, w_corr), halo)
+    w_corr = scatter_w(addr, ids, wc, od, w2).reshape(LEV, ROWS, N)
+    sent, g, tok = block_forward(horiz_div, w_corr)
     xs = swap(sent, "px")
-    shift = ((iy % 4) * SLOT).astype(jnp.int32).reshape(1)
-    theta, fl = heat_cells(addr, shift, sent, ids, wc, od, a2)
-    al = y_forward(xs, lam)
-    pu = swap(ladder(swap(al, "py"), lam_mine, fl), "py")
-    ys = swap(y_inverse(xs, pu, lam), "px")
-    base = (iy * LEV).astype(jnp.int32).reshape(1)
-    w_new, temp_new = block_inverse(base, ys, g, w_corr, roof_level, ft, nr, hc)
+    flux, fl, tok = heat_flux(addr, tok, ids, wc, od, a2)
+    pu = swap(ladder(swap(y_forward(xs, tok), "py"), fl), "py")
+    back, tok = y_inverse(xs, pu)
+    ys = swap(back, "px")
+    theta, tok = new_theta(addr, tok, ids, flux, a2)
+    w_new, temp_new = block_inverse(ys, g, w_corr, roof_level, ft, nr, hc, tok)
     return w_new, theta.reshape(LEV, ROWS, N), temp_new.reshape(1, OWNERS * SLOT)
 
 

time: 213 us -> 186 us (0.87)
  waiting for transfers between devices: 37.6 us -> 8.94 us
  local copies, waits for them, and re-layouts: 29.5 us -> 2.71 us
  Pallas kernels: 84.6 us -> 107 us
  blocking collectives: 22.3 us -> 42.7 us
  starting transfers between devices: 34.7 us -> 23.2 us
  other arithmetic: 2.22 us -> 0 us
    unnamed x76 -> x6, local copies, waits for them, and re-layouts: 27.4 us -> 2.71 us
    all_to_all x4 -> x3, waiting for transfers between devices: 29.8 us -> 8.94 us  [swap(): return lax.all_to_all(x, axes, split_axis=0, concat_axis=0, tiled=True)]
    all_to_all x1 -> x2, blocking collectives: 22.3 us -> 42.7 us  [swap(): return lax.all_to_all(x, axes, split_axis=0, concat_axis=0, tiled=True)]
    pallas_call x4, Pallas kernels: 39.5 us -> 50.9 us  [the longest x1 18.4 us: block_forward(): pl.pallas_call(block_forward_kernel, grid=(4 + NPX,), out_shape=(jax.Shap...]
    all_to_all x4 -> x3, starting transfers between devices: 33.4 us -> 23.2 us  [swap(): return lax.all_to_all(x, axes, split_axis=0, concat_axis=0, tiled=True)]
    ppermute x1 -> x0, waiting for transfers between devices: 7.81 us -> none  [body(): lax.ppermute(w_corr[:ROWS], 'py', [(j, j - 1) for j in range(1, NPY)])]
    pallas_call x1, Pallas kernels: 11.3 us -> 14.9 us  [scatter_w(): pl.pallas_call(scatter_w_kernel, out_shape=jax.ShapeDtypeStruct((1024, 10...]
    pallas_call x1, Pallas kernels: 3.72 us -> 6.79 us  [y_forward(): pl.pallas_call(y_forward_kernel, grid=(1,), out_shape=jax.ShapeDtypeStruc...]
  transfers between devices with their start and end apart: 5 -> 3, of which waited for: 3 -> 2; matrix products, arithmetic and copies ran while one was open for 2% -> 0% of each run, Pallas kernels for 15% -> 18%
where the time goes in v4:
time: 186 us
  Pallas kernels  107 us (58%)
  blocking collectives  42.7 us (23%)
  starting transfers between devices  23.2 us (12%)
  waiting for transfers between devices  8.94 us (5%)
  local copies, waits for them, and re-layouts  2.71 us (1%)
    all_to_all x2, blocking collectives, swap(): return lax.all_to_all(x, axes, split_axis=0, concat_axis=0, tiled=True)  42.7 us
    all_to_all x3, starting transfers between devices, swap(): return lax.all_to_all(x, axes, split_axis=0, concat_axis=0, tiled=True)  23.2 us
    pallas_call x1, Pallas kernels, block_inverse(): pl.pallas_call(block_inverse_kernel, grid=(NPX + 4,), out_shape=(jax.Shap...  19.4 us
    pallas_call x1, Pallas kernels, block_forward(): pl.pallas_call(block_forward_kernel, grid=(4 + NPX,), out_shape=(jax.Shap...  18.4 us
    pallas_call x1, Pallas kernels, scatter_w(): pl.pallas_call(scatter_w_kernel, out_shape=jax.ShapeDtypeStruct((1024, 10...  14.9 us
    pallas_call x1, Pallas kernels, new_theta(): pl.pallas_call(theta_kernel, out_shape=(jax.ShapeDtypeStruct((1024, 1024)...  13 us
    pallas_call x1, Pallas kernels, gather_w(): pl.pallas_call(gather_kernel, out_shape=jax.ShapeDtypeStruct((OWNERS, 128...  10.7 us
    pallas_call x1, Pallas kernels, heat_flux(): pl.pallas_call(flux_kernel, out_shape=(jax.ShapeDtypeStruct((OWNERS, 128)...  10 us
  transfers between devices with their start and end apart: 3, of which 2 were waited for; matrix products, arithmetic and copies ran while one was open for 0% of the time, Pallas kernels for 18%

profile of v4, /device:TPU:1, one launch (start us, length us, event | category | flops | bytes accessed | tf_op | source)
XLA Modules:
  0.0 185.7 jit_solution(8789470079114977022)
XLA Ops:
  0.6 1.5 pack_owner.1
  2.2 11.5 %all-to-all-start = ((f32[128,1,128]{2,1,0:T(1,128)}), f32[128,1,128]{2,1,0:T(1,128)S(1)}, u32[]{:S(2)}, u32[]{:S(2)}) async-start(f32[128,1,128]{2,1,0:T(1,128)} %bitcast.31), calls=%async_computation | async-start | bytes 131072 | tf_op jit(solution)/shard_map/all_to_all | solution.py:649
  13.7 10.7 %facet_gather.1.wc_ref = f32[128,128]{1,0:T(8,128)} custom-call(s32[4096]{0:T(1024)} %bitcast.25, s32[128,128]{1,0:T(8,128)} %get-tuple-element.19.ids_ref, f32[1024,1024]{1,0:T(8,128)} %bitcast.19), custom_call_target="tpu_custom_call" | custom-call | tf_op jit(solution)/shard_map/facet_gather/pallas_call | solution.py:173
  24.4 0.0 all-to-all-done
  24.4 0.0 copy-start.2
  24.4 0.6 copy-done.2
  25.0 14.9 %scatter_w.1 = f32[1024,1024]{1,0:T(8,128)} custom-call(s32[4096]{0:T(1024)} %bitcast.26, s32[128,128]{1,0:T(8,128)} %get-tuple-element.19.ids_ref, f32[128,128]{1,0:T(8,128)} %facet_gather.1.wc_ref, f32[128,128]{1,0:T(8,128)} %bitcast.23, f32[1024,1024]{1,0:T(8,128)} %bitcast.20), custom_call_target="tpu_custom_call" | custom-call | tf_op jit(solution)/shard_map/scatter_w/pallas_call | solution.py:200
  39.9 18.4 %block_forward.1 = (f32[8,272,128]{2,1,0:T(8,128)}, f32[8,128,1024]{2,1,0:T(8,128)}, f32[8,128]{1,0:T(8,128)}) custom-call(f32[8,128,1024]{2,1,0:T(8,128)} %h_ref.1, f32[8,128,1024]{2,1,0:T(8,128)} %bitcast.16, f32[8,128,1024]{2,1,0:T(8,128)} %bitcast.17, bf16[1536,512]{1,0:T(8,128)(2,1)} %constant.16.clone.tab, bf16[256,128]{1,0:T(8,128)(2,1)} %constant.17.clone.sine, ...), custom_call_target="tpu_custom_call" | custom-call | tf_op jit(solution)/shard_map/block_forward/pallas_call | solution.py:398
  58.3 4.8 %all-to-all-start.1 = ((f32[8,272,128]{2,1,0:T(8,128)}), f32[8,272,128]{2,1,0:T(8,128)S(1)}, u32[]{:S(2)}, u32[]{:S(2)}) async-start(f32[8,272,128]{2,1,0:T(8,128)} %get-tuple-element.21), calls=%async_computation.1 | async-start | bytes 2228224 | tf_op jit(solution)/shard_map/all_to_all | solution.py:649
  63.0 10.0 %heat_flux.1 = (f32[128,128]{1,0:T(8,128)}, f32[16,8,128]{2,1,0:T(8,128)}, f32[8,128]{1,0:T(8,128)}) custom-call(s32[4096]{0:T(1024)} %bitcast.27, f32[8,128]{1,0:T(8,128)} %get-tuple-element.22.tok_in, s32[128,128]{1,0:T(8,128)} %get-tuple-element.19.ids_ref, f32[128,128]{1,0:T(8,128)} %facet_gather.1.wc_ref, f32[128,128]{1,0:T(8,128)} %bitcast.24, ...), custom_call_target="tpu_custom_call" | custom-call | bytes 26214400 | tf_op jit(solution)/shard_map/heat_flux/pallas_call | solution.py:222
  73.1 5.8 %all-to-all-done.1.x_ref = f32[8,272,128]{2,1,0:T(8,128)S(1)} async-done(((f32[8,272,128]{2,1,0:T(8,128)}), f32[8,272,128]{2,1,0:T(8,128)S(1)}, u32[]{:S(2)}, u32[]{:S(2)}) %all-to-all-start.1) | async-done | bytes 1114144 | tf_op jit(solution)/shard_map/all_to_all | solution.py:649
  78.8 0.0 copy-start
  78.8 1.0 copy-done
  79.8 6.8 %y_forward.1 = f32[16,128,128]{2,1,0:T(8,128)} custom-call(f32[8,272,128]{2,1,0:T(8,128)} %copy-done, f32[8,128]{1,0:T(8,128)} %get-tuple-element.23.tok, f32[8,1024]{1,0:T(8,128)} %constant.18.clone.lx, f32[1024,128]{1,0:T(8,128)} %constant.20.clone.ly, bf16[1536,512]{1,0:T(8,128)(2,1)} %constant.21.clone.tab, bf16[2048,16]{1,0:T(8,128)(2,1)} %constant.22.clone.edge.edge_f), custom_call_target="tpu_custom_call" | custom-call | tf_op jit(solution)/shard_map/y_forward/pallas_call | solution.py:460
  86.6 22.9 %all_to_all.25.al_ref = f32[16,128,128]{2,1,0:T(8,128)} all-to-all(f32[16,128,128]{2,1,0:T(8,128)} %y_forward.1), channel_id=1, replica_groups=mesh['px'=8,'py'=16] {'py'}, dimensions={0} | all-to-all | bytes 2097152 | tf_op jit(solution)/shard_map/all_to_all | solution.py:649
  109.6 3.1 %ladder.1 = f32[16,136,128]{2,1,0:T(8,128)} custom-call(f32[16,128,128]{2,1,0:T(8,128)} %all_to_all.25.al_ref, f32[8,1024]{1,0:T(8,128)} %constant.18.clone.lx, f32[1024,128]{1,0:T(8,128)} %constant.20.clone.ly, f32[16,8,128]{2,1,0:T(8,128)} %get-tuple-element.24.fl_ref), custom_call_target="tpu_custom_call" | custom-call | tf_op jit(solution)/shard_map/ladder/pallas_call | solution.py:501
  112.6 19.7 %all_to_all.26.pu_ref = f32[16,136,128]{2,1,0:T(8,128)} all-to-all(f32[16,136,128]{2,1,0:T(8,128)} %ladder.1), channel_id=1, replica_groups=mesh['px'=8,'py'=16] {'py'}, dimensions={0} | all-to-all | bytes 2228224 | tf_op jit(solution)/shard_map/all_to_all | solution.py:649
  132.4 9.6 %y_inverse.1 = (f32[8,280,128]{2,1,0:T(8,128)}, f32[8,128]{1,0:T(8,128)}) custom-call(f32[8,272,128]{2,1,0:T(8,128)} %copy-done, f32[16,136,128]{2,1,0:T(8,128)} %all_to_all.26.pu_ref, f32[8,1024]{1,0:T(8,128)} %constant.18.clone.lx, f32[1024,128]{1,0:T(8,128)} %constant.20.clone.ly, bf16[1536,512]{1,0:T(8,128)(2,1)} %constant.16.clone.tab, ...), custom_call_target="tpu_custom_call" | custom-call | tf_op jit(solution)/shard_map/y_inverse/pallas_call | solution.py:565
  141.9 6.9 %all-to-all-start.4 = ((f32[8,280,128]{2,1,0:T(8,128)}), f32[8,280,128]{2,1,0:T(8,128)S(1)}, u32[]{:S(2)}, u32[]{:S(2)}) async-start(f32[8,280,128]{2,1,0:T(8,128)} %get-tuple-element.25), calls=%async_computation.4 | async-start | bytes 2293760 | tf_op jit(solution)/shard_map/all_to_all | solution.py:649
  148.9 13.0 %new_theta.1 = (bf16[1024,1024]{1,0:T(8,128)(2,1)}, f32[8,128]{1,0:T(8,128)}) custom-call(s32[4096]{0:T(1024)} %bitcast.28, f32[8,128]{1,0:T(8,128)} %get-tuple-element.27.tok_in, s32[128,128]{1,0:T(8,128)} %get-tuple-element.19.ids_ref, f32[128,128]{1,0:T(8,128)} %get-tuple-element.28.flux_ref, bf16[1024,1024]{1,0:T(8,128)(2,1)} %bitcast.22), custom_call_target="tpu_custom_call" | custom-call | bytes 41943040 | tf_op jit(solution)/shard_map/new_theta/pallas_call | solution.py:250
  161.9 3.2 %all-to-all-done.4.y_ref = f32[8,280,128]{2,1,0:T(8,128)S(1)} async-done(((f32[8,280,128]{2,1,0:T(8,128)}), f32[8,280,128]{2,1,0:T(8,128)S(1)}, u32[]{:S(2)}, u32[]{:S(2)}) %all-to-all-start.4) | async-done | bytes 1146912 | tf_op jit(solution)/shard_map/all_to_all | solution.py:649
  165.0 0.0 copy-start.1
  165.0 1.1 copy-done.1
  166.1 19.4 %block_inverse.1 = (f32[8,128,1024]{2,1,0:T(8,128)}, f32[32,128]{1,0:T(8,128)}) custom-call(f32[8,280,128]{2,1,0:T(8,128)} %copy-done.1, f32[8,128,1024]{2,1,0:T(8,128)} %get-tuple-element.26.g_ref, f32[8,128,1024]{2,1,0:T(8,128)} %bitcast.18, s32[128,1024]{1,0:T(8,128)} %roof_ref.1, bf16[1536,512]{1,0:T(8,128)(2,1)} %constant.21.clone.tab, ...), custom_call_target="tpu_custom_call" | custom-call | tf_op jit(solution)/shard_map/block_inverse/pallas_call | solution.py:633
Async XLA Ops:
  2.2 22.2 %all-to-all-start = ((f32[128,1,128]{2,1,0:T(1,128)}), f32[128,1,128]{2,1,0:T(1,128)S(1)}, u32[]{:S(2)}, u32[]{:S(2)}) async-start(f32[128,1,128]{2,1,0:T(1,128)} %bitcast.31), calls=%async_computation | async-start | bytes 131072 | tf_op jit(solution)/shard_map/all_to_all | solution.py:649
  24.4 0.6 copy-start.2
  58.3 20.6 %all-to-all-start.1 = ((f32[8,272,128]{2,1,0:T(8,128)}), f32[8,272,128]{2,1,0:T(8,128)S(1)}, u32[]{:S(2)}, u32[]{:S(2)}) async-start(f32[8,272,128]{2,1,0:T(8,128)} %get-tuple-element.21), calls=%async_computation.1 | async-start | bytes 2228224 | tf_op jit(solution)/shard_map/all_to_all | solution.py:649
  78.8 1.0 copy-start
  141.9 23.1 %all-to-all-start.4 = ((f32[8,280,128]{2,1,0:T(8,128)}), f32[8,280,128]{2,1,0:T(8,128)S(1)}, u32[]{:S(2)}, u32[]{:S(2)}) async-start(f32[8,280,128]{2,1,0:T(8,128)} %get-tuple-element.25), calls=%async_computation.4 | async-start | bytes 2293760 | tf_op jit(solution)/shard_map/all_to_all | solution.py:649
  165.0 1.1 copy-start.1

commit v5 on v4

--- a/solution.py
+++ b/solution.py
@@ -177,31 +177,7 @@
     )(addr, ids, w2)
 
 
-def scatter_w_kernel(addr, ids_ref, wc_ref, od_ref, w_ref, wo_ref, acc0, acc1, acc2, acc3, buf):
-    accs = (acc0, acc1, acc2, acc3)
-    load_w(w_ref, acc0)
-    clear(accs[1:])
-    wc = wc_ref[:, :SLOT]
-    stress = od_ref[:, 32:64] * jnp.sqrt(wc * wc + 0.25) * wc
-    spread_rows(ids_ref[...], -stress, buf)
-    add_rows(addr, accs, buf)
-
-    def put(tr, c):
-        for ct in range(8):
-            wo_ref[tile(tr), ct * 128:(ct + 1) * 128] = total(accs, tile(tr * 8 + ct))
-        return c
-    lax.fori_loop(0, 128, put, 0)
-
-
 FOUR = [pltpu.VMEM((8192, 128), F32)] * 4 + [pltpu.VMEM((4096, 128), F32)]
-
-
-def scatter_w(addr, ids, wc, od, w2):
-    return pl.pallas_call(
-        scatter_w_kernel, out_shape=jax.ShapeDtypeStruct((1024, 1024), F32),
-        in_specs=[SM, VM, VM, VM, VM], out_specs=VM, scratch_shapes=FOUR,
-        compiler_params=params(VMEM_MIB), name="scatter_w",
-    )(addr, ids, wc, od, w2)
 
 
 def flux_kernel(addr, tok_in, ids_ref, wc_ref, od_ref, a_ref, flux_ref, fl_ref, tok_ref, tt, buf, turned):
@@ -259,13 +235,6 @@
 BACK = BLK + 8
 
 
-def z_basis():
-    k, m = np.arange(LEV)[:, None], np.arange(LEV)[None, :]
-    q = math.sqrt(4 / 17) * np.sin(np.pi * (2 * m + 1) * (k + 1) / 17)
-    theta = -4.0 * np.sin(np.pi * (2 * np.arange(LEV) + 1) / 34) ** 2
-    return q, theta
-
-
 def y_basis():
     i = np.arange(ROWS) + 1
     s = math.sqrt(2 / 129) * np.sin(np.pi * (np.outer(i, i) % 258) / 129)
@@ -273,8 +242,6 @@
     return s, mu
 
 
-Q, THETA = z_basis()
-DQ = Q - np.concatenate([np.zeros((1, LEV)), Q[:-1]])
 SINE, MU = y_basis()
 EDGE = np.concatenate([TABLE[0::ROWS], TABLE[ROWS - 1::ROWS]])
 
@@ -291,20 +258,23 @@
 EDGE_B = np.concatenate(split_np(EDGE))
 LAM_Y = np.broadcast_to(EIGEN.astype(np.float32)[:, None], (N, 128)).copy()
 LAM_X = np.broadcast_to(EIGEN.astype(np.float32), (8, N)).copy()
-COLS = np.stack([np.broadcast_to(v[:, None], (ROWS, 128)) for v in (MU, SINE[:, 0], SINE[:, 127])]).astype(np.float32)
+COLS = np.stack([np.broadcast_to(v[:, None], (ROWS, 128)) for v in (SINE[:, 0], SINE[:, 127])]).astype(np.float32)
+
+
+def pivots():
+    lam = MU[:, None] + EIGEN[None, :]
+    c = [1.0 / (1.0 - lam)]
+    for _ in range(LEV - 1):
+        c.insert(0, 1.0 / (2.0 - lam - c[0]))
+    return np.stack(c).astype(np.float32)
+
+
+PIVOT = pivots()
 
 
 def tab_parts(t):
     return ((t[1024:1280, :256], t[1280:1536, :256]), (t[1024:1280, 256:], t[1280:1536, 256:]),
             (t[:512], t[512:1024]))
-
-
-def combine(coefs, vs):
-    out = None
-    for c, v in zip(coefs, vs):
-        t = float(c) * v
-        out = t if out is None else out + t
-    return out
 
 
 def tile(i, size=8):
@@ -342,71 +312,103 @@
             (512, dot3(*split(d), *td)))
 
 
-def block_forward_kernel(h_ref, w_ref, wn_ref, tab, sine, lx, cols, out_ref, g_ref, tok_ref, r2, hx, a07):
+STRIP = 32
+
+
+def fold(v):
+    return jnp.sum(v.reshape(STRIP // 8, 8, 128), axis=0)
+
+
+def eliminate(fs, cs):
+    fs = list(fs)
+    for k in range(LEV - 2, -1, -1):
+        fs[k] = fs[k] + cs[k + 1] * fs[k + 1]
+    ps = [cs[0] * fs[0]]
+    for k in range(1, LEV):
+        ps.append(cs[k] * (fs[k] + ps[k - 1]))
+    return ps
+
+
+def block_forward_kernel(addr, ids_ref, wc_ref, od_ref, w_ref, h_ref, tab, sine, piv, cols,
+                         wo_ref, out_ref, r_ref, tok_ref,
+                         acc0, acc1, acc2, acc3, buf, wf, r2, hx, a07):
     step = pl.program_id(0)
     sh, sl = sine[:128, :], sine[128:, :]
 
     @pl.when(step == 0)
     def _():
         tok_ref[...] = jnp.zeros((8, 128), F32)
+        accs = (acc0, acc1, acc2, acc3)
+        load_w(w_ref, acc0)
+        clear(accs[1:])
+        wc = wc_ref[:, :SLOT]
+        stress = od_ref[:, 32:64] * jnp.sqrt(wc * wc + 0.25) * wc
+        spread_rows(ids_ref[...], -stress, buf)
+        add_rows(addr, accs, buf)
+
+        def put(tr, c):
+            for ct in range(8):
+                wf[tr // 16, tile(tr % 16), ct * 128:(ct + 1) * 128] = total(accs, tile(tr * 8 + ct))
+            return c
+        lax.fori_loop(0, 128, put, 0)
         lifted = (lax.axis_index("py") > 0).astype(F32)
-        for c0, res in x_modes(w_ref[0] * lifted, tab):
+        for c0, res in x_modes(wf[0] * lifted, tab):
             for b in range(res.shape[1] // 128):
                 hx[c0 // 128 + b] = res[:, b * 128:(b + 1) * 128]
 
-    @pl.when(step < 4)
+    @pl.when((step > 0) & (step < 5))
     def _():
-        up = jnp.where(step == 3, 0.0, wn_ref[0])
-        r = jnp.concatenate([h_ref[0] + w_ref[1] - w_ref[0], h_ref[1] + up - w_ref[1]], axis=0)
+        lv = 2 * step - 2
+        w0, w1 = wf[lv], wf[lv + 1]
+        wo_ref[0] = w0
+        wo_ref[1] = w1
+        up = jnp.where(step == 4, 0.0, wf[jnp.minimum(lv + 2, LEV - 1)])
+        r = jnp.concatenate([h_ref[0] + w1 - w0, h_ref[1] + up - w1], axis=0)
         for c0, res in x_modes(r, tab):
             for l in range(2):
                 v = dot3(sh, sl, *split(res[l * 128:(l + 1) * 128]))
                 for b in range(res.shape[1] // 128):
-                    r2[c0 // 128 + b, 2 * step + l] = v[:, b * 128:(b + 1) * 128]
-
-    @pl.when(step >= 4)
+                    r2[c0 // 128 + b, lv + l] = v[:, b * 128:(b + 1) * 128]
+
+    @pl.when(step >= 5)
     def _():
-        lt = step - 4
-        lam = lx[...]
+        lt = step - 5
 
         def inner(bt, acc):
-            rows = tile(bt)
+            rows = tile(bt, STRIP)
             rs = [r2[lt, k, rows, :] for k in range(LEV)]
-            mu, s0, s1 = cols[0, rows, :], cols[1, rows, :], cols[2, rows, :]
-            base = lam + mu
-            ps = []
-            for m in range(LEV):
-                p = combine(Q[:, m], rs) * inverse_of(base + float(THETA[m]))
-                g_ref[m, rows, :] = p
-                ps.append(p)
-            a07[rows, :128] = combine(Q[0], ps)
-            a07[rows, 128:] = combine(Q[7], ps)
-            return tuple(acc[m] + s0 * ps[m] for m in range(LEV)) + tuple(
-                acc[LEV + m] + s1 * ps[m] for m in range(LEV))
-        acc = lax.fori_loop(0, ROWS // 8, inner, tuple(jnp.zeros((8, 128), F32) for _ in range(16)))
+            for k in range(LEV):
+                r_ref[k, rows, :] = rs[k]
+            ps = eliminate(rs, [piv[k, rows, :] for k in range(LEV)])
+            s0, s1 = cols[0, rows, :], cols[1, rows, :]
+            a07[rows, :128] = ps[0]
+            a07[rows, 128:] = ps[7]
+            return tuple(acc[k] + fold(s0 * ps[k]) for k in range(LEV)) + tuple(
+                acc[LEV + k] + fold(s1 * ps[k]) for k in range(LEV))
+        acc = lax.fori_loop(0, ROWS // STRIP, inner, tuple(jnp.zeros((8, 128), F32) for _ in range(16)))
         for e in range(2):
-            sums = [jnp.sum(acc[e * LEV + m], axis=0, keepdims=True) for m in range(LEV)]
-            out_ref[0, 2 * ROWS + e * LEV:2 * ROWS + (e + 1) * LEV, :] = jnp.concatenate(
-                [combine(Q[k], sums) for k in range(LEV)], axis=0)
+            sums = [jnp.sum(acc[e * LEV + k], axis=0, keepdims=True) for k in range(LEV)]
+            out_ref[0, 2 * ROWS + e * LEV:2 * ROWS + (e + 1) * LEV, :] = -jnp.concatenate(sums, axis=0)
         res = dot3(sh, sl, *split(a07[...]))
-        out_ref[0, :ROWS, :] = res[:, :128] - hx[lt]
-        out_ref[0, ROWS:2 * ROWS, :] = res[:, 128:]
-
-
-def block_forward(h, w):
-    two = pl.BlockSpec((2, ROWS, N), lambda g: (jnp.minimum(g, 3), 0, 0))
-    return pl.pallas_call(
-        block_forward_kernel, grid=(4 + NPX,),
-        out_shape=(jax.ShapeDtypeStruct((NPX, BLK, 128), F32), jax.ShapeDtypeStruct((LEV, ROWS, N), F32), TOKEN),
-        in_specs=[two, two, pl.BlockSpec((1, ROWS, N), lambda g: (jnp.minimum(2 * g + 2, 7), 0, 0)),
-                  fixed((1536, 512)), fixed((256, 128)),
-                  pl.BlockSpec((8, 128), lambda g: (0, jnp.maximum(g - 4, 0))), fixed((3, ROWS, 128))],
-        out_specs=(pl.BlockSpec((1, BLK, 128), lambda g: (jnp.maximum(g - 4, 0), 0, 0)),
-                   pl.BlockSpec((LEV, ROWS, 128), lambda g: (0, 0, jnp.maximum(g - 4, 0))), fixed((8, 128))),
-        scratch_shapes=[pltpu.VMEM((NPX, LEV, ROWS, 128), F32), pltpu.VMEM((NPX, ROWS, 128), F32),
-                        pltpu.VMEM((ROWS, 256), F32)],
+        out_ref[0, :ROWS, :] = -res[:, :128] - hx[lt]
+        out_ref[0, ROWS:2 * ROWS, :] = -res[:, 128:]
+
+
+def block_forward(addr, ids, wc, od, w2, h):
+    two = pl.BlockSpec((2, ROWS, N), lambda g: (jnp.clip(g - 1, 0, 3), 0, 0))
+    col = pl.BlockSpec((LEV, ROWS, 128), lambda g: (0, 0, jnp.maximum(g - 5, 0)))
+    small = fixed((OWNERS, 128))
+    big = jax.ShapeDtypeStruct((LEV, ROWS, N), F32)
+    return pl.pallas_call(
+        block_forward_kernel, grid=(5 + NPX,),
+        out_shape=(big, jax.ShapeDtypeStruct((NPX, BLK, 128), F32), big, TOKEN),
+        in_specs=[SM, small, small, small, pl.BlockSpec((N, N), lambda g: (0, 0)), two, fixed((1536, 512)),
+                  fixed((256, 128)), col, fixed((2, ROWS, 128))],
+        out_specs=(two, pl.BlockSpec((1, BLK, 128), lambda g: (jnp.maximum(g - 5, 0), 0, 0)), col, fixed((8, 128))),
+        scratch_shapes=FOUR + [pltpu.VMEM((LEV, ROWS, N), F32), pltpu.VMEM((NPX, LEV, ROWS, 128), F32),
+                               pltpu.VMEM((NPX, ROWS, 128), F32), pltpu.VMEM((ROWS, 256), F32)],
         compiler_params=params(VMEM_MIB), name="block_forward",
-    )(h, w, w, jnp.asarray(TAB), jnp.asarray(SINE2), jnp.asarray(LAM_X), jnp.asarray(COLS))
+    )(addr, ids, wc, od, w2, h, jnp.asarray(TAB), jnp.asarray(SINE2), jnp.asarray(PIVOT), jnp.asarray(COLS))
 
 
 def lam_row(lx):
@@ -573,7 +575,7 @@
     )(x, pu, jnp.asarray(LAM_X), jnp.asarray(LAM_Y), jnp.asarray(TAB), jnp.asarray(EDGE_F), jnp.asarray(EDGE_B))
 
 
-def block_inverse_kernel(y_ref, g_ref, w_ref, roof_ref, tab, sine, lx, cols, ft, nr, hc, tok,
+def block_inverse_kernel(y_ref, g_ref, w_ref, roof_ref, tab, sine, piv, cols, ft, nr, hc, tok,
                          out_ref, nt_ref, field, wv, spu, fb):
     step = pl.program_id(0)
     sh, sl = sine[:128, :], sine[128:, :]
@@ -582,27 +584,21 @@
     def _():
         fb[step] = y_ref[0, BLK:, :]
         spu[...] = dot3(sh, sl, *split(jnp.concatenate([y_ref[0, :ROWS, :], y_ref[0, ROWS:2 * ROWS, :]], axis=1)))
-        lam = lx[...]
-        ql, qh = [], []
-        for e, dst in ((0, ql), (1, qh)):
-            rows = [y_ref[0, 2 * ROWS + e * LEV + k:2 * ROWS + e * LEV + k + 1, :] for k in range(LEV)]
-            for m in range(LEV):
-                dst.append(jnp.broadcast_to(combine(Q[:, m], rows), (8, 128)))
+        edge = [y_ref[0, 2 * ROWS + k:2 * ROWS + k + 1, :] for k in range(2 * LEV)]
 
         def inner(bt, c):
-            rows = tile(bt)
-            mu, s0, s1 = cols[0, rows, :], cols[1, rows, :], cols[2, rows, :]
-            base = lam + mu
+            rows = tile(bt, STRIP)
+            s0, s1 = cols[0, rows, :], cols[1, rows, :]
             low, top = spu[rows, :128], spu[rows, 128:]
-            ps = []
-            for m in range(LEV):
-                f = (float(Q[0, m]) * low + float(Q[7, m]) * top) + (s0 * ql[m] + s1 * qh[m])
-                ps.append(g_ref[m, rows, :] - f * inverse_of(base + float(THETA[m])))
-            for k in range(LEV):
-                v = combine(DQ[k], ps)
-                wv[rows, k * 128:(k + 1) * 128] = v - low if k == 0 else v
+            fs = [s0 * edge[k] + s1 * edge[LEV + k] - g_ref[k, rows, :] for k in range(LEV)]
+            fs[0] = fs[0] + low
+            fs[7] = fs[7] + top
+            prev = low
+            for k, p in enumerate(eliminate(fs, [piv[k, rows, :] for k in range(LEV)])):
+                wv[rows, k * 128:(k + 1) * 128] = p - prev
+                prev = p
             return c
-        lax.fori_loop(0, ROWS // 8, inner, 0)
+        lax.fori_loop(0, ROWS // STRIP, inner, 0)
         res = dot3(sh, sl, *split(wv[...]))
         for k in range(LEV):
             field[k, :, tile(step, 128)] = res[:, k * 128:(k + 1) * 128]
@@ -636,13 +632,13 @@
         in_specs=[pl.BlockSpec((1, BACK, 128), lambda t: (jnp.minimum(t, NPX - 1), 0, 0)),
                   pl.BlockSpec((LEV, ROWS, 128), lambda t: (0, 0, jnp.minimum(t, NPX - 1))),
                   late, fixed((ROWS, N)), fixed((1536, 512)), fixed((256, 128)),
-                  pl.BlockSpec((8, 128), lambda t: (0, jnp.minimum(t, NPX - 1))), fixed((3, ROWS, 128)),
+                  pl.BlockSpec((LEV, ROWS, 128), lambda t: (0, 0, jnp.minimum(t, NPX - 1))), fixed((2, ROWS, 128)),
                   fixed((32, 128)), fixed((32, 128)), fixed((32, 128)), fixed((8, 128))],
         out_specs=(late, fixed((32, 128))),
         scratch_shapes=[pltpu.VMEM((LEV, ROWS, N), F32), pltpu.VMEM((ROWS, N), F32), pltpu.VMEM((ROWS, 256), F32),
                         pltpu.VMEM((NPX, 8, 128), F32)],
         compiler_params=params(VMEM_MIB), name="block_inverse",
-    )(y, g, w, roof, jnp.asarray(TAB_T), jnp.asarray(SINE2), jnp.asarray(LAM_X), jnp.asarray(COLS), ft, nr, hc, tok)
+    )(y, g, w, roof, jnp.asarray(TAB_T), jnp.asarray(SINE2), jnp.asarray(PIVOT), jnp.asarray(COLS), ft, nr, hc, tok)
 
 
 def swap(x, axes):
@@ -658,8 +654,7 @@
     addr = addr.reshape(OWNERS * SLOT)
     w2, a2 = w_star.reshape(1024, 1024), air_temp.reshape(1024, 1024)
     wc = gather_w(addr, ids, w2)
-    w_corr = scatter_w(addr, ids, wc, od, w2).reshape(LEV, ROWS, N)
-    sent, g, tok = block_forward(horiz_div, w_corr)
+    w_corr, sent, g, tok = block_forward(addr, ids, wc, od, w2, horiz_div)
     xs = swap(sent, "px")
     flux, fl, tok = heat_flux(addr, tok, ids, wc, od, a2)
     pu = swap(ladder(swap(y_forward(xs, tok), "py"), fl), "py")

time: 186 us -> 179 us (0.962)
  Pallas kernels: 107 us -> 99.7 us
    pallas_call x2 -> x1, Pallas kernels: 33.3 us -> 28.5 us  [block_forward(): pl.pallas_call(block_forward_kernel, grid=(5 + NPX,), out_shape=(big, jax...]
    pallas_call x1, Pallas kernels: 19.4 us -> 16.7 us  [block_inverse(): pl.pallas_call(block_inverse_kernel, grid=(NPX + 4,), out_shape=(jax.Shap...]
  transfers between devices with their start and end apart: 3 -> 3, of which waited for: 2 -> 2; matrix products, arithmetic and copies ran while one was open for 0% -> 0% of each run, Pallas kernels for 18% -> 19%
where the time goes in v5:
time: 179 us; the launch traced here: 178 us
  Pallas kernels  99.7 us (56%)
  blocking collectives  42.7 us (24%)
  starting transfers between devices  23.3 us (13%)
  waiting for transfers between devices  9.09 us (5%)
  local copies, waits for them, and re-layouts  2.71 us (2%)
    all_to_all x2, blocking collectives, swap(): return lax.all_to_all(x, axes, split_axis=0, concat_axis=0, tiled=True)  42.7 us
    pallas_call x1, Pallas kernels, block_forward(): pl.pallas_call(block_forward_kernel, grid=(5 + NPX,), out_shape=(big, jax...  28.5 us
    all_to_all x3, starting transfers between devices, swap(): return lax.all_to_all(x, axes, split_axis=0, concat_axis=0, tiled=True)  23.3 us
    pallas_call x1, Pallas kernels, block_inverse(): pl.pallas_call(block_inverse_kernel, grid=(NPX + 4,), out_shape=(jax.Shap...  16.7 us
    pallas_call x1, Pallas kernels, new_theta(): pl.pallas_call(theta_kernel, out_shape=(jax.ShapeDtypeStruct((1024, 1024)...  12.9 us
    pallas_call x1, Pallas kernels, gather_w(): pl.pallas_call(gather_kernel, out_shape=jax.ShapeDtypeStruct((OWNERS, 128...  10.7 us
    pallas_call x1, Pallas kernels, heat_flux(): pl.pallas_call(flux_kernel, out_shape=(jax.ShapeDtypeStruct((OWNERS, 128)...  10 us
    pallas_call x1, Pallas kernels, y_inverse(): pl.pallas_call(y_inverse_kernel, grid=(1,), out_shape=(jax.ShapeDtypeStru...  9.56 us
  transfers between devices with their start and end apart: 3, of which 2 were waited for; matrix products, arithmetic and copies ran while one was open for 0% of the time, Pallas kernels for 19%

profile of v5, /device:TPU:1, one launch (start us, length us, event | category | flops | bytes accessed | tf_op | source)
XLA Modules:
  0.0 178.3 jit_solution(10137009851460361860)
XLA Ops:
  0.6 1.5 pack_owner.1
  2.2 11.5 %all-to-all-start = ((f32[128,1,128]{2,1,0:T(1,128)}), f32[128,1,128]{2,1,0:T(1,128)S(1)}, u32[]{:S(2)}, u32[]{:S(2)}) async-start(f32[128,1,128]{2,1,0:T(1,128)} %bitcast.25), calls=%async_computation | async-start | bytes 131072 | tf_op jit(solution)/shard_map/all_to_all | solution.py:645
  13.7 10.7 %facet_gather.1.wc_ref = f32[128,128]{1,0:T(8,128)} custom-call(s32[4096]{0:T(1024)} %bitcast.21, s32[128,128]{1,0:T(8,128)} %get-tuple-element.20.ids_ref, f32[1024,1024]{1,0:T(8,128)} %bitcast.15), custom_call_target="tpu_custom_call" | custom-call | tf_op jit(solution)/shard_map/facet_gather/pallas_call | solution.py:173
  24.4 0.0 all-to-all-done
  24.4 0.0 copy-start.2
  24.4 0.6 copy-done.2
  25.0 28.5 %block_forward.1 = (f32[8,128,1024]{2,1,0:T(8,128)}, f32[8,272,128]{2,1,0:T(8,128)}, f32[8,128,1024]{2,1,0:T(8,128)}, f32[8,128]{1,0:T(8,128)}) custom-call(s32[4096]{0:T(1024)} %bitcast.22, s32[128,128]{1,0:T(8,128)} %get-tuple-element.20.ids_ref, f32[128,128]{1,0:T(8,128)} %facet_gather.1.wc_ref, f32[128,128]{1,0:T(8,128)} %bitcast.19, ...), custom_call_target="tpu_custom_call" | custom-call | tf_op jit(solution)/shard_map/block_forward/pallas_call | solution.py:402
  53.6 4.9 %all-to-all-start.1 = ((f32[8,272,128]{2,1,0:T(8,128)}), f32[8,272,128]{2,1,0:T(8,128)S(1)}, u32[]{:S(2)}, u32[]{:S(2)}) async-start(f32[8,272,128]{2,1,0:T(8,128)} %get-tuple-element.22), calls=%async_computation.1 | async-start | bytes 2228224 | tf_op jit(solution)/shard_map/all_to_all | solution.py:645
  58.5 10.0 %heat_flux.1 = (f32[128,128]{1,0:T(8,128)}, f32[16,8,128]{2,1,0:T(8,128)}, f32[8,128]{1,0:T(8,128)}) custom-call(s32[4096]{0:T(1024)} %bitcast.23, f32[8,128]{1,0:T(8,128)} %get-tuple-element.23.tok_in, s32[128,128]{1,0:T(8,128)} %get-tuple-element.20.ids_ref, f32[128,128]{1,0:T(8,128)} %facet_gather.1.wc_ref, f32[128,128]{1,0:T(8,128)} %bitcast.20, ...), custom_call_target="tpu_custom_call" | custom-call | bytes 26214400 | tf_op jit(solution)/shard_map/heat_flux/pallas_call | solution.py:198
  68.5 5.8 %all-to-all-done.1.x_ref = f32[8,272,128]{2,1,0:T(8,128)S(1)} async-done(((f32[8,272,128]{2,1,0:T(8,128)}), f32[8,272,128]{2,1,0:T(8,128)S(1)}, u32[]{:S(2)}, u32[]{:S(2)}) %all-to-all-start.1) | async-done | bytes 1114144 | tf_op jit(solution)/shard_map/all_to_all | solution.py:645
  74.3 0.0 copy-start
  74.3 1.0 copy-done
  75.2 6.8 %y_forward.1 = f32[16,128,128]{2,1,0:T(8,128)} custom-call(f32[8,272,128]{2,1,0:T(8,128)} %copy-done, f32[8,128]{1,0:T(8,128)} %get-tuple-element.24.tok, f32[8,1024]{1,0:T(8,128)} %constant.22.clone.lx, f32[1024,128]{1,0:T(8,128)} %constant.23.clone.ly, bf16[1536,512]{1,0:T(8,128)(2,1)} %constant.24.clone.tab, bf16[2048,16]{1,0:T(8,128)(2,1)} %constant.25.clone.edge.edge_f), custom_call_target="tpu_custom_call" | custom-call | tf_op jit(solution)/shard_map/y_forward/pallas_call | solution.py:462
  82.0 22.9 %all_to_all.25.al_ref = f32[16,128,128]{2,1,0:T(8,128)} all-to-all(f32[16,128,128]{2,1,0:T(8,128)} %y_forward.1), channel_id=1, replica_groups=mesh['px'=8,'py'=16] {'py'}, dimensions={0} | all-to-all | bytes 2097152 | tf_op jit(solution)/shard_map/all_to_all | solution.py:645
  104.9 3.1 %ladder.1 = f32[16,136,128]{2,1,0:T(8,128)} custom-call(f32[16,128,128]{2,1,0:T(8,128)} %all_to_all.25.al_ref, f32[8,1024]{1,0:T(8,128)} %constant.22.clone.lx, f32[1024,128]{1,0:T(8,128)} %constant.23.clone.ly, f32[16,8,128]{2,1,0:T(8,128)} %get-tuple-element.25.fl_ref), custom_call_target="tpu_custom_call" | custom-call | tf_op jit(solution)/shard_map/ladder/pallas_call | solution.py:503
  108.0 19.8 %all_to_all.26.pu_ref = f32[16,136,128]{2,1,0:T(8,128)} all-to-all(f32[16,136,128]{2,1,0:T(8,128)} %ladder.1), channel_id=1, replica_groups=mesh['px'=8,'py'=16] {'py'}, dimensions={0} | all-to-all | bytes 2228224 | tf_op jit(solution)/shard_map/all_to_all | solution.py:645
  127.8 9.6 %y_inverse.1 = (f32[8,280,128]{2,1,0:T(8,128)}, f32[8,128]{1,0:T(8,128)}) custom-call(f32[8,272,128]{2,1,0:T(8,128)} %copy-done, f32[16,136,128]{2,1,0:T(8,128)} %all_to_all.26.pu_ref, f32[8,1024]{1,0:T(8,128)} %constant.22.clone.lx, f32[1024,128]{1,0:T(8,128)} %constant.23.clone.ly, bf16[1536,512]{1,0:T(8,128)(2,1)} %constant.18.clone.tab, ...), custom_call_target="tpu_custom_call" | custom-call | tf_op jit(solution)/shard_map/y_inverse/pallas_call | solution.py:567
  137.3 6.9 %all-to-all-start.4 = ((f32[8,280,128]{2,1,0:T(8,128)}), f32[8,280,128]{2,1,0:T(8,128)S(1)}, u32[]{:S(2)}, u32[]{:S(2)}) async-start(f32[8,280,128]{2,1,0:T(8,128)} %get-tuple-element.26), calls=%async_computation.4 | async-start | bytes 2293760 | tf_op jit(solution)/shard_map/all_to_all | solution.py:645
  144.3 12.9 %new_theta.1 = (bf16[1024,1024]{1,0:T(8,128)(2,1)}, f32[8,128]{1,0:T(8,128)}) custom-call(s32[4096]{0:T(1024)} %bitcast.24, f32[8,128]{1,0:T(8,128)} %get-tuple-element.29.tok_in, s32[128,128]{1,0:T(8,128)} %get-tuple-element.20.ids_ref, f32[128,128]{1,0:T(8,128)} %get-tuple-element.30.flux_ref, bf16[1024,1024]{1,0:T(8,128)(2,1)} %bitcast.18), custom_call_target="tpu_custom_call" | custom-call | bytes 41943040 | tf_op jit(solution)/shard_map/new_theta/pallas_call | solution.py:226
  157.1 3.3 %all-to-all-done.4.y_ref = f32[8,280,128]{2,1,0:T(8,128)S(1)} async-done(((f32[8,280,128]{2,1,0:T(8,128)}), f32[8,280,128]{2,1,0:T(8,128)S(1)}, u32[]{:S(2)}, u32[]{:S(2)}) %all-to-all-start.4) | async-done | bytes 1146912 | tf_op jit(solution)/shard_map/all_to_all | solution.py:645
  160.4 0.0 copy-start.1
  160.4 1.1 copy-done.1
  161.5 16.7 %block_inverse.1 = (f32[8,128,1024]{2,1,0:T(8,128)}, f32[32,128]{1,0:T(8,128)}) custom-call(f32[8,280,128]{2,1,0:T(8,128)} %copy-done.1, f32[8,128,1024]{2,1,0:T(8,128)} %get-tuple-element.27.g_ref, f32[8,128,1024]{2,1,0:T(8,128)} %get-tuple-element.28.w_ref, s32[128,1024]{1,0:T(8,128)} %roof_ref.1, bf16[1536,512]{1,0:T(8,128)(2,1)} %constant.24.clone.tab, ...), custom_call_target="tpu_custom_call" | custom-call | tf_op jit(solution)/shard_map/block_inverse/pallas_call | solution.py:629
Async XLA Ops:
  2.2 22.2 %all-to-all-start = ((f32[128,1,128]{2,1,0:T(1,128)}), f32[128,1,128]{2,1,0:T(1,128)S(1)}, u32[]{:S(2)}, u32[]{:S(2)}) async-start(f32[128,1,128]{2,1,0:T(1,128)} %bitcast.25), calls=%async_computation | async-start | bytes 131072 | tf_op jit(solution)/shard_map/all_to_all | solution.py:645
  24.4 0.6 copy-start.2
  53.6 20.7 %all-to-all-start.1 = ((f32[8,272,128]{2,1,0:T(8,128)}), f32[8,272,128]{2,1,0:T(8,128)S(1)}, u32[]{:S(2)}, u32[]{:S(2)}) async-start(f32[8,272,128]{2,1,0:T(8,128)} %get-tuple-element.22), calls=%async_computation.1 | async-start | bytes 2228224 | tf_op jit(solution)/shard_map/all_to_all | solution.py:645
  74.3 1.0 copy-start
  137.3 23.1 %all-to-all-start.4 = ((f32[8,280,128]{2,1,0:T(8,128)}), f32[8,280,128]{2,1,0:T(8,128)S(1)}, u32[]{:S(2)}, u32[]{:S(2)}) async-start(f32[8,280,128]{2,1,0:T(8,128)} %get-tuple-element.26), calls=%async_computation.4 | async-start | bytes 2293760 | tf_op jit(solution)/shard_map/all_to_all | solution.py:645
  160.4 1.1 copy-start.1

commit v6 on v5

--- a/solution.py
+++ b/solution.py
@@ -14,7 +14,7 @@
 LEV, ROWS = 8, 128
 OWNERS, SLOT = 128, 32
 MIB = 1 << 20
-VMEM_MIB = 58
+VMEM_MIB = 50
 F32, BF16 = jnp.float32, jnp.bfloat16
 
 
@@ -87,16 +87,8 @@
     return pl.pallas_call(
         pack_kernel, out_shape=(full, jax.ShapeDtypeStruct((OWNERS, 128), jnp.int32),
                                 jax.ShapeDtypeStruct((32, 128), jnp.int32)),
-        in_specs=[VM] * 4, out_specs=(VM,) * 3, compiler_params=params(VMEM_MIB), name="pack_owner",
+        in_specs=[VM] * 4, out_specs=(VM,) * 3, compiler_params=params(58), name="pack_owner",
     )(ft, dr, he, ce)
-
-
-def load_w(w_ref, wt):
-    def one(tr, c):
-        for ct in range(8):
-            wt[tile(tr * 8 + ct), :] = w_ref[tile(tr), ct * 128:(ct + 1) * 128]
-        return c
-    lax.fori_loop(0, 128, one, 0)
 
 
 def load_temp(a_ref, tt):
@@ -150,11 +142,15 @@
     width = len(accs)
 
     def one(o, c):
-        for s in range(0, SLOT, width):
-            at = [addr[o * SLOT + s + j] for j in range(width)]
-            new = [accs[j][pl.ds(at[j], 1), :] + buf[pl.ds((s + j) * OWNERS + o, 1), :] for j in range(width)]
+        for s in range(0, SLOT, 2 * width):
+            at = [addr[o * SLOT + s + j] for j in range(2 * width)]
+            x = [buf[pl.ds((s + j) * OWNERS + o, 1), :] for j in range(2 * width)]
+            old = [accs[j % width][pl.ds(at[j], 1), :] for j in range(2 * width)]
             for j in range(width):
-                accs[j][pl.ds(at[j], 1), :] = new[j]
+                first = old[j] + x[j]
+                second = jnp.where(at[j] == at[j + width], first, old[j + width]) + x[j + width]
+                accs[j][pl.ds(at[j], 1), :] = first
+                accs[j][pl.ds(at[j + width], 1), :] = second
         return c
     lax.fori_loop(0, OWNERS, one, 0)
 
@@ -163,16 +159,15 @@
     return (accs[0][rows, :] + accs[1][rows, :]) + (accs[2][rows, :] + accs[3][rows, :])
 
 
-def gather_kernel(addr, ids_ref, w_ref, wc_ref, wt, buf):
-    load_w(w_ref, wt)
-    gather_rows(addr, wt, buf)
+def gather_kernel(addr, ids_ref, w_ref, wc_ref, buf):
+    gather_rows(addr, w_ref, buf)
     wc_ref[...] = pick(ids_ref[...], buf)
 
 
 def gather_w(addr, ids, w2):
     return pl.pallas_call(
         gather_kernel, out_shape=jax.ShapeDtypeStruct((OWNERS, 128), F32), in_specs=[SM, VM, VM], out_specs=VM,
-        scratch_shapes=[pltpu.VMEM((8192, 128), F32), pltpu.VMEM((4096, 128), F32)],
+        scratch_shapes=[pltpu.VMEM((4096, 128), F32)],
         compiler_params=params(VMEM_MIB), name="facet_gather",
     )(addr, ids, w2)
 
@@ -201,7 +196,7 @@
         in_specs=[SM] + [VM] * 5, out_specs=(VM,) * 3,
         scratch_shapes=[pltpu.VMEM((8192, 128), F32), pltpu.VMEM((4096, 128), F32), pltpu.VMEM((OWNERS, 128), F32)],
         cost_estimate=pl.CostEstimate(flops=0, bytes_accessed=25 * MIB, transcendentals=0),
-        compiler_params=params(VMEM_MIB), name="heat_flux",
+        compiler_params=params(30), name="heat_flux",
     )(addr, tok, ids, wc, od, a2)
 
 
@@ -227,7 +222,7 @@
         theta_kernel, out_shape=(jax.ShapeDtypeStruct((1024, 1024), BF16), TOKEN),
         in_specs=[SM] + [VM] * 4, out_specs=(VM, VM), scratch_shapes=FOUR,
         cost_estimate=pl.CostEstimate(flops=0, bytes_accessed=40 * MIB, transcendentals=0),
-        compiler_params=params(VMEM_MIB), name="new_theta",
+        compiler_params=params(42), name="new_theta",
     )(addr, tok, ids, flux, a2)
 
 
@@ -257,7 +252,7 @@
 EDGE_F = np.concatenate(split_np(EDGE.T))
 EDGE_B = np.concatenate(split_np(EDGE))
 LAM_Y = np.broadcast_to(EIGEN.astype(np.float32)[:, None], (N, 128)).copy()
-LAM_X = np.broadcast_to(EIGEN.astype(np.float32), (8, N)).copy()
+LAMS = np.concatenate([LAM_Y, EIGEN.astype(np.float32).reshape(NPX, 128)])
 COLS = np.stack([np.broadcast_to(v[:, None], (ROWS, 128)) for v in (SINE[:, 0], SINE[:, 127])]).astype(np.float32)
 
 
@@ -329,28 +324,31 @@
     return ps
 
 
-def block_forward_kernel(addr, ids_ref, wc_ref, od_ref, w_ref, h_ref, tab, sine, piv, cols,
+def block_forward_kernel(addr, ids_ref, wc_ref, od_ref, w_ref, wn_ref, h_ref, tab, sine, piv, cols,
                          wo_ref, out_ref, r_ref, tok_ref,
                          acc0, acc1, acc2, acc3, buf, wf, r2, hx, a07):
     step = pl.program_id(0)
     sh, sl = sine[:128, :], sine[128:, :]
 
+    accs = (acc0, acc1, acc2, acc3)
+
+    def corrected(src, l, level):
+        def put(tr, c):
+            for ct in range(8):
+                cs = slice(ct * 128, (ct + 1) * 128)
+                wf[level, tile(tr), cs] = src[l, tile(tr), cs] + total(accs, tile((level * 16 + tr) * 8 + ct))
+            return c
+        lax.fori_loop(0, 16, put, 0)
+
     @pl.when(step == 0)
     def _():
         tok_ref[...] = jnp.zeros((8, 128), F32)
-        accs = (acc0, acc1, acc2, acc3)
-        load_w(w_ref, acc0)
-        clear(accs[1:])
+        clear(accs)
         wc = wc_ref[:, :SLOT]
         stress = od_ref[:, 32:64] * jnp.sqrt(wc * wc + 0.25) * wc
         spread_rows(ids_ref[...], -stress, buf)
         add_rows(addr, accs, buf)
-
-        def put(tr, c):
-            for ct in range(8):
-                wf[tr // 16, tile(tr % 16), ct * 128:(ct + 1) * 128] = total(accs, tile(tr * 8 + ct))
-            return c
-        lax.fori_loop(0, 128, put, 0)
+        corrected(w_ref, 0, 0)
         lifted = (lax.axis_index("py") > 0).astype(F32)
         for c0, res in x_modes(wf[0] * lifted, tab):
             for b in range(res.shape[1] // 128):
@@ -359,6 +357,11 @@
     @pl.when((step > 0) & (step < 5))
     def _():
         lv = 2 * step - 2
+        corrected(w_ref, 1, lv + 1)
+
+        @pl.when(step < 4)
+        def _():
+            corrected(wn_ref, 0, lv + 2)
         w0, w1 = wf[lv], wf[lv + 1]
         wo_ref[0] = w0
         wo_ref[1] = w1
@@ -394,7 +397,7 @@
         out_ref[0, ROWS:2 * ROWS, :] = -res[:, 128:]
 
 
-def block_forward(addr, ids, wc, od, w2, h):
+def block_forward(addr, ids, wc, od, w, h):
     two = pl.BlockSpec((2, ROWS, N), lambda g: (jnp.clip(g - 1, 0, 3), 0, 0))
     col = pl.BlockSpec((LEV, ROWS, 128), lambda g: (0, 0, jnp.maximum(g - 5, 0)))
     small = fixed((OWNERS, 128))
@@ -402,17 +405,18 @@
     return pl.pallas_call(
         block_forward_kernel, grid=(5 + NPX,),
         out_shape=(big, jax.ShapeDtypeStruct((NPX, BLK, 128), F32), big, TOKEN),
-        in_specs=[SM, small, small, small, pl.BlockSpec((N, N), lambda g: (0, 0)), two, fixed((1536, 512)),
+        in_specs=[SM, small, small, small, two,
+                  pl.BlockSpec((1, ROWS, N), lambda g: (jnp.clip(2 * g, 2, 7), 0, 0)), two, fixed((1536, 512)),
                   fixed((256, 128)), col, fixed((2, ROWS, 128))],
         out_specs=(two, pl.BlockSpec((1, BLK, 128), lambda g: (jnp.maximum(g - 5, 0), 0, 0)), col, fixed((8, 128))),
         scratch_shapes=FOUR + [pltpu.VMEM((LEV, ROWS, N), F32), pltpu.VMEM((NPX, LEV, ROWS, 128), F32),
                                pltpu.VMEM((NPX, ROWS, 128), F32), pltpu.VMEM((ROWS, 256), F32)],
         compiler_params=params(VMEM_MIB), name="block_forward",
-    )(addr, ids, wc, od, w2, h, jnp.asarray(TAB), jnp.asarray(SINE2), jnp.asarray(PIVOT), jnp.asarray(COLS))
-
-
-def lam_row(lx):
-    return lx[0:1, pl.ds(pl.multiple_of(lax.axis_index("px") * 128, 128), 128)]
+    )(addr, ids, wc, od, w, w, h, jnp.asarray(TAB), jnp.asarray(SINE2), jnp.asarray(PIVOT), jnp.asarray(COLS))
+
+
+def lam_row(ly):
+    return ly[pl.ds(N + lax.axis_index("px"), 1), :]
 
 
 def edge_rows(x_ref, sr):
@@ -428,7 +432,7 @@
     return dot3(edge[tile(t, 128), :], edge[pl.ds(pl.multiple_of(N + t * 128, 128), 128), :], sh, sl)
 
 
-def y_forward_kernel(x_ref, tok, lx, ly, tab, edge, al_ref, pp, sr, st):
+def y_forward_kernel(x_ref, tok, ly, tab, edge, al_ref, pp, sr, st):
     x = jnp.concatenate([x_ref[:, :ROWS], x_ref[:, ROWS:2 * ROWS]], axis=-1).reshape(N, 256)
     s, d = x[:512] + x[512:], x[:512] - x[512:]
     ee, eo = s[:256] + s[256:], s[:256] - s[256:]
@@ -437,7 +441,7 @@
         res = dot3(*t, *split(v))
         pp[k0:k0 + res.shape[0], :] = res
     sh, sl = edge_rows(x_ref, sr)
-    lam_x = lam_row(lx)
+    lam_x = lam_row(ly)
 
     def some(t, c):
         st[...] = edge_modes(edge, t, sh, sl)
@@ -462,19 +466,19 @@
     return pl.pallas_call(
         y_forward_kernel, grid=(1,),
         out_shape=jax.ShapeDtypeStruct((NPY, 128, 128), F32),
-        in_specs=[fixed((NPX, BLK, 128)), fixed((8, 128)), fixed((8, N)), fixed((N, 128)), fixed((1536, 512)),
+        in_specs=[fixed((NPX, BLK, 128)), fixed((8, 128)), fixed((N + NPX, 128)), fixed((1536, 512)),
                   fixed((2 * N, 16))],
         out_specs=fixed((NPY, 128, 128)),
         scratch_shapes=[pltpu.VMEM((N, 256), F32), pltpu.VMEM((16, N), F32), pltpu.VMEM((128, N), F32)],
         compiler_params=params(VMEM_MIB), name="y_forward",
-    )(x, tok, jnp.asarray(LAM_X), jnp.asarray(LAM_Y), jnp.asarray(TAB_T), jnp.asarray(EDGE_F))
-
-
-def ladder_kernel(al_ref, lx, ly, fl_ref, out_ref):
+    )(x, tok, jnp.asarray(LAMS), jnp.asarray(TAB_T), jnp.asarray(EDGE_F))
+
+
+def ladder_kernel(al_ref, ly, fl_ref, out_ref):
     for j in range(NPY):
         out_ref[j, 128:, :] = fl_ref[j]
 
-    lam_x = lam_row(lx)
+    lam_x = lam_row(ly)
     mine = lax.axis_index("py") * 64
     for t in range(8):
         rows, tops = slice(t * 8, (t + 1) * 8), slice(64 + t * 8, 72 + t * 8)
@@ -502,15 +506,15 @@
 def ladder(al, fl):
     return pl.pallas_call(
         ladder_kernel, grid=(1,), out_shape=jax.ShapeDtypeStruct((NPY, 136, 128), F32),
-        in_specs=[fixed((NPY, 128, 128)), fixed((8, N)), fixed((N, 128)), fixed((NPY, 8, 128))],
+        in_specs=[fixed((NPY, 128, 128)), fixed((N + NPX, 128)), fixed((NPY, 8, 128))],
         out_specs=fixed((NPY, 136, 128)), compiler_params=params(VMEM_MIB), name="ladder",
-    )(al, jnp.asarray(LAM_X), jnp.asarray(LAM_Y), fl)
-
-
-def y_inverse_kernel(x_ref, pu_ref, lx, ly, tab, edge_f, edge_b, out_ref, tok_ref, sr, st, ph, pl_):
+    )(al, jnp.asarray(LAMS), fl)
+
+
+def y_inverse_kernel(x_ref, pu_ref, ly, tab, edge_f, edge_b, out_ref, tok_ref, sr, st, ph, pl_):
     tok_ref[...] = jnp.zeros((8, 128), F32)
     sh, sl = edge_rows(x_ref, sr)
-    lam_x = lam_row(lx)
+    lam_x = lam_row(ly)
 
     def some(t, c):
         st[...] = edge_modes(edge_f, t, sh, sl)
@@ -566,13 +570,13 @@
 def y_inverse(x, pu):
     return pl.pallas_call(
         y_inverse_kernel, grid=(1,), out_shape=(jax.ShapeDtypeStruct((NPX, BACK, 128), F32), TOKEN),
-        in_specs=[fixed((NPX, BLK, 128)), fixed((NPY, 136, 128)), fixed((8, N)), fixed((N, 128)), fixed((1536, 512)),
+        in_specs=[fixed((NPX, BLK, 128)), fixed((NPY, 136, 128)), fixed((N + NPX, 128)), fixed((1536, 512)),
                   fixed((2 * N, 16)), fixed((32, N))],
         out_specs=(fixed((NPX, BACK, 128)), fixed((8, 128))),
         scratch_shapes=[pltpu.VMEM((16, N), F32), pltpu.VMEM((128, N), F32),
                         pltpu.VMEM((N, N), BF16), pltpu.VMEM((N, N), BF16)],
         compiler_params=params(VMEM_MIB), name="y_inverse",
-    )(x, pu, jnp.asarray(LAM_X), jnp.asarray(LAM_Y), jnp.asarray(TAB), jnp.asarray(EDGE_F), jnp.asarray(EDGE_B))
+    )(x, pu, jnp.asarray(LAMS), jnp.asarray(TAB), jnp.asarray(EDGE_F), jnp.asarray(EDGE_B))
 
 
 def block_inverse_kernel(y_ref, g_ref, w_ref, roof_ref, tab, sine, piv, cols, ft, nr, hc, tok,
@@ -653,8 +657,9 @@
     od = swap(owner.reshape(OWNERS, 1, 128), ("px", "py")).reshape(OWNERS, 128)
     addr = addr.reshape(OWNERS * SLOT)
     w2, a2 = w_star.reshape(1024, 1024), air_temp.reshape(1024, 1024)
-    wc = gather_w(addr, ids, w2)
-    w_corr, sent, g, tok = block_forward(addr, ids, wc, od, w2, horiz_div)
+    tiles = w2.reshape(128, 8, 8, 128).transpose(0, 2, 1, 3).reshape(8192, 128)
+    wc = gather_w(addr, ids, tiles)
+    w_corr, sent, g, tok = block_forward(addr, ids, wc, od, w_star, horiz_div)
     xs = swap(sent, "px")
     flux, fl, tok = heat_flux(addr, tok, ids, wc, od, a2)
     pu = swap(ladder(swap(y_forward(xs, tok), "py"), fl), "py")

time: 179 us -> 175 us (0.978)
  Pallas kernels: 99.7 us -> 87.6 us
  local copies, waits for them, and re-layouts: 2.71 us -> 10.5 us
    unnamed x6 -> x60, local copies, waits for them, and re-layouts: 2.71 us -> 10.5 us
    pallas_call x1, Pallas kernels: 3.07 us -> 0.69 us  [ladder(): pl.pallas_call(ladder_kernel, grid=(1,), out_shape=jax.ShapeDtypeStruct((...]
    pallas_call x1, Pallas kernels: 28.5 us -> 26.5 us  [block_forward(): pl.pallas_call(block_forward_kernel, grid=(5 + NPX,), out_shape=(big, jax...]
  transfers between devices with their start and end apart: 3 -> 3, of which waited for: 2 -> 2; matrix products, arithmetic and copies ran while one was open for 0% -> 0% of each run, Pallas kernels for 19% -> 17%
where the time goes in v6:
time: 175 us; the launch traced here: 174 us
  Pallas kernels  87.6 us (50%)
  blocking collectives  41.3 us (24%)
  starting transfers between devices  24.2 us (14%)
  local copies, waits for them, and re-layouts  10.5 us (6%)
  waiting for transfers between devices  9.53 us (5%)
    all_to_all x2, blocking collectives, swap(): return lax.all_to_all(x, axes, split_axis=0, concat_axis=0, tiled=True)  41.3 us
    pallas_call x1, Pallas kernels, block_forward(): pl.pallas_call(block_forward_kernel, grid=(5 + NPX,), out_shape=(big, jax...  26.5 us
    all_to_all x3, starting transfers between devices, swap(): return lax.all_to_all(x, axes, split_axis=0, concat_axis=0, tiled=True)  24.2 us
    pallas_call x1, Pallas kernels, block_inverse(): pl.pallas_call(block_inverse_kernel, grid=(NPX + 4,), out_shape=(jax.Shap...  15.7 us
    pallas_call x1, Pallas kernels, new_theta(): pl.pallas_call(theta_kernel, out_shape=(jax.ShapeDtypeStruct((1024, 1024)...  11.5 us
    unnamed x60, local copies, waits for them, and re-layouts  10.5 us
    all_to_all x3, waiting for transfers between devices, swap(): return lax.all_to_all(x, axes, split_axis=0, concat_axis=0, tiled=True)  9.53 us
    pallas_call x1, Pallas kernels, gather_w(): pl.pallas_call(gather_kernel, out_shape=jax.ShapeDtypeStruct((OWNERS, 128...  9.31 us
  transfers between devices with their start and end apart: 3, of which 2 were waited for; matrix products, arithmetic and copies ran while one was open for 0% of the time, Pallas kernels for 17%

profile of v6, /device:TPU:1, one launch (start us, length us, event | category | flops | bytes accessed | tf_op | source)
XLA Modules:
  0.0 173.9 jit_solution(6387413526135898676)
XLA Ops:
  0.6 1.5 pack_owner.1
  2.2 11.5 %all-to-all-start = ((f32[128,1,128]{2,1,0:T(1,128)}), f32[128,1,128]{2,1,0:T(1,128)S(1)}, u32[]{:S(2)}, u32[]{:S(2)}) async-start(f32[128,1,128]{2,1,0:T(1,128)} %bitcast.32), calls=%async_computation | async-start | bytes 131072 | tf_op jit(solution)/shard_map/all_to_all | solution.py:649
  13.7 0.8 copy-done.8
  14.5 0.7 copy-done.14
  15.2 9.3 %facet_gather.1.wc_ref = f32[128,128]{1,0:T(8,128)S(1)} custom-call(s32[4096]{0:T(1024)S(1)} %bitcast.23, s32[128,128]{1,0:T(8,128)S(1)} %copy-done.8, f32[8192,128]{1,0:T(8,128)} %bitcast.31), custom_call_target="tpu_custom_call" | custom-call | tf_op jit(solution)/shard_map/facet_gather/pallas_call | solution.py:168
  24.6 26.5 %block_forward.1 = (f32[8,128,1024]{2,1,0:T(8,128)}, f32[8,272,128]{2,1,0:T(8,128)S(1)}, f32[8,128,1024]{2,1,0:T(8,128)}, f32[8,128]{1,0:T(8,128)S(1)}) custom-call(s32[4096]{0:T(1024)S(1)} %bitcast.24, s32[128,128]{1,0:T(8,128)S(1)} %copy-done.9, f32[128,128]{1,0:T(8,128)S(1)} %facet_gather.1.wc_ref, f32[128,128]{1,0:T(8,128)S(1)} %bitcast.21, ...), custom_call_target="tpu_custom_call" | custom-call | tf_op jit(solution)/shard_map/block_forward/pallas_call | solution.py:405
  51.1 1.0 copy-done.7
  52.1 0.6 copy-done.26
  52.7 4.9 %all-to-all-start.1 = ((f32[8,272,128]{2,1,0:T(8,128)}), f32[8,272,128]{2,1,0:T(8,128)S(1)}, u32[]{:S(2)}, u32[]{:S(2)}) async-start(f32[8,272,128]{2,1,0:T(8,128)} %copy-done.7), calls=%async_computation.1 | async-start | bytes 2228224 | tf_op jit(solution)/shard_map/all_to_all | solution.py:649
  57.7 0.0 copy-start.27
  57.7 0.7 copy-done.27
  58.3 8.5 %heat_flux.1 = (f32[128,128]{1,0:T(8,128)S(1)}, f32[16,8,128]{2,1,0:T(8,128)S(1)}, f32[8,128]{1,0:T(8,128)S(1)}) custom-call(s32[4096]{0:T(1024)S(1)} %bitcast.25, f32[8,128]{1,0:T(8,128)S(1)} %copy-done.27, s32[128,128]{1,0:T(8,128)S(1)} %copy-done.9, f32[128,128]{1,0:T(8,128)S(1)} %facet_gather.1.wc_ref, f32[128,128]{1,0:T(8,128)S(1)} %bitcast.22, ...), custom_call_target="tpu_custom_call" | custom-call | bytes 26214400 | tf_op jit(solution)/shard_map/heat_flux/pallas_call | solution.py:193
  66.8 0.6 copy-done.17
  67.4 0.6 copy-done.19
  68.1 0.6 copy-done.28
  68.7 4.8 %all-to-all-done.1.x_ref = f32[8,272,128]{2,1,0:T(8,128)S(1)} async-done(((f32[8,272,128]{2,1,0:T(8,128)}), f32[8,272,128]{2,1,0:T(8,128)S(1)}, u32[]{:S(2)}, u32[]{:S(2)}) %all-to-all-start.1) | async-done | bytes 1114144 | tf_op jit(solution)/shard_map/all_to_all | solution.py:649
  73.4 1.0 copy-done.3
  74.5 1.0 copy-done.5
  75.5 0.7 copy-done.29
  76.2 5.2 %y_forward.1 = f32[16,128,128]{2,1,0:T(8,128)S(1)} custom-call(f32[8,272,128]{2,1,0:T(8,128)S(1)} %all-to-all-done.1.x_ref, f32[8,128]{1,0:T(8,128)S(1)} %copy-done.29, f32[1032,128]{1,0:T(8,128)S(1)} %copy-done.3, bf16[1536,512]{1,0:T(8,128)(2,1)} %constant.21.clone.tab, bf16[2048,16]{1,0:T(8,128)(2,1)S(1)} %copy-done.5), custom_call_target="tpu_custom_call" | custom-call | tf_op jit(solution)/shard_map/y_forward/pallas_call | solution.py:466
  81.4 0.0 copy-start.4
  81.4 22.7 %all_to_all.25.al_ref = f32[16,128,128]{2,1,0:T(8,128)S(1)} all-to-all(f32[16,128,128]{2,1,0:T(8,128)S(1)} %y_forward.1), channel_id=1, replica_groups=mesh['px'=8,'py'=16] {'py'}, dimensions={0} | all-to-all | bytes 2097152 | tf_op jit(solution)/shard_map/all_to_all | solution.py:649
  104.2 0.7 ladder.1
  104.9 18.6 %all_to_all.26.pu_ref = f32[16,136,128]{2,1,0:T(8,128)S(1)} all-to-all(f32[16,136,128]{2,1,0:T(8,128)S(1)} %ladder.1), channel_id=1, replica_groups=mesh['px'=8,'py'=16] {'py'}, dimensions={0} | all-to-all | bytes 2228224 | tf_op jit(solution)/shard_map/all_to_all | solution.py:649
  123.5 8.6 %y_inverse.1 = (f32[8,280,128]{2,1,0:T(8,128)}, f32[8,128]{1,0:T(8,128)S(1)}) custom-call(f32[8,272,128]{2,1,0:T(8,128)S(1)} %all-to-all-done.1.x_ref, f32[16,136,128]{2,1,0:T(8,128)S(1)} %all_to_all.26.pu_ref, f32[1032,128]{1,0:T(8,128)S(1)} %copy-done.4, bf16[1536,512]{1,0:T(8,128)(2,1)} %constant.16.clone.tab, bf16[2048,16]{1,0:T(8,128)(2,1)S(1)} %copy-done.6, ...), custom_call_target="tpu_custom_call" | custom-call | tf_op jit(solution)/shard_map/y_inverse/pallas_call | solution.py:571
  132.0 0.6 copy-done.24
  132.7 7.8 %all-to-all-start.4 = ((f32[8,280,128]{2,1,0:T(8,128)}), f32[8,280,128]{2,1,0:T(8,128)}, u32[]{:S(2)}, u32[]{:S(2)}) async-start(f32[8,280,128]{2,1,0:T(8,128)} %get-tuple-element.26), calls=%async_computation.4 | async-start | bytes 2293760 | tf_op jit(solution)/shard_map/all_to_all | solution.py:649
  140.5 11.5 %new_theta.1 = (bf16[1024,1024]{1,0:T(8,128)(2,1)}, f32[8,128]{1,0:T(8,128)S(1)}) custom-call(s32[4096]{0:T(1024)S(1)} %bitcast.26, f32[8,128]{1,0:T(8,128)S(1)} %copy-done.25, s32[128,128]{1,0:T(8,128)S(1)} %copy-done.9, f32[128,128]{1,0:T(8,128)S(1)} %copy-done.18, bf16[1024,1024]{1,0:T(8,128)(2,1)S(1)} %bitcast.20), custom_call_target="tpu_custom_call" | custom-call | bytes 41943040 | tf_op jit(solution)/shard_map/new_theta/pallas_call | solution.py:221
  152.0 4.7 %all-to-all-done.4.y_ref = f32[8,280,128]{2,1,0:T(8,128)} async-done(((f32[8,280,128]{2,1,0:T(8,128)}), f32[8,280,128]{2,1,0:T(8,128)}, u32[]{:S(2)}, u32[]{:S(2)}) %all-to-all-start.4) | async-done | bytes 1146912 | tf_op jit(solution)/shard_map/all_to_all | solution.py:649
  156.8 0.0 copy-start.1
  156.8 1.4 copy-done.1
  158.2 15.7 %block_inverse.1 = (f32[8,128,1024]{2,1,0:T(8,128)}, f32[32,128]{1,0:T(8,128)}) custom-call(f32[8,280,128]{2,1,0:T(8,128)} %all-to-all-done.4.y_ref, f32[8,128,1024]{2,1,0:T(8,128)} %get-tuple-element.27.g_ref, f32[8,128,1024]{2,1,0:T(8,128)} %get-tuple-element.28.w_ref, s32[128,1024]{1,0:T(8,128)S(1)} %copy-done.11, bf16[1536,512]{1,0:T(8,128)(2,1)S(1)} %copy-done.1, ...), custom_call_target="tpu_custom_call" | custom-call | tf_op jit(solution)/shard_map/block_inverse/pallas_call | solution.py:633
  (45 shorter events, 0.1 us)
Async XLA Ops:
  2.2 22.4 %all-to-all-start = ((f32[128,1,128]{2,1,0:T(1,128)}), f32[128,1,128]{2,1,0:T(1,128)S(1)}, u32[]{:S(2)}, u32[]{:S(2)}) async-start(f32[128,1,128]{2,1,0:T(1,128)} %bitcast.32), calls=%async_computation | async-start | bytes 131072 | tf_op jit(solution)/shard_map/all_to_all | solution.py:649
  13.7 0.8 copy-start.8
  14.5 0.7 copy-start.14
  15.2 9.3 %copy-start.2 = (bf16[1536,512]{1,0:T(8,128)(2,1)S(1)}, bf16[1536,512]{1,0:T(8,128)(2,1)}, u32[]{:S(2)}) copy-start(bf16[1536,512]{1,0:T(8,128)(2,1)} %constant.16.clone.tab) | copy-start | bytes 4718596
  15.2 9.3 %copy-start.9 = (s32[128,128]{1,0:T(8,128)S(1)}, s32[128,128]{1,0:T(8,128)}, u32[]{:S(2)}) copy-start(s32[128,128]{1,0:T(8,128)} %get-tuple-element.20.ids_ref) | copy-start | bytes 196612
  15.2 9.4 %copy-start.10 = (f32[2,128,128]{2,1,0:T(8,128)S(1)}, f32[2,128,128]{2,1,0:T(8,128)}, u32[]{:S(2)}) copy-start(f32[2,128,128]{2,1,0:T(8,128)} %constant.19.clone.cols) | copy-start | bytes 393220
  15.2 9.4 %copy-start.12 = (bf16[256,128]{1,0:T(8,128)(2,1)S(1)}, bf16[256,128]{1,0:T(8,128)(2,1)}, u32[]{:S(2)}) copy-start(bf16[256,128]{1,0:T(8,128)(2,1)} %constant.17.clone.sine) | copy-start | bytes 196612
  51.1 1.0 copy-start.7
  52.1 0.6 copy-start.26
  52.7 4.9 %copy-start = (bf16[8,128,1024]{2,1,0:T(8,128)(2,1)S(1)}, bf16[8,128,1024]{2,1,0:T(8,128)(2,1)}, u32[]{:S(2)}) copy-start(bf16[8,128,1024]{2,1,0:T(8,128)(2,1)} %param.20) | copy-start | bytes 6291460
  52.7 4.9 %copy-start.15 = (s32[32,128]{1,0:T(8,128)S(1)}, s32[32,128]{1,0:T(8,128)}, u32[]{:S(2)}) copy-start(s32[32,128]{1,0:T(8,128)} %get-tuple-element.19) | copy-start | bytes 49156
  52.7 20.7 %all-to-all-start.1 = ((f32[8,272,128]{2,1,0:T(8,128)}), f32[8,272,128]{2,1,0:T(8,128)S(1)}, u32[]{:S(2)}, u32[]{:S(2)}) async-start(f32[8,272,128]{2,1,0:T(8,128)} %copy-done.7), calls=%async_computation.1 | async-start | bytes 2228224 | tf_op jit(solution)/shard_map/all_to_all | solution.py:649
  57.7 0.7 copy-start.27
  66.8 0.6 copy-start.17
  67.4 0.6 copy-start.19
  68.1 0.6 copy-start.28
  73.4 1.0 copy-start.3
  74.5 1.0 copy-start.5
  75.5 0.7 copy-start.29
  81.4 22.8 %copy-start.4 = (f32[1032,128]{1,0:T(8,128)S(1)}, f32[1032,128]{1,0:T(8,128)}, u32[]{:S(2)}) copy-start(f32[1032,128]{1,0:T(8,128)} %constant.20.clone.ly) | copy-start | bytes 1585156
  81.4 22.8 %copy-start.20 = (f32[16,8,128]{2,1,0:T(8,128)S(1)}, f32[16,8,128]{2,1,0:T(8,128)}, u32[]{:S(2)}) copy-start(f32[16,8,128]{2,1,0:T(8,128)} %copy-done.19) | copy-start | bytes 196612
  104.2 19.3 %copy-start.6 = (bf16[2048,16]{1,0:T(8,128)(2,1)S(1)}, bf16[2048,16]{1,0:T(8,128)(2,1)}, u32[]{:S(2)}) copy-start(bf16[2048,16]{1,0:T(8,128)(2,1)} %constant.22.clone.edge.edge_f) | copy-start | bytes 196612
  104.2 19.3 %copy-start.16 = (bf16[32,1024]{1,0:T(8,128)(2,1)S(1)}, bf16[32,1024]{1,0:T(8,128)(2,1)}, u32[]{:S(2)}) copy-start(bf16[32,1024]{1,0:T(8,128)(2,1)} %constant.23.clone.edge_b) | copy-start | bytes 196612
  132.6 7.8 %copy-start.18 = (f32[128,128]{1,0:T(8,128)S(1)}, f32[128,128]{1,0:T(8,128)}, u32[]{:S(2)}) copy-start(f32[128,128]{1,0:T(8,128)} %copy-done.17) | copy-start | bytes 196612
  132.6 7.8 %copy-start.25 = (f32[8,128]{1,0:T(8,128)S(1)}, f32[8,128]{1,0:T(8,128)}, u32[]{:S(2)}) copy-start(f32[8,128]{1,0:T(8,128)} %copy-done.24) | copy-start | bytes 12292
  132.6 24.1 %copy-start.11 = (s32[128,1024]{1,0:T(8,128)S(1)}, s32[128,1024]{1,0:T(8,128)}, u32[]{:S(2)}) copy-start(s32[128,1024]{1,0:T(8,128)} %roof_ref.1) | copy-start | bytes 1572868
  132.6 24.1 %copy-start.13 = (bf16[256,128]{1,0:T(8,128)(2,1)S(1)}, bf16[256,128]{1,0:T(8,128)(2,1)}, u32[]{:S(2)}) copy-start(bf16[256,128]{1,0:T(8,128)(2,1)} %constant.17.clone.sine) | copy-start | bytes 196612
  132.6 24.1 %copy-start.21 = (f32[1,4096]{1,0:T(1,128)S(1)}, f32[1,4096]{1,0:T(1,128)}, u32[]{:S(2)}) copy-start(f32[1,4096]{1,0:T(1,128)} %param.23) | copy-start | bytes 49156
  132.7 24.1 %copy-start.22 = (f32[1,4096]{1,0:T(1,128)S(1)}, f32[1,4096]{1,0:T(1,128)}, u32[]{:S(2)}) copy-start(f32[1,4096]{1,0:T(1,128)} %param.24) | copy-start | bytes 49156
  132.7 24.1 %copy-start.23 = (f32[1,4096]{1,0:T(1,128)S(1)}, f32[1,4096]{1,0:T(1,128)}, u32[]{:S(2)}) copy-start(f32[1,4096]{1,0:T(1,128)} %param.25) | copy-start | bytes 49156
  132.7 24.1 %all-to-all-start.4 = ((f32[8,280,128]{2,1,0:T(8,128)}), f32[8,280,128]{2,1,0:T(8,128)}, u32[]{:S(2)}, u32[]{:S(2)}) async-start(f32[8,280,128]{2,1,0:T(8,128)} %get-tuple-element.26), calls=%async_computation.4 | async-start | bytes 2293760 | tf_op jit(solution)/shard_map/all_to_all | solution.py:649
  156.8 1.4 copy-start.1
  (1 other events, 0.6 us)

commit v7 on v6

--- a/solution.py
+++ b/solution.py
@@ -375,42 +375,45 @@
 
     @pl.when(step >= 5)
     def _():
-        lt = step - 5
-
-        def inner(bt, acc):
-            rows = tile(bt, STRIP)
-            rs = [r2[lt, k, rows, :] for k in range(LEV)]
-            for k in range(LEV):
-                r_ref[k, rows, :] = rs[k]
-            ps = eliminate(rs, [piv[k, rows, :] for k in range(LEV)])
-            s0, s1 = cols[0, rows, :], cols[1, rows, :]
-            a07[rows, :128] = ps[0]
-            a07[rows, 128:] = ps[7]
-            return tuple(acc[k] + fold(s0 * ps[k]) for k in range(LEV)) + tuple(
-                acc[LEV + k] + fold(s1 * ps[k]) for k in range(LEV))
-        acc = lax.fori_loop(0, ROWS // STRIP, inner, tuple(jnp.zeros((8, 128), F32) for _ in range(16)))
-        for e in range(2):
-            sums = [jnp.sum(acc[e * LEV + k], axis=0, keepdims=True) for k in range(LEV)]
-            out_ref[0, 2 * ROWS + e * LEV:2 * ROWS + (e + 1) * LEV, :] = -jnp.concatenate(sums, axis=0)
+        for sub in range(2):
+            lt = 2 * (step - 5) + sub
+            ln = slice(sub * 128, (sub + 1) * 128)
+
+            def inner(bt, acc):
+                rows = tile(bt, STRIP)
+                rs = [r2[lt, k, rows, :] for k in range(LEV)]
+                for k in range(LEV):
+                    r_ref[k, rows, ln] = rs[k]
+                ps = eliminate(rs, [piv[k, rows, ln] for k in range(LEV)])
+                s0, s1 = cols[0, rows, :], cols[1, rows, :]
+                a07[rows, sub * 256:sub * 256 + 128] = ps[0]
+                a07[rows, sub * 256 + 128:(sub + 1) * 256] = ps[7]
+                return tuple(acc[k] + fold(s0 * ps[k]) for k in range(LEV)) + tuple(
+                    acc[LEV + k] + fold(s1 * ps[k]) for k in range(LEV))
+            acc = lax.fori_loop(0, ROWS // STRIP, inner, tuple(jnp.zeros((8, 128), F32) for _ in range(16)))
+            for e in range(2):
+                sums = [jnp.sum(acc[e * LEV + k], axis=0, keepdims=True) for k in range(LEV)]
+                out_ref[sub, 2 * ROWS + e * LEV:2 * ROWS + (e + 1) * LEV, :] = -jnp.concatenate(sums, axis=0)
         res = dot3(sh, sl, *split(a07[...]))
-        out_ref[0, :ROWS, :] = -res[:, :128] - hx[lt]
-        out_ref[0, ROWS:2 * ROWS, :] = -res[:, 128:]
+        for sub in range(2):
+            out_ref[sub, :ROWS, :] = -res[:, sub * 256:sub * 256 + 128] - hx[2 * (step - 5) + sub]
+            out_ref[sub, ROWS:2 * ROWS, :] = -res[:, sub * 256 + 128:(sub + 1) * 256]
 
 
 def block_forward(addr, ids, wc, od, w, h):
     two = pl.BlockSpec((2, ROWS, N), lambda g: (jnp.clip(g - 1, 0, 3), 0, 0))
-    col = pl.BlockSpec((LEV, ROWS, 128), lambda g: (0, 0, jnp.maximum(g - 5, 0)))
+    col = pl.BlockSpec((LEV, ROWS, 256), lambda g: (0, 0, jnp.maximum(g - 5, 0)))
     small = fixed((OWNERS, 128))
     big = jax.ShapeDtypeStruct((LEV, ROWS, N), F32)
     return pl.pallas_call(
-        block_forward_kernel, grid=(5 + NPX,),
+        block_forward_kernel, grid=(9,),
         out_shape=(big, jax.ShapeDtypeStruct((NPX, BLK, 128), F32), big, TOKEN),
         in_specs=[SM, small, small, small, two,
                   pl.BlockSpec((1, ROWS, N), lambda g: (jnp.clip(2 * g, 2, 7), 0, 0)), two, fixed((1536, 512)),
                   fixed((256, 128)), col, fixed((2, ROWS, 128))],
-        out_specs=(two, pl.BlockSpec((1, BLK, 128), lambda g: (jnp.maximum(g - 5, 0), 0, 0)), col, fixed((8, 128))),
+        out_specs=(two, pl.BlockSpec((2, BLK, 128), lambda g: (jnp.maximum(g - 5, 0), 0, 0)), col, fixed((8, 128))),
         scratch_shapes=FOUR + [pltpu.VMEM((LEV, ROWS, N), F32), pltpu.VMEM((NPX, LEV, ROWS, 128), F32),
-                               pltpu.VMEM((NPX, ROWS, 128), F32), pltpu.VMEM((ROWS, 256), F32)],
+                               pltpu.VMEM((NPX, ROWS, 128), F32), pltpu.VMEM((ROWS, 512), F32)],
         compiler_params=params(VMEM_MIB), name="block_forward",
     )(addr, ids, wc, od, w, w, h, jnp.asarray(TAB), jnp.asarray(SINE2), jnp.asarray(PIVOT), jnp.asarray(COLS))
 
@@ -584,32 +587,37 @@
     step = pl.program_id(0)
     sh, sl = sine[:128, :], sine[128:, :]
 
-    @pl.when(step < NPX)
+    @pl.when(step < 4)
     def _():
-        fb[step] = y_ref[0, BLK:, :]
-        spu[...] = dot3(sh, sl, *split(jnp.concatenate([y_ref[0, :ROWS, :], y_ref[0, ROWS:2 * ROWS, :]], axis=1)))
-        edge = [y_ref[0, 2 * ROWS + k:2 * ROWS + k + 1, :] for k in range(2 * LEV)]
-
-        def inner(bt, c):
-            rows = tile(bt, STRIP)
-            s0, s1 = cols[0, rows, :], cols[1, rows, :]
-            low, top = spu[rows, :128], spu[rows, 128:]
-            fs = [s0 * edge[k] + s1 * edge[LEV + k] - g_ref[k, rows, :] for k in range(LEV)]
-            fs[0] = fs[0] + low
-            fs[7] = fs[7] + top
-            prev = low
-            for k, p in enumerate(eliminate(fs, [piv[k, rows, :] for k in range(LEV)])):
-                wv[rows, k * 128:(k + 1) * 128] = p - prev
-                prev = p
-            return c
-        lax.fori_loop(0, ROWS // STRIP, inner, 0)
-        res = dot3(sh, sl, *split(wv[...]))
-        for k in range(LEV):
-            field[k, :, tile(step, 128)] = res[:, k * 128:(k + 1) * 128]
-
-    @pl.when(step >= NPX)
+        parts = [y_ref[sub, f * ROWS:(f + 1) * ROWS, :] for sub in range(2) for f in range(2)]
+        spu[...] = dot3(sh, sl, *split(jnp.concatenate(parts, axis=1)))
+        for sub in range(2):
+            lt = 2 * step + sub
+            ln = slice(sub * 128, (sub + 1) * 128)
+            fb[lt] = y_ref[sub, BLK:, :]
+            edge = [y_ref[sub, 2 * ROWS + k:2 * ROWS + k + 1, :] for k in range(2 * LEV)]
+
+            def inner(bt, c):
+                rows = tile(bt, STRIP)
+                s0, s1 = cols[0, rows, :], cols[1, rows, :]
+                low = spu[rows, sub * 256:sub * 256 + 128]
+                top = spu[rows, sub * 256 + 128:(sub + 1) * 256]
+                fs = [s0 * edge[k] + s1 * edge[LEV + k] - g_ref[k, rows, ln] for k in range(LEV)]
+                fs[0] = fs[0] + low
+                fs[7] = fs[7] + top
+                prev = low
+                for k, p in enumerate(eliminate(fs, [piv[k, rows, ln] for k in range(LEV)])):
+                    wv[sub, rows, k * 128:(k + 1) * 128] = p - prev
+                    prev = p
+                return c
+            lax.fori_loop(0, ROWS // STRIP, inner, 0)
+            res = dot3(sh, sl, *split(wv[sub]))
+            for k in range(LEV):
+                field[k, :, tile(lt, 128)] = res[:, k * 128:(k + 1) * 128]
+
+    @pl.when(step >= 4)
     def _():
-        pair = step - NPX
+        pair = step - 4
         v = jnp.concatenate([field[2 * pair], field[2 * pair + 1]], axis=0)
         te, to, td = tab_parts(tab)
         t0 = dot3(*split(v[:, :256]), *te)
@@ -622,24 +630,24 @@
                 solid = lax.axis_index("py") * LEV + 2 * pair + l < roof_ref[:, cs]
                 out_ref[l, :, cs] = jnp.where(solid, 0.0, w_ref[l, :, cs] - res[l * 128:(l + 1) * 128])
 
-    @pl.when(step == NPX + 3)
+    @pl.when(step == 7)
     def _():
         flux = jnp.concatenate([fb[i, :4, :] for i in range(NPX)], axis=0)
         nt_ref[...] = ft[...] + (nr[...] - flux - 0.5 * ft[...]) / hc[...]
 
 
 def block_inverse(y, g, w, roof, ft, nr, hc, tok):
-    late = pl.BlockSpec((2, ROWS, N), lambda t: (jnp.maximum(t - NPX, 0), 0, 0))
-    return pl.pallas_call(
-        block_inverse_kernel, grid=(NPX + 4,),
+    late = pl.BlockSpec((2, ROWS, N), lambda t: (jnp.maximum(t - 4, 0), 0, 0))
+    return pl.pallas_call(
+        block_inverse_kernel, grid=(8,),
         out_shape=(jax.ShapeDtypeStruct((LEV, ROWS, N), F32), jax.ShapeDtypeStruct((32, 128), F32)),
-        in_specs=[pl.BlockSpec((1, BACK, 128), lambda t: (jnp.minimum(t, NPX - 1), 0, 0)),
-                  pl.BlockSpec((LEV, ROWS, 128), lambda t: (0, 0, jnp.minimum(t, NPX - 1))),
+        in_specs=[pl.BlockSpec((2, BACK, 128), lambda t: (jnp.minimum(t, 3), 0, 0)),
+                  pl.BlockSpec((LEV, ROWS, 256), lambda t: (0, 0, jnp.minimum(t, 3))),
                   late, fixed((ROWS, N)), fixed((1536, 512)), fixed((256, 128)),
-                  pl.BlockSpec((LEV, ROWS, 128), lambda t: (0, 0, jnp.minimum(t, NPX - 1))), fixed((2, ROWS, 128)),
+                  pl.BlockSpec((LEV, ROWS, 256), lambda t: (0, 0, jnp.minimum(t, 3))), fixed((2, ROWS, 128)),
                   fixed((32, 128)), fixed((32, 128)), fixed((32, 128)), fixed((8, 128))],
         out_specs=(late, fixed((32, 128))),
-        scratch_shapes=[pltpu.VMEM((LEV, ROWS, N), F32), pltpu.VMEM((ROWS, N), F32), pltpu.VMEM((ROWS, 256), F32),
+        scratch_shapes=[pltpu.VMEM((LEV, ROWS, N), F32), pltpu.VMEM((2, ROWS, N), F32), pltpu.VMEM((ROWS, 512), F32),
                         pltpu.VMEM((NPX, 8, 128), F32)],
         compiler_params=params(VMEM_MIB), name="block_inverse",
     )(y, g, w, roof, jnp.asarray(TAB_T), jnp.asarray(SINE2), jnp.asarray(PIVOT), jnp.asarray(COLS), ft, nr, hc, tok)

time: 175 us -> 171 us (0.977)
  Pallas kernels: 87.6 us -> 83.7 us
    pallas_call x2, Pallas kernels: 42.3 us -> 38.4 us  [the longest x1 24.6 us: block_forward(): pl.pallas_call(block_forward_kernel, grid=(9,), out_shape=(big, jax.Shape...]
where the time goes in v7:
time: 171 us; the launch traced here: 170 us
  Pallas kernels  83.7 us (49%)
  blocking collectives  41.3 us (24%)
  starting transfers between devices  24.2 us (14%)
  local copies, waits for them, and re-layouts  10.5 us (6%)
  waiting for transfers between devices  9.53 us (6%)
    all_to_all x2, blocking collectives, swap(): return lax.all_to_all(x, axes, split_axis=0, concat_axis=0, tiled=True)  41.3 us
    pallas_call x1, Pallas kernels, block_forward(): pl.pallas_call(block_forward_kernel, grid=(9,), out_shape=(big, jax.Shape...  24.6 us
    all_to_all x3, starting transfers between devices, swap(): return lax.all_to_all(x, axes, split_axis=0, concat_axis=0, tiled=True)  24.2 us
    pallas_call x1, Pallas kernels, block_inverse(): pl.pallas_call(block_inverse_kernel, grid=(8,), out_shape=(jax.ShapeDtype...  13.8 us
    pallas_call x1, Pallas kernels, new_theta(): pl.pallas_call(theta_kernel, out_shape=(jax.ShapeDtypeStruct((1024, 1024)...  11.5 us
    unnamed x60, local copies, waits for them, and re-layouts  10.5 us
    all_to_all x3, waiting for transfers between devices, swap(): return lax.all_to_all(x, axes, split_axis=0, concat_axis=0, tiled=True)  9.53 us
    pallas_call x1, Pallas kernels, gather_w(): pl.pallas_call(gather_kernel, out_shape=jax.ShapeDtypeStruct((OWNERS, 128...  9.31 us
  transfers between devices with their start and end apart: 3, of which 2 were waited for; matrix products, arithmetic and copies ran while one was open for 0% of the time, Pallas kernels for 17%

profile of v7, /device:TPU:1, one launch (start us, length us, event | category | flops | bytes accessed | tf_op | source)
XLA Modules:
  0.0 170.1 jit_solution(12914042484878591605)
XLA Ops:
  0.6 1.5 pack_owner.1
  2.2 11.5 %all-to-all-start = ((f32[128,1,128]{2,1,0:T(1,128)}), f32[128,1,128]{2,1,0:T(1,128)S(1)}, u32[]{:S(2)}, u32[]{:S(2)}) async-start(f32[128,1,128]{2,1,0:T(1,128)} %bitcast.32), calls=%async_computation | async-start | bytes 131072 | tf_op jit(solution)/shard_map/all_to_all | solution.py:657
  13.7 0.0 copy-start.8
  13.7 0.8 copy-done.8
  14.5 0.7 copy-done.14
  15.2 9.3 %facet_gather.1.wc_ref = f32[128,128]{1,0:T(8,128)S(1)} custom-call(s32[4096]{0:T(1024)S(1)} %bitcast.23, s32[128,128]{1,0:T(8,128)S(1)} %copy-done.8, f32[8192,128]{1,0:T(8,128)} %bitcast.31), custom_call_target="tpu_custom_call" | custom-call | tf_op jit(solution)/shard_map/facet_gather/pallas_call | solution.py:168
  24.6 24.6 %block_forward.1 = (f32[8,128,1024]{2,1,0:T(8,128)}, f32[8,272,128]{2,1,0:T(8,128)S(1)}, f32[8,128,1024]{2,1,0:T(8,128)}, f32[8,128]{1,0:T(8,128)S(1)}) custom-call(s32[4096]{0:T(1024)S(1)} %bitcast.24, s32[128,128]{1,0:T(8,128)S(1)} %copy-done.9, f32[128,128]{1,0:T(8,128)S(1)} %facet_gather.1.wc_ref, f32[128,128]{1,0:T(8,128)S(1)} %bitcast.21, ...), custom_call_target="tpu_custom_call" | custom-call | tf_op jit(solution)/shard_map/block_forward/pallas_call | solution.py:408
  49.2 1.0 copy-done.7
  50.2 0.6 copy-done.26
  50.8 4.9 %all-to-all-start.1 = ((f32[8,272,128]{2,1,0:T(8,128)}), f32[8,272,128]{2,1,0:T(8,128)S(1)}, u32[]{:S(2)}, u32[]{:S(2)}) async-start(f32[8,272,128]{2,1,0:T(8,128)} %copy-done.7), calls=%async_computation.1 | async-start | bytes 2228224 | tf_op jit(solution)/shard_map/all_to_all | solution.py:657
  55.8 0.7 copy-done.27
  56.4 8.5 %heat_flux.1 = (f32[128,128]{1,0:T(8,128)S(1)}, f32[16,8,128]{2,1,0:T(8,128)S(1)}, f32[8,128]{1,0:T(8,128)S(1)}) custom-call(s32[4096]{0:T(1024)S(1)} %bitcast.25, f32[8,128]{1,0:T(8,128)S(1)} %copy-done.27, s32[128,128]{1,0:T(8,128)S(1)} %copy-done.9, f32[128,128]{1,0:T(8,128)S(1)} %facet_gather.1.wc_ref, f32[128,128]{1,0:T(8,128)S(1)} %bitcast.22, ...), custom_call_target="tpu_custom_call" | custom-call | bytes 26214400 | tf_op jit(solution)/shard_map/heat_flux/pallas_call | solution.py:193
  64.9 0.6 copy-done.17
  65.5 0.6 copy-done.19
  66.2 0.6 copy-done.28
  66.8 4.8 %all-to-all-done.1.x_ref = f32[8,272,128]{2,1,0:T(8,128)S(1)} async-done(((f32[8,272,128]{2,1,0:T(8,128)}), f32[8,272,128]{2,1,0:T(8,128)S(1)}, u32[]{:S(2)}, u32[]{:S(2)}) %all-to-all-start.1) | async-done | bytes 1114144 | tf_op jit(solution)/shard_map/all_to_all | solution.py:657
  71.5 1.0 copy-done.3
  72.6 1.0 copy-done.5
  73.6 0.7 copy-done.29
  74.3 5.2 %y_forward.1 = f32[16,128,128]{2,1,0:T(8,128)S(1)} custom-call(f32[8,272,128]{2,1,0:T(8,128)S(1)} %all-to-all-done.1.x_ref, f32[8,128]{1,0:T(8,128)S(1)} %copy-done.29, f32[1032,128]{1,0:T(8,128)S(1)} %copy-done.3, bf16[1536,512]{1,0:T(8,128)(2,1)} %constant.21.clone.tab, bf16[2048,16]{1,0:T(8,128)(2,1)S(1)} %copy-done.5), custom_call_target="tpu_custom_call" | custom-call | tf_op jit(solution)/shard_map/y_forward/pallas_call | solution.py:469
  79.5 0.0 copy-start.4
  79.5 22.7 %all_to_all.25.al_ref = f32[16,128,128]{2,1,0:T(8,128)S(1)} all-to-all(f32[16,128,128]{2,1,0:T(8,128)S(1)} %y_forward.1), channel_id=1, replica_groups=mesh['px'=8,'py'=16] {'py'}, dimensions={0} | all-to-all | bytes 2097152 | tf_op jit(solution)/shard_map/all_to_all | solution.py:657
  102.3 0.7 ladder.1
  103.0 18.6 %all_to_all.26.pu_ref = f32[16,136,128]{2,1,0:T(8,128)S(1)} all-to-all(f32[16,136,128]{2,1,0:T(8,128)S(1)} %ladder.1), channel_id=1, replica_groups=mesh['px'=8,'py'=16] {'py'}, dimensions={0} | all-to-all | bytes 2228224 | tf_op jit(solution)/shard_map/all_to_all | solution.py:657
  121.6 8.6 %y_inverse.1 = (f32[8,280,128]{2,1,0:T(8,128)}, f32[8,128]{1,0:T(8,128)S(1)}) custom-call(f32[8,272,128]{2,1,0:T(8,128)S(1)} %all-to-all-done.1.x_ref, f32[16,136,128]{2,1,0:T(8,128)S(1)} %all_to_all.26.pu_ref, f32[1032,128]{1,0:T(8,128)S(1)} %copy-done.4, bf16[1536,512]{1,0:T(8,128)(2,1)} %constant.16.clone.tab, bf16[2048,16]{1,0:T(8,128)(2,1)S(1)} %copy-done.6, ...), custom_call_target="tpu_custom_call" | custom-call | tf_op jit(solution)/shard_map/y_inverse/pallas_call | solution.py:574
  130.2 0.6 copy-done.24
  130.8 7.8 %all-to-all-start.4 = ((f32[8,280,128]{2,1,0:T(8,128)}), f32[8,280,128]{2,1,0:T(8,128)}, u32[]{:S(2)}, u32[]{:S(2)}) async-start(f32[8,280,128]{2,1,0:T(8,128)} %get-tuple-element.26), calls=%async_computation.4 | async-start | bytes 2293760 | tf_op jit(solution)/shard_map/all_to_all | solution.py:657
  138.6 11.5 %new_theta.1 = (bf16[1024,1024]{1,0:T(8,128)(2,1)}, f32[8,128]{1,0:T(8,128)S(1)}) custom-call(s32[4096]{0:T(1024)S(1)} %bitcast.26, f32[8,128]{1,0:T(8,128)S(1)} %copy-done.25, s32[128,128]{1,0:T(8,128)S(1)} %copy-done.9, f32[128,128]{1,0:T(8,128)S(1)} %copy-done.18, bf16[1024,1024]{1,0:T(8,128)(2,1)S(1)} %bitcast.20), custom_call_target="tpu_custom_call" | custom-call | bytes 41943040 | tf_op jit(solution)/shard_map/new_theta/pallas_call | solution.py:221
  150.1 4.7 %all-to-all-done.4.y_ref = f32[8,280,128]{2,1,0:T(8,128)} async-done(((f32[8,280,128]{2,1,0:T(8,128)}), f32[8,280,128]{2,1,0:T(8,128)}, u32[]{:S(2)}, u32[]{:S(2)}) %all-to-all-start.4) | async-done | bytes 1146912 | tf_op jit(solution)/shard_map/all_to_all | solution.py:657
  154.9 0.0 copy-start.1
  154.9 1.4 copy-done.1
  156.3 13.8 %block_inverse.1 = (f32[8,128,1024]{2,1,0:T(8,128)}, f32[32,128]{1,0:T(8,128)}) custom-call(f32[8,280,128]{2,1,0:T(8,128)} %all-to-all-done.4.y_ref, f32[8,128,1024]{2,1,0:T(8,128)} %get-tuple-element.27.g_ref, f32[8,128,1024]{2,1,0:T(8,128)} %get-tuple-element.28.w_ref, s32[128,1024]{1,0:T(8,128)S(1)} %copy-done.11, bf16[1536,512]{1,0:T(8,128)(2,1)S(1)} %copy-done.1, ...), custom_call_target="tpu_custom_call" | custom-call | tf_op jit(solution)/shard_map/block_inverse/pallas_call | solution.py:641
  (45 shorter events, 0.1 us)
Async XLA Ops:
  2.2 22.4 %all-to-all-start = ((f32[128,1,128]{2,1,0:T(1,128)}), f32[128,1,128]{2,1,0:T(1,128)S(1)}, u32[]{:S(2)}, u32[]{:S(2)}) async-start(f32[128,1,128]{2,1,0:T(1,128)} %bitcast.32), calls=%async_computation | async-start | bytes 131072 | tf_op jit(solution)/shard_map/all_to_all | solution.py:657
  13.7 0.8 copy-start.8
  14.5 0.7 copy-start.14
  15.2 9.3 %copy-start.2 = (bf16[1536,512]{1,0:T(8,128)(2,1)S(1)}, bf16[1536,512]{1,0:T(8,128)(2,1)}, u32[]{:S(2)}) copy-start(bf16[1536,512]{1,0:T(8,128)(2,1)} %constant.16.clone.tab) | copy-start | bytes 4718596
  15.2 9.3 %copy-start.9 = (s32[128,128]{1,0:T(8,128)S(1)}, s32[128,128]{1,0:T(8,128)}, u32[]{:S(2)}) copy-start(s32[128,128]{1,0:T(8,128)} %get-tuple-element.20.ids_ref) | copy-start | bytes 196612
  15.2 9.4 %copy-start.10 = (f32[2,128,128]{2,1,0:T(8,128)S(1)}, f32[2,128,128]{2,1,0:T(8,128)}, u32[]{:S(2)}) copy-start(f32[2,128,128]{2,1,0:T(8,128)} %constant.19.clone.cols) | copy-start | bytes 393220
  15.2 9.4 %copy-start.12 = (bf16[256,128]{1,0:T(8,128)(2,1)S(1)}, bf16[256,128]{1,0:T(8,128)(2,1)}, u32[]{:S(2)}) copy-start(bf16[256,128]{1,0:T(8,128)(2,1)} %constant.17.clone.sine) | copy-start | bytes 196612
  49.2 1.0 copy-start.7
  50.2 0.6 copy-start.26
  50.8 4.9 %copy-start = (bf16[8,128,1024]{2,1,0:T(8,128)(2,1)S(1)}, bf16[8,128,1024]{2,1,0:T(8,128)(2,1)}, u32[]{:S(2)}) copy-start(bf16[8,128,1024]{2,1,0:T(8,128)(2,1)} %param.20) | copy-start | bytes 6291460
  50.8 4.9 %copy-start.15 = (s32[32,128]{1,0:T(8,128)S(1)}, s32[32,128]{1,0:T(8,128)}, u32[]{:S(2)}) copy-start(s32[32,128]{1,0:T(8,128)} %get-tuple-element.19) | copy-start | bytes 49156
  50.8 20.7 %all-to-all-start.1 = ((f32[8,272,128]{2,1,0:T(8,128)}), f32[8,272,128]{2,1,0:T(8,128)S(1)}, u32[]{:S(2)}, u32[]{:S(2)}) async-start(f32[8,272,128]{2,1,0:T(8,128)} %copy-done.7), calls=%async_computation.1 | async-start | bytes 2228224 | tf_op jit(solution)/shard_map/all_to_all | solution.py:657
  55.7 0.7 copy-start.27
  64.9 0.6 copy-start.17
  65.5 0.6 copy-start.19
  66.2 0.6 copy-start.28
  71.5 1.0 copy-start.3
  72.6 1.0 copy-start.5
  73.6 0.7 copy-start.29
  79.5 22.8 %copy-start.4 = (f32[1032,128]{1,0:T(8,128)S(1)}, f32[1032,128]{1,0:T(8,128)}, u32[]{:S(2)}) copy-start(f32[1032,128]{1,0:T(8,128)} %constant.20.clone.ly) | copy-start | bytes 1585156
  79.5 22.8 %copy-start.20 = (f32[16,8,128]{2,1,0:T(8,128)S(1)}, f32[16,8,128]{2,1,0:T(8,128)}, u32[]{:S(2)}) copy-start(f32[16,8,128]{2,1,0:T(8,128)} %copy-done.19) | copy-start | bytes 196612
  102.3 19.3 %copy-start.6 = (bf16[2048,16]{1,0:T(8,128)(2,1)S(1)}, bf16[2048,16]{1,0:T(8,128)(2,1)}, u32[]{:S(2)}) copy-start(bf16[2048,16]{1,0:T(8,128)(2,1)} %constant.22.clone.edge.edge_f) | copy-start | bytes 196612
  102.3 19.3 %copy-start.16 = (bf16[32,1024]{1,0:T(8,128)(2,1)S(1)}, bf16[32,1024]{1,0:T(8,128)(2,1)}, u32[]{:S(2)}) copy-start(bf16[32,1024]{1,0:T(8,128)(2,1)} %constant.23.clone.edge_b) | copy-start | bytes 196612
  130.8 7.9 %copy-start.18 = (f32[128,128]{1,0:T(8,128)S(1)}, f32[128,128]{1,0:T(8,128)}, u32[]{:S(2)}) copy-start(f32[128,128]{1,0:T(8,128)} %copy-done.17) | copy-start | bytes 196612
  130.8 7.9 %copy-start.25 = (f32[8,128]{1,0:T(8,128)S(1)}, f32[8,128]{1,0:T(8,128)}, u32[]{:S(2)}) copy-start(f32[8,128]{1,0:T(8,128)} %copy-done.24) | copy-start | bytes 12292
  130.8 24.1 %copy-start.11 = (s32[128,1024]{1,0:T(8,128)S(1)}, s32[128,1024]{1,0:T(8,128)}, u32[]{:S(2)}) copy-start(s32[128,1024]{1,0:T(8,128)} %roof_ref.1) | copy-start | bytes 1572868
  130.8 24.1 %copy-start.13 = (bf16[256,128]{1,0:T(8,128)(2,1)S(1)}, bf16[256,128]{1,0:T(8,128)(2,1)}, u32[]{:S(2)}) copy-start(bf16[256,128]{1,0:T(8,128)(2,1)} %constant.17.clone.sine) | copy-start | bytes 196612
  130.8 24.1 %copy-start.21 = (f32[1,4096]{1,0:T(1,128)S(1)}, f32[1,4096]{1,0:T(1,128)}, u32[]{:S(2)}) copy-start(f32[1,4096]{1,0:T(1,128)} %param.23) | copy-start | bytes 49156
  130.8 24.1 %copy-start.22 = (f32[1,4096]{1,0:T(1,128)S(1)}, f32[1,4096]{1,0:T(1,128)}, u32[]{:S(2)}) copy-start(f32[1,4096]{1,0:T(1,128)} %param.24) | copy-start | bytes 49156
  130.8 24.1 %copy-start.23 = (f32[1,4096]{1,0:T(1,128)S(1)}, f32[1,4096]{1,0:T(1,128)}, u32[]{:S(2)}) copy-start(f32[1,4096]{1,0:T(1,128)} %param.25) | copy-start | bytes 49156
  130.8 24.1 %all-to-all-start.4 = ((f32[8,280,128]{2,1,0:T(8,128)}), f32[8,280,128]{2,1,0:T(8,128)}, u32[]{:S(2)}, u32[]{:S(2)}) async-start(f32[8,280,128]{2,1,0:T(8,128)} %get-tuple-element.26), calls=%async_computation.4 | async-start | bytes 2293760 | tf_op jit(solution)/shard_map/all_to_all | solution.py:657
  154.9 1.4 copy-start.1
  (1 other events, 0.6 us)

commit v8 on v7

--- a/solution.py
+++ b/solution.py
@@ -414,7 +414,7 @@
         out_specs=(two, pl.BlockSpec((2, BLK, 128), lambda g: (jnp.maximum(g - 5, 0), 0, 0)), col, fixed((8, 128))),
         scratch_shapes=FOUR + [pltpu.VMEM((LEV, ROWS, N), F32), pltpu.VMEM((NPX, LEV, ROWS, 128), F32),
                                pltpu.VMEM((NPX, ROWS, 128), F32), pltpu.VMEM((ROWS, 512), F32)],
-        compiler_params=params(VMEM_MIB), name="block_forward",
+        compiler_params=params(58), name="block_forward",
     )(addr, ids, wc, od, w, w, h, jnp.asarray(TAB), jnp.asarray(SINE2), jnp.asarray(PIVOT), jnp.asarray(COLS))
 
 

time: 171 us -> 170 us (level)
  local copies, waits for them, and re-layouts: 10.5 us -> 7.17 us
    unnamed x60 -> x44, local copies, waits for them, and re-layouts: 10.5 us -> 7.17 us
where the time goes in v8:
time: 170 us; the launch traced here: 169 us
  Pallas kernels  84.2 us (50%)
  blocking collectives  41.3 us (24%)
  starting transfers between devices  24.2 us (14%)
  waiting for transfers between devices  11.2 us (7%)
  local copies, waits for them, and re-layouts  7.17 us (4%)
    all_to_all x2, blocking collectives, swap(): return lax.all_to_all(x, axes, split_axis=0, concat_axis=0, tiled=True)  41.3 us
    pallas_call x1, Pallas kernels, block_forward(): pl.pallas_call(block_forward_kernel, grid=(9,), out_shape=(big, jax.Shape...  25.3 us
    all_to_all x3, starting transfers between devices, swap(): return lax.all_to_all(x, axes, split_axis=0, concat_axis=0, tiled=True)  24.2 us
    pallas_call x1, Pallas kernels, block_inverse(): pl.pallas_call(block_inverse_kernel, grid=(8,), out_shape=(jax.ShapeDtype...  13.8 us
    pallas_call x1, Pallas kernels, new_theta(): pl.pallas_call(theta_kernel, out_shape=(jax.ShapeDtypeStruct((1024, 1024)...  11.5 us
    all_to_all x3, waiting for transfers between devices, swap(): return lax.all_to_all(x, axes, split_axis=0, concat_axis=0, tiled=True)  11.2 us
    pallas_call x1, Pallas kernels, gather_w(): pl.pallas_call(gather_kernel, out_shape=jax.ShapeDtypeStruct((OWNERS, 128...  9.17 us
    pallas_call x1, Pallas kernels, y_inverse(): pl.pallas_call(y_inverse_kernel, grid=(1,), out_shape=(jax.ShapeDtypeStru...  8.59 us
  transfers between devices with their start and end apart: 3, of which 2 were waited for; matrix products, arithmetic and copies ran while one was open for 0% of the time, Pallas kernels for 17%

profile of v8, /device:TPU:1, one launch (start us, length us, event | category | flops | bytes accessed | tf_op | source)
XLA Modules:
  0.0 169.0 jit_solution(4424385519899209341)
XLA Ops:
  0.6 1.5 pack_owner.1
  2.2 11.5 %all-to-all-start = ((f32[128,1,128]{2,1,0:T(1,128)}), f32[128,1,128]{2,1,0:T(1,128)S(1)}, u32[]{:S(2)}, u32[]{:S(2)}) async-start(f32[128,1,128]{2,1,0:T(1,128)} %bitcast.32), calls=%async_computation | async-start | bytes 131072 | tf_op jit(solution)/shard_map/all_to_all | solution.py:657
  13.7 0.0 copy-start.6
  13.7 0.8 copy-done.6
  14.5 0.7 copy-done.15
  15.2 9.2 %facet_gather.1.wc_ref = f32[128,128]{1,0:T(8,128)S(1)} custom-call(s32[4096]{0:T(1024)S(1)} %bitcast.24, s32[128,128]{1,0:T(8,128)S(1)} %copy-done.6, f32[8192,128]{1,0:T(8,128)} %bitcast.31), custom_call_target="tpu_custom_call" | custom-call | tf_op jit(solution)/shard_map/facet_gather/pallas_call | solution.py:168
  24.4 0.6 copy-done.8
  25.0 0.0 all-to-all-done
  25.0 0.6 copy-done.10
  25.7 25.3 %block_forward.1 = (f32[8,128,1024]{2,1,0:T(8,128)}, f32[8,272,128]{2,1,0:T(8,128)}, f32[8,128,1024]{2,1,0:T(8,128)}, f32[8,128]{1,0:T(8,128)}) custom-call(s32[4096]{0:T(1024)} %bitcast.23, s32[128,128]{1,0:T(8,128)} %get-tuple-element.20.ids_ref, f32[128,128]{1,0:T(8,128)} %copy-done.8, f32[128,128]{1,0:T(8,128)} %bitcast.21, f32[8,128,1024]{2,1,0:T(8,128)} %wn_ref.1, ...), custom_call_target="tpu_custom_call" | custom-call | tf_op jit(solution)/shard_map/block_forward/pallas_call | solution.py:408
  50.9 0.0 copy-start
  50.9 0.0 copy-start.7
  51.0 4.9 %all-to-all-start.1 = ((f32[8,272,128]{2,1,0:T(8,128)}), f32[8,272,128]{2,1,0:T(8,128)S(1)}, u32[]{:S(2)}, u32[]{:S(2)}) async-start(f32[8,272,128]{2,1,0:T(8,128)} %get-tuple-element.22), calls=%async_computation.1 | async-start | bytes 2228224 | tf_op jit(solution)/shard_map/all_to_all | solution.py:657
  56.0 0.8 copy-done.11
  56.8 8.5 %heat_flux.1 = (f32[128,128]{1,0:T(8,128)S(1)}, f32[16,8,128]{2,1,0:T(8,128)S(1)}, f32[8,128]{1,0:T(8,128)S(1)}) custom-call(s32[4096]{0:T(1024)S(1)} %bitcast.25, f32[8,128]{1,0:T(8,128)S(1)} %copy-done.21, s32[128,128]{1,0:T(8,128)S(1)} %copy-done.7, f32[128,128]{1,0:T(8,128)S(1)} %copy-done.9, f32[128,128]{1,0:T(8,128)S(1)} %bitcast.22, ...), custom_call_target="tpu_custom_call" | custom-call | bytes 26214400 | tf_op jit(solution)/shard_map/heat_flux/pallas_call | solution.py:193
  65.3 6.5 %all-to-all-done.1.x_ref = f32[8,272,128]{2,1,0:T(8,128)S(1)} async-done(((f32[8,272,128]{2,1,0:T(8,128)}), f32[8,272,128]{2,1,0:T(8,128)S(1)}, u32[]{:S(2)}, u32[]{:S(2)}) %all-to-all-start.1) | async-done | bytes 1114144 | tf_op jit(solution)/shard_map/all_to_all | solution.py:657
  71.7 1.0 copy-done.2
  72.8 1.0 copy-done.4
  73.8 5.2 %y_forward.1 = f32[16,128,128]{2,1,0:T(8,128)S(1)} custom-call(f32[8,272,128]{2,1,0:T(8,128)S(1)} %all-to-all-done.1.x_ref, f32[8,128]{1,0:T(8,128)S(1)} %get-tuple-element.24.tok, f32[1032,128]{1,0:T(8,128)S(1)} %copy-done.2, bf16[1536,512]{1,0:T(8,128)(2,1)} %constant.21.clone.tab, bf16[2048,16]{1,0:T(8,128)(2,1)S(1)} %copy-done.4), custom_call_target="tpu_custom_call" | custom-call | tf_op jit(solution)/shard_map/y_forward/pallas_call | solution.py:469
  79.0 0.0 copy-start.3
  79.0 22.8 %all_to_all.25.al_ref = f32[16,128,128]{2,1,0:T(8,128)S(1)} all-to-all(f32[16,128,128]{2,1,0:T(8,128)S(1)} %y_forward.1), channel_id=1, replica_groups=mesh['px'=8,'py'=16] {'py'}, dimensions={0} | all-to-all | bytes 2097152 | tf_op jit(solution)/shard_map/all_to_all | solution.py:657
  101.8 0.7 ladder.1
  102.5 18.6 %all_to_all.26.pu_ref = f32[16,136,128]{2,1,0:T(8,128)S(1)} all-to-all(f32[16,136,128]{2,1,0:T(8,128)S(1)} %ladder.1), channel_id=1, replica_groups=mesh['px'=8,'py'=16] {'py'}, dimensions={0} | all-to-all | bytes 2228224 | tf_op jit(solution)/shard_map/all_to_all | solution.py:657
  121.0 8.6 %y_inverse.1 = (f32[8,280,128]{2,1,0:T(8,128)}, f32[8,128]{1,0:T(8,128)S(1)}) custom-call(f32[8,272,128]{2,1,0:T(8,128)S(1)} %all-to-all-done.1.x_ref, f32[16,136,128]{2,1,0:T(8,128)S(1)} %all_to_all.26.pu_ref, f32[1032,128]{1,0:T(8,128)S(1)} %copy-done.3, bf16[1536,512]{1,0:T(8,128)(2,1)} %constant.16.clone.tab, bf16[2048,16]{1,0:T(8,128)(2,1)S(1)} %copy-done.5, ...), custom_call_target="tpu_custom_call" | custom-call | tf_op jit(solution)/shard_map/y_inverse/pallas_call | solution.py:574
  129.6 0.0 copy-start.19
  129.6 0.0 copy-start.20
  129.7 7.8 %all-to-all-start.4 = ((f32[8,280,128]{2,1,0:T(8,128)}), f32[8,280,128]{2,1,0:T(8,128)}, u32[]{:S(2)}, u32[]{:S(2)}) async-start(f32[8,280,128]{2,1,0:T(8,128)} %get-tuple-element.26), calls=%async_computation.4 | async-start | bytes 2293760 | tf_op jit(solution)/shard_map/all_to_all | solution.py:657
  137.4 11.5 %new_theta.1 = (bf16[1024,1024]{1,0:T(8,128)(2,1)}, f32[8,128]{1,0:T(8,128)S(1)}) custom-call(s32[4096]{0:T(1024)S(1)} %bitcast.26, f32[8,128]{1,0:T(8,128)S(1)} %get-tuple-element.29.tok_in, s32[128,128]{1,0:T(8,128)S(1)} %copy-done.7, f32[128,128]{1,0:T(8,128)S(1)} %get-tuple-element.30.flux_ref, bf16[1024,1024]{1,0:T(8,128)(2,1)S(1)} %bitcast.20), custom_call_target="tpu_custom_call" | custom-call | bytes 41943040 | tf_op jit(solution)/shard_map/new_theta/pallas_call | solution.py:221
  149.0 4.7 %all-to-all-done.4.y_ref = f32[8,280,128]{2,1,0:T(8,128)} async-done(((f32[8,280,128]{2,1,0:T(8,128)}), f32[8,280,128]{2,1,0:T(8,128)}, u32[]{:S(2)}, u32[]{:S(2)}) %all-to-all-start.4) | async-done | bytes 1146912 | tf_op jit(solution)/shard_map/all_to_all | solution.py:657
  153.8 0.0 copy-start.1
  153.8 1.4 copy-done.1
  155.2 13.8 %block_inverse.1 = (f32[8,128,1024]{2,1,0:T(8,128)}, f32[32,128]{1,0:T(8,128)}) custom-call(f32[8,280,128]{2,1,0:T(8,128)} %all-to-all-done.4.y_ref, f32[8,128,1024]{2,1,0:T(8,128)} %get-tuple-element.27.g_ref, f32[8,128,1024]{2,1,0:T(8,128)} %get-tuple-element.28.w_ref, s32[128,1024]{1,0:T(8,128)S(1)} %copy-done.13, bf16[1536,512]{1,0:T(8,128)(2,1)S(1)} %copy-done.1, ...), custom_call_target="tpu_custom_call" | custom-call | tf_op jit(solution)/shard_map/block_inverse/pallas_call | solution.py:641
  (29 shorter events, 0.1 us)
Async XLA Ops:
  2.2 22.9 %all-to-all-start = ((f32[128,1,128]{2,1,0:T(1,128)}), f32[128,1,128]{2,1,0:T(1,128)S(1)}, u32[]{:S(2)}, u32[]{:S(2)}) async-start(f32[128,1,128]{2,1,0:T(1,128)} %bitcast.32), calls=%async_computation | async-start | bytes 131072 | tf_op jit(solution)/shard_map/all_to_all | solution.py:657
  13.7 0.8 copy-start.6
  14.5 0.7 copy-start.15
  24.4 0.6 copy-start.8
  25.0 0.6 copy-start.10
  25.7 30.3 %copy-start.16 = (s32[32,128]{1,0:T(8,128)S(1)}, s32[32,128]{1,0:T(8,128)}, u32[]{:S(2)}) copy-start(s32[32,128]{1,0:T(8,128)} %get-tuple-element.19) | copy-start | bytes 49156
  50.9 5.0 %copy-start = (bf16[8,128,1024]{2,1,0:T(8,128)(2,1)S(1)}, bf16[8,128,1024]{2,1,0:T(8,128)(2,1)}, u32[]{:S(2)}) copy-start(bf16[8,128,1024]{2,1,0:T(8,128)(2,1)} %param.20) | copy-start | bytes 6291460
  50.9 5.0 %copy-start.7 = (s32[128,128]{1,0:T(8,128)S(1)}, s32[128,128]{1,0:T(8,128)}, u32[]{:S(2)}) copy-start(s32[128,128]{1,0:T(8,128)} %get-tuple-element.20.ids_ref) | copy-start | bytes 196612
  50.9 5.0 %copy-start.9 = (f32[128,128]{1,0:T(8,128)S(1)}, f32[128,128]{1,0:T(8,128)}, u32[]{:S(2)}) copy-start(f32[128,128]{1,0:T(8,128)} %copy-done.8) | copy-start | bytes 196612
  50.9 5.0 %copy-start.21 = (f32[8,128]{1,0:T(8,128)S(1)}, f32[8,128]{1,0:T(8,128)}, u32[]{:S(2)}) copy-start(f32[8,128]{1,0:T(8,128)} %get-tuple-element.23.tok_in) | copy-start | bytes 12292
  51.0 20.8 %all-to-all-start.1 = ((f32[8,272,128]{2,1,0:T(8,128)}), f32[8,272,128]{2,1,0:T(8,128)S(1)}, u32[]{:S(2)}, u32[]{:S(2)}) async-start(f32[8,272,128]{2,1,0:T(8,128)} %get-tuple-element.22), calls=%async_computation.1 | async-start | bytes 2228224 | tf_op jit(solution)/shard_map/all_to_all | solution.py:657
  55.9 0.8 copy-start.11
  71.7 1.0 copy-start.2
  72.8 1.0 copy-start.4
  79.0 22.8 %copy-start.3 = (f32[1032,128]{1,0:T(8,128)S(1)}, f32[1032,128]{1,0:T(8,128)}, u32[]{:S(2)}) copy-start(f32[1032,128]{1,0:T(8,128)} %constant.20.clone.ly) | copy-start | bytes 1585156
  101.8 19.3 %copy-start.5 = (bf16[2048,16]{1,0:T(8,128)(2,1)S(1)}, bf16[2048,16]{1,0:T(8,128)(2,1)}, u32[]{:S(2)}) copy-start(bf16[2048,16]{1,0:T(8,128)(2,1)} %constant.22.clone.edge.edge_f) | copy-start | bytes 196612
  101.8 19.3 %copy-start.17 = (bf16[32,1024]{1,0:T(8,128)(2,1)S(1)}, bf16[32,1024]{1,0:T(8,128)(2,1)}, u32[]{:S(2)}) copy-start(bf16[32,1024]{1,0:T(8,128)(2,1)} %constant.23.clone.edge_b) | copy-start | bytes 196612
  129.6 24.1 %copy-start.12 = (f32[2,128,128]{2,1,0:T(8,128)S(1)}, f32[2,128,128]{2,1,0:T(8,128)}, u32[]{:S(2)}) copy-start(f32[2,128,128]{2,1,0:T(8,128)} %constant.19.clone.cols) | copy-start | bytes 393220
  129.6 24.1 %copy-start.13 = (s32[128,1024]{1,0:T(8,128)S(1)}, s32[128,1024]{1,0:T(8,128)}, u32[]{:S(2)}) copy-start(s32[128,1024]{1,0:T(8,128)} %roof_ref.1) | copy-start | bytes 1572868
  129.6 24.1 %copy-start.14 = (bf16[256,128]{1,0:T(8,128)(2,1)S(1)}, bf16[256,128]{1,0:T(8,128)(2,1)}, u32[]{:S(2)}) copy-start(bf16[256,128]{1,0:T(8,128)(2,1)} %constant.17.clone.sine) | copy-start | bytes 196612
  129.6 24.1 %copy-start.18 = (f32[1,4096]{1,0:T(1,128)S(1)}, f32[1,4096]{1,0:T(1,128)}, u32[]{:S(2)}) copy-start(f32[1,4096]{1,0:T(1,128)} %param.23) | copy-start | bytes 49156
  129.6 24.1 %copy-start.19 = (f32[1,4096]{1,0:T(1,128)S(1)}, f32[1,4096]{1,0:T(1,128)}, u32[]{:S(2)}) copy-start(f32[1,4096]{1,0:T(1,128)} %param.24) | copy-start | bytes 49156
  129.6 24.1 %copy-start.20 = (f32[1,4096]{1,0:T(1,128)S(1)}, f32[1,4096]{1,0:T(1,128)}, u32[]{:S(2)}) copy-start(f32[1,4096]{1,0:T(1,128)} %param.25) | copy-start | bytes 49156
  129.7 24.1 %all-to-all-start.4 = ((f32[8,280,128]{2,1,0:T(8,128)}), f32[8,280,128]{2,1,0:T(8,128)}, u32[]{:S(2)}, u32[]{:S(2)}) async-start(f32[8,280,128]{2,1,0:T(8,128)} %get-tuple-element.26), calls=%async_computation.4 | async-start | bytes 2293760 | tf_op jit(solution)/shard_map/all_to_all | solution.py:657
  153.8 1.4 copy-start.1

commit v9 on v7

--- a/solution.py
+++ b/solution.py
@@ -307,7 +307,7 @@
             (512, dot3(*split(d), *td)))
 
 
-STRIP = 32
+STRIP = 16
 
 
 def fold(v):

time: 171 us -> 172 us (level)
  no operation moved by 1% of the time
where the time goes in v9:
time: 172 us; the launch traced here: 171 us
  Pallas kernels  84.8 us (49%)
  blocking collectives  41.3 us (24%)
  starting transfers between devices  24.2 us (14%)
  local copies, waits for them, and re-layouts  10.5 us (6%)
  waiting for transfers between devices  9.53 us (6%)
    all_to_all x2, blocking collectives, swap(): return lax.all_to_all(x, axes, split_axis=0, concat_axis=0, tiled=True)  41.3 us
    pallas_call x1, Pallas kernels, block_forward(): pl.pallas_call(block_forward_kernel, grid=(9,), out_shape=(big, jax.Shape...  25 us
    all_to_all x3, starting transfers between devices, swap(): return lax.all_to_all(x, axes, split_axis=0, concat_axis=0, tiled=True)  24.2 us
    pallas_call x1, Pallas kernels, block_inverse(): pl.pallas_call(block_inverse_kernel, grid=(8,), out_shape=(jax.ShapeDtype...  14.6 us
    pallas_call x1, Pallas kernels, new_theta(): pl.pallas_call(theta_kernel, out_shape=(jax.ShapeDtypeStruct((1024, 1024)...  11.5 us
    unnamed x60, local copies, waits for them, and re-layouts  10.5 us
    all_to_all x3, waiting for transfers between devices, swap(): return lax.all_to_all(x, axes, split_axis=0, concat_axis=0, tiled=True)  9.53 us
    pallas_call x1, Pallas kernels, gather_w(): pl.pallas_call(gather_kernel, out_shape=jax.ShapeDtypeStruct((OWNERS, 128...  9.31 us
  transfers between devices with their start and end apart: 3, of which 2 were waited for; matrix products, arithmetic and copies ran while one was open for 0% of the time, Pallas kernels for 17%

profile of v9, /device:TPU:1, one launch (start us, length us, event | category | flops | bytes accessed | tf_op | source)
XLA Modules:
  0.0 171.3 jit_solution(11956550637460786967)
XLA Ops:
  0.6 1.5 pack_owner.1
  2.2 11.5 %all-to-all-start = ((f32[128,1,128]{2,1,0:T(1,128)}), f32[128,1,128]{2,1,0:T(1,128)S(1)}, u32[]{:S(2)}, u32[]{:S(2)}) async-start(f32[128,1,128]{2,1,0:T(1,128)} %bitcast.32), calls=%async_computation | async-start | bytes 131072 | tf_op jit(solution)/shard_map/all_to_all | solution.py:657
  13.7 0.8 copy-done.8
  14.5 0.7 copy-done.14
  15.2 9.3 %facet_gather.1.wc_ref = f32[128,128]{1,0:T(8,128)S(1)} custom-call(s32[4096]{0:T(1024)S(1)} %bitcast.23, s32[128,128]{1,0:T(8,128)S(1)} %copy-done.8, f32[8192,128]{1,0:T(8,128)} %bitcast.31), custom_call_target="tpu_custom_call" | custom-call | tf_op jit(solution)/shard_map/facet_gather/pallas_call | solution.py:168
  24.6 25.0 %block_forward.1 = (f32[8,128,1024]{2,1,0:T(8,128)}, f32[8,272,128]{2,1,0:T(8,128)S(1)}, f32[8,128,1024]{2,1,0:T(8,128)}, f32[8,128]{1,0:T(8,128)S(1)}) custom-call(s32[4096]{0:T(1024)S(1)} %bitcast.24, s32[128,128]{1,0:T(8,128)S(1)} %copy-done.9, f32[128,128]{1,0:T(8,128)S(1)} %facet_gather.1.wc_ref, f32[128,128]{1,0:T(8,128)S(1)} %bitcast.21, ...), custom_call_target="tpu_custom_call" | custom-call | tf_op jit(solution)/shard_map/block_forward/pallas_call | solution.py:408
  49.6 1.0 copy-done.7
  50.6 0.6 copy-done.26
  51.2 4.9 %all-to-all-start.1 = ((f32[8,272,128]{2,1,0:T(8,128)}), f32[8,272,128]{2,1,0:T(8,128)S(1)}, u32[]{:S(2)}, u32[]{:S(2)}) async-start(f32[8,272,128]{2,1,0:T(8,128)} %copy-done.7), calls=%async_computation.1 | async-start | bytes 2228224 | tf_op jit(solution)/shard_map/all_to_all | solution.py:657
  56.1 0.0 copy-start.27
  56.1 0.7 copy-done.27
  56.8 8.5 %heat_flux.1 = (f32[128,128]{1,0:T(8,128)S(1)}, f32[16,8,128]{2,1,0:T(8,128)S(1)}, f32[8,128]{1,0:T(8,128)S(1)}) custom-call(s32[4096]{0:T(1024)S(1)} %bitcast.25, f32[8,128]{1,0:T(8,128)S(1)} %copy-done.27, s32[128,128]{1,0:T(8,128)S(1)} %copy-done.9, f32[128,128]{1,0:T(8,128)S(1)} %facet_gather.1.wc_ref, f32[128,128]{1,0:T(8,128)S(1)} %bitcast.22, ...), custom_call_target="tpu_custom_call" | custom-call | bytes 26214400 | tf_op jit(solution)/shard_map/heat_flux/pallas_call | solution.py:193
  65.3 0.6 copy-done.17
  65.9 0.6 copy-done.19
  66.5 0.6 copy-done.28
  67.1 4.8 %all-to-all-done.1.x_ref = f32[8,272,128]{2,1,0:T(8,128)S(1)} async-done(((f32[8,272,128]{2,1,0:T(8,128)}), f32[8,272,128]{2,1,0:T(8,128)S(1)}, u32[]{:S(2)}, u32[]{:S(2)}) %all-to-all-start.1) | async-done | bytes 1114144 | tf_op jit(solution)/shard_map/all_to_all | solution.py:657
  71.9 1.0 copy-done.3
  73.0 1.0 copy-done.5
  74.0 0.7 copy-done.29
  74.7 5.2 %y_forward.1 = f32[16,128,128]{2,1,0:T(8,128)S(1)} custom-call(f32[8,272,128]{2,1,0:T(8,128)S(1)} %all-to-all-done.1.x_ref, f32[8,128]{1,0:T(8,128)S(1)} %copy-done.29, f32[1032,128]{1,0:T(8,128)S(1)} %copy-done.3, bf16[1536,512]{1,0:T(8,128)(2,1)} %constant.21.clone.tab, bf16[2048,16]{1,0:T(8,128)(2,1)S(1)} %copy-done.5), custom_call_target="tpu_custom_call" | custom-call | tf_op jit(solution)/shard_map/y_forward/pallas_call | solution.py:469
  79.9 0.0 copy-start.4
  79.9 22.8 %all_to_all.25.al_ref = f32[16,128,128]{2,1,0:T(8,128)S(1)} all-to-all(f32[16,128,128]{2,1,0:T(8,128)S(1)} %y_forward.1), channel_id=1, replica_groups=mesh['px'=8,'py'=16] {'py'}, dimensions={0} | all-to-all | bytes 2097152 | tf_op jit(solution)/shard_map/all_to_all | solution.py:657
  102.7 0.7 ladder.1
  103.4 18.6 %all_to_all.26.pu_ref = f32[16,136,128]{2,1,0:T(8,128)S(1)} all-to-all(f32[16,136,128]{2,1,0:T(8,128)S(1)} %ladder.1), channel_id=1, replica_groups=mesh['px'=8,'py'=16] {'py'}, dimensions={0} | all-to-all | bytes 2228224 | tf_op jit(solution)/shard_map/all_to_all | solution.py:657
  122.0 8.6 %y_inverse.1 = (f32[8,280,128]{2,1,0:T(8,128)}, f32[8,128]{1,0:T(8,128)S(1)}) custom-call(f32[8,272,128]{2,1,0:T(8,128)S(1)} %all-to-all-done.1.x_ref, f32[16,136,128]{2,1,0:T(8,128)S(1)} %all_to_all.26.pu_ref, f32[1032,128]{1,0:T(8,128)S(1)} %copy-done.4, bf16[1536,512]{1,0:T(8,128)(2,1)} %constant.16.clone.tab, bf16[2048,16]{1,0:T(8,128)(2,1)S(1)} %copy-done.6, ...), custom_call_target="tpu_custom_call" | custom-call | tf_op jit(solution)/shard_map/y_inverse/pallas_call | solution.py:574
  130.5 0.6 copy-done.24
  131.2 7.8 %all-to-all-start.4 = ((f32[8,280,128]{2,1,0:T(8,128)}), f32[8,280,128]{2,1,0:T(8,128)}, u32[]{:S(2)}, u32[]{:S(2)}) async-start(f32[8,280,128]{2,1,0:T(8,128)} %get-tuple-element.26), calls=%async_computation.4 | async-start | bytes 2293760 | tf_op jit(solution)/shard_map/all_to_all | solution.py:657
  139.0 11.5 %new_theta.1 = (bf16[1024,1024]{1,0:T(8,128)(2,1)}, f32[8,128]{1,0:T(8,128)S(1)}) custom-call(s32[4096]{0:T(1024)S(1)} %bitcast.26, f32[8,128]{1,0:T(8,128)S(1)} %copy-done.25, s32[128,128]{1,0:T(8,128)S(1)} %copy-done.9, f32[128,128]{1,0:T(8,128)S(1)} %copy-done.18, bf16[1024,1024]{1,0:T(8,128)(2,1)S(1)} %bitcast.20), custom_call_target="tpu_custom_call" | custom-call | bytes 41943040 | tf_op jit(solution)/shard_map/new_theta/pallas_call | solution.py:221
  150.5 4.7 %all-to-all-done.4.y_ref = f32[8,280,128]{2,1,0:T(8,128)} async-done(((f32[8,280,128]{2,1,0:T(8,128)}), f32[8,280,128]{2,1,0:T(8,128)}, u32[]{:S(2)}, u32[]{:S(2)}) %all-to-all-start.4) | async-done | bytes 1146912 | tf_op jit(solution)/shard_map/all_to_all | solution.py:657
  155.3 0.0 copy-start.1
  155.3 1.4 copy-done.1
  156.7 14.6 %block_inverse.1 = (f32[8,128,1024]{2,1,0:T(8,128)}, f32[32,128]{1,0:T(8,128)}) custom-call(f32[8,280,128]{2,1,0:T(8,128)} %all-to-all-done.4.y_ref, f32[8,128,1024]{2,1,0:T(8,128)} %get-tuple-element.27.g_ref, f32[8,128,1024]{2,1,0:T(8,128)} %get-tuple-element.28.w_ref, s32[128,1024]{1,0:T(8,128)S(1)} %copy-done.11, bf16[1536,512]{1,0:T(8,128)(2,1)S(1)} %copy-done.1, ...), custom_call_target="tpu_custom_call" | custom-call | tf_op jit(solution)/shard_map/block_inverse/pallas_call | solution.py:641
  (45 shorter events, 0.1 us)
Async XLA Ops:
  2.2 22.4 %all-to-all-start = ((f32[128,1,128]{2,1,0:T(1,128)}), f32[128,1,128]{2,1,0:T(1,128)S(1)}, u32[]{:S(2)}, u32[]{:S(2)}) async-start(f32[128,1,128]{2,1,0:T(1,128)} %bitcast.32), calls=%async_computation | async-start | bytes 131072 | tf_op jit(solution)/shard_map/all_to_all | solution.py:657
  13.7 0.8 copy-start.8
  14.5 0.7 copy-start.14
  15.2 9.3 %copy-start.2 = (bf16[1536,512]{1,0:T(8,128)(2,1)S(1)}, bf16[1536,512]{1,0:T(8,128)(2,1)}, u32[]{:S(2)}) copy-start(bf16[1536,512]{1,0:T(8,128)(2,1)} %constant.16.clone.tab) | copy-start | bytes 4718596
  15.2 9.3 %copy-start.9 = (s32[128,128]{1,0:T(8,128)S(1)}, s32[128,128]{1,0:T(8,128)}, u32[]{:S(2)}) copy-start(s32[128,128]{1,0:T(8,128)} %get-tuple-element.20.ids_ref) | copy-start | bytes 196612
  15.2 9.4 %copy-start.10 = (f32[2,128,128]{2,1,0:T(8,128)S(1)}, f32[2,128,128]{2,1,0:T(8,128)}, u32[]{:S(2)}) copy-start(f32[2,128,128]{2,1,0:T(8,128)} %constant.19.clone.cols) | copy-start | bytes 393220
  15.2 9.4 %copy-start.12 = (bf16[256,128]{1,0:T(8,128)(2,1)S(1)}, bf16[256,128]{1,0:T(8,128)(2,1)}, u32[]{:S(2)}) copy-start(bf16[256,128]{1,0:T(8,128)(2,1)} %constant.17.clone.sine) | copy-start | bytes 196612
  49.6 1.0 copy-start.7
  50.6 0.6 copy-start.26
  51.2 4.9 %copy-start = (bf16[8,128,1024]{2,1,0:T(8,128)(2,1)S(1)}, bf16[8,128,1024]{2,1,0:T(8,128)(2,1)}, u32[]{:S(2)}) copy-start(bf16[8,128,1024]{2,1,0:T(8,128)(2,1)} %param.20) | copy-start | bytes 6291460
  51.2 4.9 %copy-start.15 = (s32[32,128]{1,0:T(8,128)S(1)}, s32[32,128]{1,0:T(8,128)}, u32[]{:S(2)}) copy-start(s32[32,128]{1,0:T(8,128)} %get-tuple-element.19) | copy-start | bytes 49156
  51.2 20.7 %all-to-all-start.1 = ((f32[8,272,128]{2,1,0:T(8,128)}), f32[8,272,128]{2,1,0:T(8,128)S(1)}, u32[]{:S(2)}, u32[]{:S(2)}) async-start(f32[8,272,128]{2,1,0:T(8,128)} %copy-done.7), calls=%async_computation.1 | async-start | bytes 2228224 | tf_op jit(solution)/shard_map/all_to_all | solution.py:657
  56.1 0.7 copy-start.27
  65.3 0.6 copy-start.17
  65.9 0.6 copy-start.19
  66.5 0.6 copy-start.28
  71.9 1.0 copy-start.3
  73.0 1.0 copy-start.5
  74.0 0.7 copy-start.29
  79.9 22.8 %copy-start.4 = (f32[1032,128]{1,0:T(8,128)S(1)}, f32[1032,128]{1,0:T(8,128)}, u32[]{:S(2)}) copy-start(f32[1032,128]{1,0:T(8,128)} %constant.20.clone.ly) | copy-start | bytes 1585156
  79.9 22.8 %copy-start.20 = (f32[16,8,128]{2,1,0:T(8,128)S(1)}, f32[16,8,128]{2,1,0:T(8,128)}, u32[]{:S(2)}) copy-start(f32[16,8,128]{2,1,0:T(8,128)} %copy-done.19) | copy-start | bytes 196612
  102.7 19.3 %copy-start.6 = (bf16[2048,16]{1,0:T(8,128)(2,1)S(1)}, bf16[2048,16]{1,0:T(8,128)(2,1)}, u32[]{:S(2)}) copy-start(bf16[2048,16]{1,0:T(8,128)(2,1)} %constant.22.clone.edge.edge_f) | copy-start | bytes 196612
  102.7 19.3 %copy-start.16 = (bf16[32,1024]{1,0:T(8,128)(2,1)S(1)}, bf16[32,1024]{1,0:T(8,128)(2,1)}, u32[]{:S(2)}) copy-start(bf16[32,1024]{1,0:T(8,128)(2,1)} %constant.23.clone.edge_b) | copy-start | bytes 196612
  131.1 7.9 %copy-start.18 = (f32[128,128]{1,0:T(8,128)S(1)}, f32[128,128]{1,0:T(8,128)}, u32[]{:S(2)}) copy-start(f32[128,128]{1,0:T(8,128)} %copy-done.17) | copy-start | bytes 196612
  131.1 7.9 %copy-start.25 = (f32[8,128]{1,0:T(8,128)S(1)}, f32[8,128]{1,0:T(8,128)}, u32[]{:S(2)}) copy-start(f32[8,128]{1,0:T(8,128)} %copy-done.24) | copy-start | bytes 12292
  131.1 24.1 %copy-start.11 = (s32[128,1024]{1,0:T(8,128)S(1)}, s32[128,1024]{1,0:T(8,128)}, u32[]{:S(2)}) copy-start(s32[128,1024]{1,0:T(8,128)} %roof_ref.1) | copy-start | bytes 1572868
  131.1 24.1 %copy-start.13 = (bf16[256,128]{1,0:T(8,128)(2,1)S(1)}, bf16[256,128]{1,0:T(8,128)(2,1)}, u32[]{:S(2)}) copy-start(bf16[256,128]{1,0:T(8,128)(2,1)} %constant.17.clone.sine) | copy-start | bytes 196612
  131.1 24.1 %copy-start.21 = (f32[1,4096]{1,0:T(1,128)S(1)}, f32[1,4096]{1,0:T(1,128)}, u32[]{:S(2)}) copy-start(f32[1,4096]{1,0:T(1,128)} %param.23) | copy-start | bytes 49156
  131.1 24.1 %copy-start.22 = (f32[1,4096]{1,0:T(1,128)S(1)}, f32[1,4096]{1,0:T(1,128)}, u32[]{:S(2)}) copy-start(f32[1,4096]{1,0:T(1,128)} %param.24) | copy-start | bytes 49156
  131.1 24.1 %copy-start.23 = (f32[1,4096]{1,0:T(1,128)S(1)}, f32[1,4096]{1,0:T(1,128)}, u32[]{:S(2)}) copy-start(f32[1,4096]{1,0:T(1,128)} %param.25) | copy-start | bytes 49156
  131.2 24.1 %all-to-all-start.4 = ((f32[8,280,128]{2,1,0:T(8,128)}), f32[8,280,128]{2,1,0:T(8,128)}, u32[]{:S(2)}, u32[]{:S(2)}) async-start(f32[8,280,128]{2,1,0:T(8,128)} %get-tuple-element.26), calls=%async_computation.4 | async-start | bytes 2293760 | tf_op jit(solution)/shard_map/all_to_all | solution.py:657
  155.3 1.4 copy-start.1
  (1 other events, 0.6 us)
